TPU v7x, 256 devices: a whole 4x4x8 slice. The times are simulated.
256 devices in a mesh: dp: 16 (over x, y), tensor: 16 (over z, core).
Axes of the slice: x: 4, y: 4, z: 8, core: 2. Of those that a mesh axis runs over, the one named last changes fastest.
Arguments:
- grad_out: bfloat16 [16384, 3584], P(('dp', 'tensor')), may hold values from -1.5 to 1.5
- pre_act: bfloat16 [2, 16384, 8192], P(None, 'dp', 'tensor'), may hold values from -6 to 6
- down_weight: bfloat16 [8192, 3584], P('tensor'), may hold values from -0.09375 to 0.09375
- error: bfloat16 [131072, 3584], P(('dp', 'tensor')), may hold values from -12 to 12
- q_start: float32 [512, 3584], P('tensor'), may hold values from -0.09375 to 0.09375
Outputs:
- grad_pre: bfloat16 [2, 16384, 8192], P(None, 'dp', 'tensor')
- new_error: bfloat16 [131072, 3584], P(('dp', 'tensor'))
- p_factor: float32 [32, 8192], P(None, 'tensor')
- q_factor: float32 [512, 3584], P('tensor')
All inputs are finite; a program needn't handle non-finite values.
Results may differ from a plain program's by a relative error of at most 0.017.
Values may be sent and summed in bfloat16 or wider, within the bound.
No kernel may reach another device: no remote copies, remote signals or barrier semaphores. Data moves between devices by JAX's collectives and lax.ppermute only.
A program may use at most 128 MiB of HBM per device.

v0:
```python
import jax
import jax.numpy as jnp
from jax import lax
from jax.sharding import PartitionSpec as P


def gelu_pair(value):
    coeff = 0.7978845608028654
    tanh_val = jnp.tanh(coeff * (value + 0.044715 * value * value * value))
    gelu_value = 0.5 * value * (1.0 + tanh_val)
    gelu_slope = 0.5 * (1.0 + tanh_val) + 0.5 * value * (1.0 - tanh_val * tanh_val) * coeff * (
        1.0 + 3.0 * 0.044715 * value * value
    )
    return (gelu_value, gelu_slope)


def on_device(grad_out, pre_act, down_weight, error, q_start):
    highest_precision = lax.Precision.HIGHEST
    gate_pre = pre_act[0].astype(jnp.float32)
    up_pre = pre_act[1].astype(jnp.float32)
    gelu_value, gelu_slope = gelu_pair(gate_pre)
    hidden = (gelu_value * up_pre).astype(jnp.bfloat16)
    collected_factors = lax.all_gather(grad_out, "tensor", axis=0, tiled=True)
    weight_grad = lax.dot_general(
        hidden, collected_factors, (((0,), (0,)), ((), ())), preferred_element_type=jnp.float32
    )
    hidden_grad = lax.dot_general(
        collected_factors, down_weight, (((1,), (1,)), ((), ())), preferred_element_type=jnp.float32
    )
    grad_pre = jnp.stack([hidden_grad * up_pre * gelu_slope, hidden_grad * gelu_value]).astype(
        jnp.bfloat16
    )
    dp_count = lax.axis_size("dp")
    merged = weight_grad + error.astype(jnp.float32)
    left_local = lax.dot_general(
        merged, q_start, (((1,), (1,)), ((), ())), precision=highest_precision
    )
    left_mean = lax.psum(left_local, "dp") / dp_count
    gram = jnp.dot(left_mean.T, left_mean, precision=highest_precision)
    chol_factor = jnp.linalg.cholesky(gram)
    orthonormal_left = jax.scipy.linalg.solve_triangular(chol_factor, left_mean.T, lower=True)
    right_local = jnp.dot(orthonormal_left, merged, precision=highest_precision)
    right_average = lax.psum(right_local.astype(jnp.bfloat16), "dp").astype(jnp.float32) / dp_count
    lowrank_estimate = lax.dot_general(
        orthonormal_left, right_average, (((0,), (0,)), ((), ())), precision=highest_precision
    )
    new_error = (merged - lowrank_estimate).astype(jnp.bfloat16)
    return (grad_pre, new_error, orthonormal_left, right_average)


def solution(mesh):
    placed = (
        P(("dp", "tensor"), None),
        P(None, "dp", "tensor"),
        P("tensor", None),
        P(("dp", "tensor"), None),
        P("tensor", None),
    )
    return jax.shard_map(
        on_device,
        mesh=mesh,
        in_specs=placed,
        out_specs=(
            P(None, "dp", "tensor"),
            P(("dp", "tensor"), None),
            P(None, "tensor"),
            P("tensor", None),
        ),
        check_vma=False,
    )
```

profile of v0, /device:TPU:96, one launch (start us, length us, event | category | flops | bytes accessed | tf_op | source)
XLA Modules:
  0.0 299.5 jit_solution(12925860299426745761)
XLA Ops:
  7.2 0.0 copy-start
  7.2 0.0 all-gather.2.cloned.1.call-start
  7.2 0.7 all-gather.2.cloned.1.call-update
  7.9 0.0 all-reduce.3.cloned.1.call-start
  8.0 54.2 %all-gather.2.cloned.1.call-done = bf16[1024,3584]{1,0:T(8,128)(2,1)} async-done(((bf16[64,3584]{1,0:T(8,128)(2,1)}), bf16[1024,3584]{1,0:T(8,128)(2,1)}) %all-gather.2.cloned.1.call-update) | async-done | bytes 7340048 | tf_op jit(solution)/shard_map/all_gather | solution.py:23
  62.1 9.2 %convert_add_fusion = f32[512,3584]{1,0:T(8,128)S(1)} fusion(bf16[512,3584]{1,0:T(8,128)(2,1)} %param.8, bf16[1024,3584]{1,0:T(8,128)(2,1)} %all-gather.2.cloned.1.call-done, bf16[2,1024,512]{2,1,0:T(8,128)(2,1)} %param.6), kind=kOutput, calls=%fused_computation.1 | convolution fusion | flops 3768057856 | bytes 20447232 | tf_op jit(solution)/shard_map/dot_general | solution.py:24
  71.4 0.0 copy-start.1
  71.4 2.9 copy-done.1
  74.3 0.0 copy-done
  74.3 7.4 %fusion.37 = f32[512,32]{0,1:T(8,128)} fusion(f32[512,3584]{1,0:T(8,128)S(1)} %convert_add_fusion, f32[32,3584]{1,0:T(8,128)S(1)} %copy-done), kind=kOutput, calls=%fused_computation.57 | convolution fusion | flops 704643072 | bytes 7864320 | tf_op jit(solution)/shard_map/dot_general | solution.py:35
  81.7 0.0 all-reduce.3.cloned.1.call-update
  81.7 0.2 all-reduce.5.cloned.1.call-start
  82.0 90.2 %all-reduce.3.cloned.1.call-done = f32[512,32]{0,1:T(8,128)} async-done(((f32[512,32]{0,1:T(8,128)}), f32[512,32]{0,1:T(8,128)}) %all-reduce.3.cloned.1.call-update) | async-done | bytes 65552 | tf_op jit(solution)/shard_map/psum | solution.py:38
  172.1 1.1 fusion.24
  173.2 0.1 copy.9
  173.3 2.9 cholesky.16
  176.3 0.6 compare_reduce_fusion
  176.9 0.7 fusion.28
  177.6 2.4 custom-call.7
  180.0 1.1 fusion.22
  181.1 0.0 copy-start.3
  181.1 0.0 copy-start.4
  181.1 7.3 %convolution_convert_fusion = bf16[32,3584]{1,0:T(8,128)(2,1)} fusion(f32[32,512]{1,0:T(8,128)S(1)} %fusion.22, f32[512,3584]{1,0:T(8,128)} %copy-done.1), kind=kOutput, calls=%fused_computation.9 | convolution fusion | flops 704757760 | bytes 7634944 | tf_op jit(solution)/shard_map/dot_general | solution.py:42
  188.4 0.0 all-reduce.5.cloned.1.call-update
  188.4 0.0 copy-done.4
  188.5 9.4 %fusion.19 = (bf16[1,1024,512]{2,1,0:T(8,128)(2,1)S(1)}, bf16[1,1024,512]{2,1,0:T(8,128)(2,1)S(1)}) fusion(bf16[2,1024,512]{2,1,0:T(8,128)(2,1)S(1)} %copy-done.4, bf16[1024,3584]{1,0:T(8,128)(2,1)} %all-gather.2.cloned.1.call-done, bf16[512,3584]{1,0:T(8,128)(2,1)} %param.7), kind=kOutput, calls=%fused_computation.32 | convolution fusion | flops 3771203584 | bytes 15204352 | tf_op jit(solution)/shard_map/dot_general | solution.py:27
  197.9 1.5 pad_maximum_fusion
  199.4 83.0 %all-reduce.5.cloned.1.call-done = bf16[32,3584]{1,0:T(8,128)(2,1)} async-done(((bf16[32,3584]{1,0:T(8,128)(2,1)}), bf16[32,3584]{1,0:T(8,128)(2,1)}) %all-reduce.5.cloned.1.call-update) | async-done | bytes 229392 | tf_op jit(solution)/shard_map/psum | solution.py:43
  282.4 1.0 convert_multiply_fusion.8
  283.3 0.0 copy-done.3
  283.4 0.0 copy-start.2
  283.4 9.6 %subtract_convert_fusion = bf16[512,3584]{1,0:T(8,128)(2,1)} fusion(f32[512,3584]{1,0:T(8,128)} %copy-done.1, f32[32,512]{1,0:T(8,128)S(1)} %fusion.22, f32[32,3584]{1,0:T(8,128)S(1)} %convert_multiply_fusion.8), kind=kOutput, calls=%fused_computation | convolution fusion | flops 708313088 | bytes 11534336 | tf_op jit(solution)/shard_map/dot_general | solution.py:44
  293.0 0.0 copy-done.2
  (2 shorter events, 0.0 us)
Async XLA Ops:
  7.2 67.2 %copy-start = (f32[32,3584]{1,0:T(8,128)S(1)}, f32[32,3584]{1,0:T(8,128)}, u32[]{:S(2)}) copy-start(f32[32,3584]{1,0:T(8,128)} %param.9) | copy-start | bytes 1376260
  7.2 54.9 %all-gather.2.cloned.1.call-start = ((), (), s32[]{:S(2)}) async-start(), calls=%async_computation | async-start | bytes 7798784 | tf_op jit(solution)/shard_map/all_gather | solution.py:23
  7.9 164.2 %all-reduce.3.cloned.1.call-start = ((), (), s32[]{:S(2)}) async-start(), calls=%async_computation.1 | async-start | bytes 131072 | tf_op jit(solution)/shard_map/psum | solution.py:38
  71.4 3.0 copy-start.1
  81.7 200.6 %all-reduce.5.cloned.1.call-start = ((), (), s32[]{:S(2)}) async-start(), calls=%async_computation.2 | async-start | bytes 458752 | tf_op jit(solution)/shard_map/psum | solution.py:43
  181.1 102.2 %copy-start.3 = (f32[32,512]{1,0:T(8,128)}, f32[32,512]{1,0:T(8,128)S(1)}, u32[]{:S(2)}) copy-start(f32[32,512]{1,0:T(8,128)S(1)} %fusion.22) | copy-start | bytes 196612
  181.1 7.3 %copy-start.4 = (bf16[2,1024,512]{2,1,0:T(8,128)(2,1)S(1)}, bf16[2,1024,512]{2,1,0:T(8,128)(2,1)}, u32[]{:S(2)}) copy-start(bf16[2,1024,512]{2,1,0:T(8,128)(2,1)} %param.6) | copy-start | bytes 6291460
  283.4 9.7 %copy-start.2 = (f32[32,3584]{1,0:T(8,128)}, f32[32,3584]{1,0:T(8,128)S(1)}, u32[]{:S(2)}) copy-start(f32[32,3584]{1,0:T(8,128)S(1)} %convert_multiply_fusion.8) | copy-start | bytes 1376260
Sparse Core Ops, SparseCore 0:
  9.8 52.2 all-gather.1
  81.9 90.2 all-reduce.2
  188.6 93.7 all-reduce.4
where the time goes:
time: 300 us
  waiting for transfers between devices  228 us (76%)
  matrix products  45.2 us (15%)
  between operations  13.9 us (5%)
  other arithmetic  9.17 us (3%)
  local copies, waits for them, and re-layouts  3.05 us (1%)
    psum x1, waiting for transfers between devices, on_device(): left_mean = lax.psum(left_local, 'dp') / dp_count  90.2 us
    psum x1, waiting for transfers between devices, on_device(): lax.psum(right_local.astype(jnp.bfloat16), 'dp').astype(jnp.float32)  83 us
    all_gather x1, waiting for transfers between devices, on_device(): collected_factors = lax.all_gather(grad_out, 'tensor', axis=0, tiled=True)  54.2 us
    dot_general x1, matrix products, on_device(): lax.dot_general(orthonormal_left, right_average, (((0,), (0,)), ((), ()))...  9.64 us
    dot_general x1, matrix products, on_device(): lax.dot_general(collected_factors, down_weight, (((1,), (1,)), ((), ())),...  9.44 us
    dot_general x1, matrix products, on_device(): lax.dot_general(hidden, collected_factors, (((0,), (0,)), ((), ())), pref...  9.25 us
    dot_general x1, matrix products, on_device(): lax.dot_general(merged, q_start, (((1,), (1,)), ((), ())), precision=high...  7.38 us
    dot_general x1, matrix products, on_device(): right_local = jnp.dot(orthonormal_left, merged, precision=highest_precision)  7.28 us
  transfers between devices with their start and end apart: 3, of which 3 were waited for; matrix products, arithmetic and copies ran while one was open for 4% of the time, Pallas kernels for 0%

commit v1 on v0

v1 whole, which is shorter than its diff:
```python
import functools

import jax
import jax.numpy as jnp
from jax import lax
from jax.experimental import pallas as pl
from jax.experimental.pallas import tpu as pltpu
from jax.sharding import PartitionSpec as P

BF = jnp.bfloat16
F32 = jnp.float32
HI = lax.Precision.HIGHEST
DP = 16
NZ = 8
TOK = 64
CHIP = 2 * TOK
D = 3584
UNITS = 512
ROWS = 1024
RANK = 32
BLK = 512
NBLK = D // BLK
VMEM = 56 * 1024 * 1024


def gelu_pair(value):
    coeff = 0.7978845608028654
    tanh_val = jnp.tanh(coeff * (value + 0.044715 * value * value * value))
    gelu_value = 0.5 * value * (1.0 + tanh_val)
    gelu_slope = 0.5 * (1.0 + tanh_val) + 0.5 * value * (1.0 - tanh_val * tanh_val) * coeff * (
        1.0 + 3.0 * 0.044715 * value * value
    )
    return (gelu_value, gelu_slope)


def split(value, terms):
    parts = []
    for _ in range(terms):
        part = value.astype(BF)
        parts.append(part)
        value = value - part.astype(F32)
    return parts


def dot(a, b, ca, cb, precision=None):
    return lax.dot_general(
        a, b, (((ca,), (cb,)), ((), ())), preferred_element_type=F32, precision=precision
    )


def fold(stacked, terms):
    total = stacked[0:RANK]
    for k in range(1, terms):
        total = total + stacked[k * RANK : (k + 1) * RANK]
    return total


def step_z(value, k):
    return lax.ppermute(value, "tensor", [(i, (i + 2 * k) % (2 * NZ)) for i in range(2 * NZ)])


def other_core(value):
    return lax.ppermute(value, "tensor", [(i, i ^ 1) for i in range(2 * NZ)])


def step_xy(value, dx, dy):
    return lax.ppermute(
        value,
        "dp",
        [(4 * x + y, 4 * ((x + dx) % 4) + (y + dy) % 4) for x in range(4) for y in range(4)],
    )


def source_rows(z, core):
    rows = [z * CHIP + core * TOK, z * CHIP + (1 - core) * TOK]
    for s in (1, 2, 3):
        behind = lax.rem(z + NZ - s, NZ) * CHIP
        ahead = lax.rem(z + s, NZ) * CHIP
        rows += [behind + core * TOK, ahead + core * TOK]
        rows += [behind + (1 - core) * TOK, ahead + (1 - core) * TOK]
    return rows


def main_kernel(place, *refs):
    pieces = refs[:14]
    hidden_t, error, q3, merged, merged_b, left, tokens_out, tokens, g_acc, e_acc, sems, out_sem = refs[14:]
    i = pl.program_id(0)
    z, core = place[0], place[1]

    def copies():
        return [
            pltpu.make_async_copy(
                piece, tokens.at[pl.ds(pl.multiple_of(row, TOK), TOK), :], sems.at[k]
            )
            for k, (piece, row) in enumerate(zip(pieces, source_rows(z, core)))
        ]

    @pl.when(i == 0)
    def _():
        for copy in copies():
            copy.start()
        far = pl.multiple_of(lax.rem(z + 4, NZ) * CHIP, CHIP)
        tokens[pl.ds(far, CHIP), :] = jnp.zeros((CHIP, D), BF)
        g_acc[...] = jnp.zeros_like(g_acc)
        e_acc[...] = jnp.zeros_like(e_acc)
        for copy in copies():
            copy.wait()
        pltpu.make_async_copy(tokens, tokens_out, out_sem).start()

    columns = pl.ds(pl.multiple_of(i * BLK, BLK), BLK)
    block = tokens[:, columns]
    err = error[...]
    total = dot(hidden_t[...], block, 1, 0) + err.astype(F32)
    merged[...] = total
    merged_b[...] = total.astype(BF)
    q = q3[...]
    g_acc[...] += dot(q, block, 1, 1)
    e_acc[...] += dot(q, err, 1, 1)

    @pl.when(i == NBLK - 1)
    def _():
        g = jnp.concatenate(split(fold(g_acc[...], 3), 2), axis=0)
        left[...] = fold(e_acc[...], 3) + fold(dot(g, hidden_t[...], 1, 1), 2)
        pltpu.make_async_copy(tokens, tokens_out, out_sem).wait()


def main_call(place, pieces, hidden_t, error, q3):
    whole = lambda shape: pl.BlockSpec(shape, lambda i, p: (0, 0))
    cols = lambda rows: pl.BlockSpec((rows, BLK), lambda i, p: (0, i))
    return pl.pallas_call(
        main_kernel,
        grid_spec=pltpu.PrefetchScalarGridSpec(
            num_scalar_prefetch=1,
            grid=(NBLK,),
            in_specs=[pl.BlockSpec(memory_space=pl.ANY)] * 14
            + [whole((UNITS, ROWS)), cols(UNITS), cols(3 * RANK)],
            out_specs=[
                cols(UNITS),
                cols(UNITS),
                whole((RANK, UNITS)),
                pl.BlockSpec(memory_space=pl.ANY),
            ],
            scratch_shapes=[
                pltpu.VMEM((ROWS, D), BF),
                pltpu.VMEM((3 * RANK, ROWS), F32),
                pltpu.VMEM((3 * RANK, UNITS), F32),
                pltpu.SemaphoreType.DMA((14,)),
                pltpu.SemaphoreType.DMA,
            ],
        ),
        out_shape=[
            jax.ShapeDtypeStruct((UNITS, D), F32),
            jax.ShapeDtypeStruct((UNITS, D), BF),
            jax.ShapeDtypeStruct((RANK, UNITS), F32),
            jax.ShapeDtypeStruct((ROWS, D), BF),
        ],
        compiler_params=pltpu.CompilerParams(vmem_limit_bytes=VMEM),
        cost_estimate=pl.CostEstimate(
            flops=2 * ROWS * UNITS * D, bytes_accessed=30_000_000, transcendentals=0
        ),
        name="weight_grad",
    )(place, *pieces, hidden_t, error, q3)


def last_kernel(place, f4, b4, cf4, cb4, hidden_t, q3, left_in, left, last):
    core = place[1]
    half = TOK // 2
    mine = core * TOK
    theirs = (1 - core) * TOK
    last[pl.ds(pl.multiple_of(mine, half), half), :] = f4[...]
    last[pl.ds(pl.multiple_of(mine + half, half), half), :] = b4[...]
    last[pl.ds(pl.multiple_of(theirs, half), half), :] = cf4[...]
    last[pl.ds(pl.multiple_of(theirs + half, half), half), :] = cb4[...]
    far = pl.multiple_of(lax.rem(place[0] + 4, NZ) * CHIP, CHIP)
    g = jnp.concatenate(split(fold(dot(q3[...], last[...], 1, 1), 3), 2), axis=0)
    left[...] = left_in[...] + fold(dot(g, hidden_t[:, pl.ds(far, CHIP)], 1, 1), 2)


def last_call(place, f4, b4, cf4, cb4, hidden_t, q3, left_in):
    smem = pl.BlockSpec(memory_space=pltpu.SMEM)
    vmem = pl.BlockSpec(memory_space=pltpu.VMEM)
    return pl.pallas_call(
        last_kernel,
        in_specs=[smem] + [vmem] * 7,
        out_specs=[vmem] * 2,
        out_shape=[
            jax.ShapeDtypeStruct((RANK, UNITS), F32),
            jax.ShapeDtypeStruct((CHIP, D), BF),
        ],
        compiler_params=pltpu.CompilerParams(vmem_limit_bytes=VMEM),
        cost_estimate=pl.CostEstimate(flops=10**8, bytes_accessed=3_000_000, transcendentals=0),
        name="left_last",
    )(place, f4, b4, cf4, cb4, hidden_t, q3, left_in)


def right_kernel(place, l0, l1, l2, l3, hidden_t, last, merged_b, p_out, p3_out, right, p2, h2):
    i = pl.program_id(0)

    @pl.when(i == 0)
    def _():
        left = ((l0[...] + l2[...]) + (l1[...] + l3[...])) * (1.0 / DP)
        rest = dot(left, left, 1, 1, HI)
        rows = lax.broadcasted_iota(jnp.int32, (RANK, RANK), 0)
        inverse = (rows == lax.broadcasted_iota(jnp.int32, (RANK, RANK), 1)).astype(F32)
        for k in range(RANK):
            scale = lax.rsqrt(rest[k : k + 1, k : k + 1])
            column = jnp.where(rows[:, 0:1] > k, rest[:, k : k + 1] * scale, 0.0)
            rest_row = rest[k : k + 1, :] * scale
            inverse_row = inverse[k : k + 1, :] * scale
            rest = rest - column * rest_row
            inverse = jnp.where(rows == k, inverse_row, inverse - column * inverse_row)
        factor = dot(inverse, left, 1, 0, HI)
        p_out[...] = factor
        high, low = split(factor, 2)
        p2[...] = jnp.concatenate([high, low], axis=0)
        p3_out[...] = jnp.concatenate([high, low, high], axis=0)
        far = pl.multiple_of(lax.rem(place[0] + 4, NZ) * CHIP, CHIP)
        mine = fold(dot(p2[...], hidden_t[:, pl.ds(far, CHIP)], 1, 0), 2)
        h2[...] = jnp.concatenate(split(mine, 2), axis=0)

    total = dot(p2[...], merged_b[...], 1, 0) + dot(h2[...], last[...], 1, 0)
    right[...] = fold(total, 2).astype(BF)


def right_call(place, lefts, hidden_t, last, merged_b):
    whole = lambda shape: pl.BlockSpec(shape, lambda i, p: (0, 0))
    cols = lambda rows: pl.BlockSpec((rows, BLK), lambda i, p: (0, i))
    return pl.pallas_call(
        right_kernel,
        grid_spec=pltpu.PrefetchScalarGridSpec(
            num_scalar_prefetch=1,
            grid=(NBLK,),
            in_specs=[whole((RANK, UNITS))] * 4
            + [whole((UNITS, ROWS)), cols(CHIP), cols(UNITS)],
            out_specs=[whole((RANK, UNITS)), whole((3 * RANK, UNITS)), cols(RANK)],
            scratch_shapes=[pltpu.VMEM((2 * RANK, UNITS), BF), pltpu.VMEM((2 * RANK, CHIP), BF)],
        ),
        out_shape=[
            jax.ShapeDtypeStruct((RANK, UNITS), F32),
            jax.ShapeDtypeStruct((3 * RANK, UNITS), BF),
            jax.ShapeDtypeStruct((RANK, D), BF),
        ],
        compiler_params=pltpu.CompilerParams(vmem_limit_bytes=VMEM),
        cost_estimate=pl.CostEstimate(flops=10**8, bytes_accessed=6_000_000, transcendentals=0),
        name="right_factor",
    )(place, *lefts, hidden_t, last, merged_b)


def error_kernel(place, p3, hidden_t, last, merged, q, out, p3_t, h_last):
    @pl.when(pl.program_id(0) == 0)
    def _():
        p3_t[...] = jnp.transpose(p3[...].astype(F32)).astype(BF)
        far = pl.multiple_of(lax.rem(place[0] + 4, NZ) * CHIP, CHIP)
        h_last[...] = hidden_t[:, pl.ds(far, CHIP)]

    high, low = split(q[...], 2)
    q3 = jnp.concatenate([high, high, low], axis=0)
    total = merged[...] + dot(h_last[...], last[...], 1, 0) - dot(p3_t[...], q3, 1, 0)
    out[...] = total.astype(BF)


def error_call(place, p3, hidden_t, last, merged, q):
    whole = lambda shape: pl.BlockSpec(shape, lambda i, p: (0, 0))
    cols = lambda rows: pl.BlockSpec((rows, BLK), lambda i, p: (0, i))
    return pl.pallas_call(
        error_kernel,
        grid_spec=pltpu.PrefetchScalarGridSpec(
            num_scalar_prefetch=1,
            grid=(NBLK,),
            in_specs=[
                whole((3 * RANK, UNITS)),
                whole((UNITS, ROWS)),
                cols(CHIP),
                cols(UNITS),
                cols(RANK),
            ],
            out_specs=cols(UNITS),
            scratch_shapes=[pltpu.VMEM((UNITS, 3 * RANK), BF), pltpu.VMEM((UNITS, CHIP), BF)],
        ),
        out_shape=jax.ShapeDtypeStruct((UNITS, D), BF),
        compiler_params=pltpu.CompilerParams(vmem_limit_bytes=VMEM),
        cost_estimate=pl.CostEstimate(flops=10**9, bytes_accessed=12_000_000, transcendentals=0),
        name="new_error",
    )(place, p3, hidden_t, last, merged, q)


TBLK = 256


def pre_kernel(place, tokens, last, weight, pre, out, grad):
    i = pl.program_id(0)
    far = lax.rem(place[0] + 4, NZ)
    grad[...] = dot(tokens[...], weight[...], 1, 1)

    @pl.when(i == far // 2)
    def _():
        row = pl.multiple_of(lax.rem(far, 2) * CHIP, CHIP)
        grad[pl.ds(row, CHIP), :] = dot(last[...], weight[...], 1, 1)

    up = pre[1].astype(F32)
    value, slope = gelu_pair(pre[0].astype(F32))
    out[0] = (grad[...] * up * slope).astype(BF)
    out[1] = (grad[...] * value).astype(BF)


def pre_call(place, tokens, last, weight, pre):
    whole = lambda shape: pl.BlockSpec(shape, lambda i, p: (0, 0))
    return pl.pallas_call(
        pre_kernel,
        grid_spec=pltpu.PrefetchScalarGridSpec(
            num_scalar_prefetch=1,
            grid=(ROWS // TBLK,),
            in_specs=[
                pl.BlockSpec((TBLK, D), lambda i, p: (i, 0)),
                whole((CHIP, D)),
                whole((UNITS, D)),
                pl.BlockSpec((2, TBLK, UNITS), lambda i, p: (0, i, 0)),
            ],
            out_specs=pl.BlockSpec((2, TBLK, UNITS), lambda i, p: (0, i, 0)),
            scratch_shapes=[pltpu.VMEM((TBLK, UNITS), F32)],
        ),
        out_shape=jax.ShapeDtypeStruct((2, ROWS, UNITS), BF),
        compiler_params=pltpu.CompilerParams(vmem_limit_bytes=VMEM),
        cost_estimate=pl.CostEstimate(
            flops=2 * ROWS * UNITS * D, bytes_accessed=16_000_000, transcendentals=0
        ),
        name="grad_pre",
    )(place, tokens, last, weight, pre)


def sum_of_four(a, b, c, d):
    return (a + c) + (b + d)


def on_device(grad_out, pre_act, down_weight, error, q_start):
    index = lax.axis_index("tensor")
    place = jnp.stack([index // 2, lax.rem(index, 2)]).astype(jnp.int32)

    gelu_value, _ = gelu_pair(pre_act[0].astype(F32))
    hidden_t = (gelu_value * pre_act[1].astype(F32)).astype(BF).T
    q3 = jnp.concatenate(split(q_start, 3), axis=0)

    pieces = [grad_out, other_core(grad_out)]
    ahead = behind = grad_out
    for _ in range(3):
        behind, ahead = step_z(behind, 1), step_z(ahead, -1)
        pieces += [behind, ahead, other_core(behind), other_core(ahead)]
    half = TOK // 2
    behind, ahead = step_z(behind[:half], 1), step_z(ahead[half:], -1)

    merged, merged_b, left, tokens = main_call(place, pieces, hidden_t, error, q3)
    left, last = last_call(
        place, behind, ahead, other_core(behind), other_core(ahead), hidden_t, q3, left
    )

    left = sum_of_four(left, *[step_xy(left, k, 0) for k in (1, 2, 3)])
    lefts = [left] + [step_xy(left, 0, k) for k in (1, 2, 3)]
    grad_pre = pre_call(place, tokens, last, down_weight, pre_act)
    p_factor, p3, right = right_call(place, lefts, hidden_t, last, merged_b)

    parts = lax.all_to_all(right.reshape(DP, RANK // DP, D), "dp", 0, 0, tiled=True)
    mine = jnp.sum(parts.astype(F32), axis=0).astype(BF)
    right = lax.all_to_all(
        jnp.broadcast_to(mine[None], (DP, RANK // DP, D)), "dp", 0, 0, tiled=True
    ).reshape(RANK, D)
    q_factor = right.astype(F32) * (1.0 / DP)
    new_error = error_call(place, p3, hidden_t, last, merged, q_factor)
    return (grad_pre, new_error, p_factor, q_factor)


def solution(mesh):
    placed = (
        P(("dp", "tensor"), None),
        P(None, "dp", "tensor"),
        P("tensor", None),
        P(("dp", "tensor"), None),
        P("tensor", None),
    )
    return jax.shard_map(
        on_device,
        mesh=mesh,
        in_specs=placed,
        out_specs=(
            P(None, "dp", "tensor"),
            P(("dp", "tensor"), None),
            P(None, "tensor"),
            P("tensor", None),
        ),
        check_vma=False,
    )
```

time: 300 us -> 154 us (0.51)
  waiting for transfers between devices: 228 us -> 41.1 us
  Pallas kernels: 0 us -> 52.8 us
  matrix products: 45.2 us -> 0 us
  starting transfers between devices: 0.3 us -> 29.6 us
  blocking collectives: 0 us -> 14.7 us
  between operations: 13.9 us -> 0.88 us
  local copies, waits for them, and re-layouts: 3.05 us -> 7.41 us
  other arithmetic: 9.17 us -> 5.8 us
    psum x2 -> x0, waiting for transfers between devices: 173 us -> none  [the longest x1 90.2 us: on_device(): left_mean = lax.psum(left_local, 'dp') / dp_count]
    all_gather x1 -> x0, waiting for transfers between devices: 54.2 us -> none  [on_device(): collected_factors = lax.all_gather(grad_out, 'tensor', axis=0, tiled=True)]
    pallas_call x0 -> x5, Pallas kernels: none -> 52.8 us  [the longest x1 16.8 us: main_call(): pl.pallas_call(main_kernel, grid_spec=pltpu.PrefetchScalarGridSpec(num_sc...]
    dot_general x6 -> x0, matrix products: 44.1 us -> none  [the longest x1 9.64 us: on_device(): lax.dot_general(orthonormal_left, right_average, (((0,), (0,)), ((), ()))...]
    ppermute x0 -> x23, waiting for transfers between devices: none -> 41.1 us  [the longest x8 35.7 us: step_z(): lax.ppermute(value, 'tensor', [(i, (i + 2 * k) % (2 * NZ)) for i in range...]
    ppermute x0 -> x23, starting transfers between devices: none -> 25.9 us  [the longest x8 12.8 us: step_z(): lax.ppermute(value, 'tensor', [(i, (i + 2 * k) % (2 * NZ)) for i in range...]
    all_to_all x0 -> x1, blocking collectives: none -> 14.7 us  [on_device(): lax.all_to_all(right.reshape(DP, RANK // DP, D), 'dp', 0, 0, tiled=True)]
    another operation x6 -> x1, other arithmetic: 8.19 us -> 0.6 us  [on_device(): place = jnp.stack([index // 2, lax.rem(index, 2)]).astype(jnp.int32)]
  transfers between devices with their start and end apart: 3 -> 24, of which waited for: 3 -> 10; matrix products, arithmetic and copies ran while one was open for 4% -> 5% of each run, Pallas kernels for 0% -> 19%
where the time goes in v1:
time: 154 us; the launch traced here: 152 us
  Pallas kernels  52.8 us (34%)
  waiting for transfers between devices  41.1 us (27%)
  starting transfers between devices  29.6 us (19%)
  blocking collectives  14.7 us (10%)
  local copies, waits for them, and re-layouts  7.41 us (5%)
  other arithmetic  5.8 us (4%)
    ppermute x8, waiting for transfers between devices, step_z(): lax.ppermute(value, 'tensor', [(i, (i + 2 * k) % (2 * NZ)) for i in range...  35.7 us
    pallas_call x1, Pallas kernels, main_call(): pl.pallas_call(main_kernel, grid_spec=pltpu.PrefetchScalarGridSpec(num_sc...  16.8 us
    all_to_all x1, blocking collectives, on_device(): lax.all_to_all(right.reshape(DP, RANK // DP, D), 'dp', 0, 0, tiled=True)  14.7 us
    ppermute x8, starting transfers between devices, step_z(): lax.ppermute(value, 'tensor', [(i, (i + 2 * k) % (2 * NZ)) for i in range...  12.8 us
    pallas_call x1, Pallas kernels, pre_call(): pl.pallas_call(pre_kernel, grid_spec=pltpu.PrefetchScalarGridSpec(num_sca...  12.5 us
    ppermute x6, starting transfers between devices, step_xy(): lax.ppermute(value, 'dp', [(4 * x + y, 4 * ((x + dx) % 4) + (y + dy) % 4)...  12.2 us
    pallas_call x1, Pallas kernels, right_call(): pl.pallas_call(right_kernel, grid_spec=pltpu.PrefetchScalarGridSpec(num_s...  10.4 us
    pallas_call x1, Pallas kernels, error_call(): pl.pallas_call(error_kernel, grid_spec=pltpu.PrefetchScalarGridSpec(num_s...  10.1 us
  transfers between devices with their start and end apart: 24, of which 10 were waited for; matrix products, arithmetic and copies ran while one was open for 5% of the time, Pallas kernels for 19%

profile of v1, /device:TPU:96, one launch (start us, length us, event | category | flops | bytes accessed | tf_op | source)
XLA Modules:
  0.0 152.3 jit_solution(3121833414972698946)
XLA Ops:
  0.6 3.2 %collective-permute-start.1 = (bf16[64,3584]{1,0:T(8,128)(2,1)}, bf16[64,3584]{1,0:T(8,128)(2,1)S(1)}, u32[]{:S(2)}, u32[]{:S(2)}) collective-permute-start(bf16[64,3584]{1,0:T(8,128)(2,1)} %refs_0_.1), channel_id=1, source_target_pairs={{0,2},{1,3},{2,4},{3,5},{4,6},{5,7},{6,8},{7,9},{8,10},{9,11},{10,... | collective-permute-start | bytes 1376264 | tf_op jit(solution)/shard_map/ppermute | solution.py:59
  3.9 10.1 %collective-permute-done.1.refs_2_ = bf16[64,3584]{1,0:T(8,128)(2,1)S(1)} collective-permute-done((bf16[64,3584]{1,0:T(8,128)(2,1)}, bf16[64,3584]{1,0:T(8,128)(2,1)S(1)}, u32[]{:S(2)}, u32[]{:S(2)}) %collective-permute-start.1) | collective-permute-done | bytes 458784 | tf_op jit(solution)/shard_map/ppermute | solution.py:59
  13.9 3.6 %collective-permute-start.5 = (bf16[64,3584]{1,0:T(8,128)(2,1)S(1)}, bf16[64,3584]{1,0:T(8,128)(2,1)}, u32[]{:S(2)}, u32[]{:S(2)}) collective-permute-start(bf16[64,3584]{1,0:T(8,128)(2,1)S(1)} %collective-permute-done.1.refs_2_), channel_id=1, source_target_pairs={{0,2},{1,3},{2,4},{3,5},{4,6},{5,7},{6,8},{7,9},{8,10},{9,11},{10,... | collective-permute-start | bytes 1376264 | tf_op jit(solution)/shard_map/ppermute | solution.py:59
  17.5 1.2 fusion.9
  18.8 0.1 collective-permute-start.3
  18.9 0.5 collective-permute-start.4
  19.4 7.1 %collective-permute-done.5.refs_6_ = bf16[64,3584]{1,0:T(8,128)(2,1)} collective-permute-done((bf16[64,3584]{1,0:T(8,128)(2,1)S(1)}, bf16[64,3584]{1,0:T(8,128)(2,1)}, u32[]{:S(2)}, u32[]{:S(2)}) %collective-permute-start.5) | collective-permute-done | bytes 458784 | tf_op jit(solution)/shard_map/ppermute | solution.py:59
  26.4 3.8 %collective-permute-start.9 = (bf16[64,3584]{1,0:T(8,128)(2,1)}, bf16[64,3584]{1,0:T(8,128)(2,1)}, u32[]{:S(2)}, u32[]{:S(2)}) collective-permute-start(bf16[64,3584]{1,0:T(8,128)(2,1)} %collective-permute-done.5.refs_6_), channel_id=1, source_target_pairs={{0,2},{1,3},{2,4},{3,5},{4,6},{5,7},{6,8},{7,9},{8,10},{9,11},{10,... | collective-permute-start | bytes 1376264 | tf_op jit(solution)/shard_map/ppermute | solution.py:59
  30.2 0.1 collective-permute-start.10
  30.3 0.9 pad_maximum_fusion.refs_16_.q3
  31.2 0.4 collective-permute-start.8
  31.7 6.9 %collective-permute-done.9.refs_10_ = bf16[64,3584]{1,0:T(8,128)(2,1)} collective-permute-done((bf16[64,3584]{1,0:T(8,128)(2,1)}, bf16[64,3584]{1,0:T(8,128)(2,1)}, u32[]{:S(2)}, u32[]{:S(2)}) %collective-permute-start.9) | collective-permute-done | bytes 458784 | tf_op jit(solution)/shard_map/ppermute | solution.py:59
  38.5 6.2 %collective-permute-done.10.refs_11_ = bf16[64,3584]{1,0:T(8,128)(2,1)} collective-permute-done((bf16[64,3584]{1,0:T(8,128)(2,1)}, bf16[64,3584]{1,0:T(8,128)(2,1)}, u32[]{:S(2)}, u32[]{:S(2)}) %collective-permute-start.10) | collective-permute-done | bytes 458784 | tf_op jit(solution)/shard_map/ppermute | solution.py:59
  44.7 0.1 fusion.8
  44.9 0.5 copy.11
  45.4 0.5 copy.12
  46.0 0.6 pad_add_fusion.place
  46.6 1.0 slice.16
  47.5 1.0 slice.17
  48.6 2.0 %collective-permute-start.14 = (bf16[32,3584]{1,0:T(8,128)(2,1)S(1)}, bf16[32,3584]{1,0:T(8,128)(2,1)S(1)}, u32[]{:S(2)}, u32[]{:S(2)}) collective-permute-start(bf16[32,3584]{1,0:T(8,128)(2,1)S(1)} %slice.17), channel_id=1, source_target_pairs={{0,14},{1,15},{2,0},{3,1},{4,2},{5,3},{6,4},{7,5},{8,6},{9,7},{10,... | collective-permute-start | bytes 688136 | tf_op jit(solution)/shard_map/ppermute | solution.py:59
  50.6 1.8 %fusion.6.refs_14_.hidden_t = bf16[512,1024]{1,0:T(8,128)(2,1)} fusion(bf16[1,1024,512]{1,2,0:T(8,128)(2,1)S(1)} %copy.12, bf16[1,1024,512]{1,2,0:T(8,128)(2,1)S(1)} %copy.11), kind=kLoop, calls=%fused_computation.11 | loop fusion | flops 6291456 | bytes 3145728 | tf_op jit(solution)/shard_map/transpose | solution.py:340
  52.4 4.1 %collective-permute-done.13.f4 = bf16[32,3584]{1,0:T(8,128)(2,1)S(1)} collective-permute-done((bf16[32,3584]{1,0:T(8,128)(2,1)S(1)}, bf16[32,3584]{1,0:T(8,128)(2,1)S(1)}, u32[]{:S(2)}, u32[]{:S(2)}) %collective-permute-start.13) | collective-permute-done | bytes 229408 | tf_op jit(solution)/shard_map/ppermute | solution.py:59
  56.6 1.3 collective-permute-done.14.b4
  57.9 16.8 %weight_grad.1 = (f32[512,3584]{1,0:T(8,128)}, bf16[512,3584]{1,0:T(8,128)(2,1)}, f32[32,512]{1,0:T(8,128)}, bf16[1024,3584]{1,0:T(8,128)(2,1)}) custom-call(s32[2]{0:T(128)} %pad_add_fusion.place, bf16[64,3584]{1,0:T(8,128)(2,1)} %refs_0_.1, bf16[64,3584]{1,0:T(8,128)(2,1)} %collective-permute-done.refs_1_, bf16[64,3584]{1,0:T(8,128)(2,1)} %copy-done.9, ...), custom_call_target="tpu_custom_call" | custom-call | flops 3758096384 | bytes 30000000 | tf_op jit(solution)/shard_map/weight_grad/pallas_call | solution.py:130
  74.8 0.7 copy-done.4
  75.5 3.1 %left_last.1 = (f32[32,512]{1,0:T(8,128)}, bf16[128,3584]{1,0:T(8,128)(2,1)}) custom-call(s32[2]{0:T(128)} %pad_add_fusion.place, bf16[32,3584]{1,0:T(8,128)(2,1)} %copy-done.2, bf16[32,3584]{1,0:T(8,128)(2,1)} %copy-done.3, bf16[32,3584]{1,0:T(8,128)(2,1)} %copy-done.4, bf16[32,3584]{1,0:T(8,128)(2,1)} %copy-done.5, ...), custom_call_target="tpu_custom_call" | custom-call | flops 100000000 | bytes 3000000 | tf_op jit(solution)/shard_map/left_last/pallas_call | solution.py:182
  78.6 3.0 %collective-permute-start.17 = (f32[32,512]{1,0:T(8,128)}, f32[32,512]{1,0:T(8,128)S(1)}, u32[]{:S(2)}, u32[]{:S(2)}) collective-permute-start(f32[32,512]{1,0:T(8,128)} %get-tuple-element.16), channel_id=1, source_target_pairs={{0,128},{16,144},{32,160},{48,176},{64,192},{80,208},{96,224},{112... | collective-permute-start | bytes 196616 | tf_op jit(solution)/shard_map/ppermute | solution.py:67
  81.6 0.6 collective-permute-start.18
  82.2 2.6 %collective-permute-start.19 = (f32[32,512]{1,0:T(8,128)}, f32[32,512]{1,0:T(8,128)S(1)}, u32[]{:S(2)}, u32[]{:S(2)}) collective-permute-start(f32[32,512]{1,0:T(8,128)} %get-tuple-element.16), channel_id=1, source_target_pairs={{0,192},{16,208},{32,224},{48,240},{64,0},{80,16},{96,32},{112,48}... | collective-permute-start | bytes 196616 | tf_op jit(solution)/shard_map/ppermute | solution.py:67
  84.9 2.4 %collective-permute-done.18 = f32[32,512]{1,0:T(8,128)S(1)} collective-permute-done((f32[32,512]{1,0:T(8,128)}, f32[32,512]{1,0:T(8,128)S(1)}, u32[]{:S(2)}, u32[]{:S(2)}) %collective-permute-start.18) | collective-permute-done | bytes 65568 | tf_op jit(solution)/shard_map/ppermute | solution.py:67
  87.3 0.9 add_add_fusion.l0
  88.2 1.7 %collective-permute-start.20 = (f32[32,512]{1,0:T(8,128)S(1)}, f32[32,512]{1,0:T(8,128)S(1)}, u32[]{:S(2)}, u32[]{:S(2)}) collective-permute-start(f32[32,512]{1,0:T(8,128)S(1)} %add_add_fusion.l0), channel_id=1, source_target_pairs={{0,16},{16,32},{32,48},{48,0},{64,80},{80,96},{96,112},{112,64},{1... | collective-permute-start | bytes 196616 | tf_op jit(solution)/shard_map/ppermute | solution.py:67
  89.9 2.9 %collective-permute-start.21 = (f32[32,512]{1,0:T(8,128)S(1)}, f32[32,512]{1,0:T(8,128)S(1)}, u32[]{:S(2)}, u32[]{:S(2)}) collective-permute-start(f32[32,512]{1,0:T(8,128)S(1)} %add_add_fusion.l0), channel_id=1, source_target_pairs={{0,32},{16,48},{32,0},{48,16},{64,96},{80,112},{96,64},{112,80},{1... | collective-permute-start | bytes 196616 | tf_op jit(solution)/shard_map/ppermute | solution.py:67
  92.8 1.3 collective-permute-start.22
  94.1 0.4 collective-permute-done.20.l1
  94.5 1.2 collective-permute-done.21.l2
  95.7 1.3 collective-permute-done.22.l3
  97.1 0.6 copy-done.8
  97.7 10.4 %right_factor.1 = (f32[32,512]{1,0:T(8,128)}, bf16[96,512]{1,0:T(8,128)(2,1)}, bf16[32,3584]{1,0:T(8,128)(2,1)}) custom-call(s32[2]{0:T(128)} %pad_add_fusion.place, f32[32,512]{1,0:T(8,128)} %copy-done.1, f32[32,512]{1,0:T(8,128)} %copy-done.6, f32[32,512]{1,0:T(8,128)} %copy-done.7, f32[32,512]{1,0:T(8,128)} %copy-done.8, ...), custom_call_target="tpu_custom_call" | custom-call | flops 100000000 | bytes 6000000 | tf_op jit(solution)/shard_map/right_factor/pallas_call | solution.py:228
  108.1 1.0 reshape.20
  109.1 14.7 %all_to_all.10 = bf16[16,2,3584]{2,1,0:T(2,128)(2,1)S(1)} all-to-all(bf16[16,2,3584]{2,1,0:T(2,128)(2,1)S(1)} %reshape.20), channel_id=1, replica_groups=mesh['dp'=16,'tensor'=16] {'dp'}, dimensions={0} | all-to-all | bytes 458752 | tf_op jit(solution)/shard_map/all_to_all | solution.py:361
  123.8 0.2 reduce_sum.12
  124.0 0.8 broadcast_in_dim.2
  124.8 3.7 %all-to-all-start.1 = ((bf16[16,2,3584]{2,1,0:T(2,128)(2,1)}), bf16[16,2,3584]{2,1,0:T(2,128)(2,1)S(1)}, u32[]{:S(2)}, u32[]{:S(2)}) async-start(bf16[16,2,3584]{2,1,0:T(2,128)(2,1)} %broadcast_in_dim.2), calls=%async_computation.1 | async-start | bytes 458752 | tf_op jit(solution)/shard_map/all_to_all | solution.py:363
  128.5 12.5 %grad_pre.1 = bf16[2,1024,512]{2,1,0:T(8,128)(2,1)} custom-call(s32[2]{0:T(128)} %pad_add_fusion.place, bf16[1024,3584]{1,0:T(8,128)(2,1)} %get-tuple-element.13.tokens, bf16[128,3584]{1,0:T(8,128)(2,1)} %get-tuple-element.15.last, bf16[512,3584]{1,0:T(8,128)(2,1)} %weight.1, bf16[2,1024,512]{2,1,0:T(8,128)(2,1)} %pre.1), custom_call_target="tpu_custom_call" | custom-call | flops 3758096384 | bytes 16000000 | tf_op jit(solution)/shard_map/grad_pre/pallas_call | solution.py:308
  141.0 0.2 convert_multiply_fusion.4
  141.2 1.1 mul.50.q
  142.3 10.1 %new_error.1 = bf16[512,3584]{1,0:T(8,128)(2,1)} custom-call(s32[2]{0:T(128)} %pad_add_fusion.place, bf16[96,512]{1,0:T(8,128)(2,1)} %get-tuple-element.18.p3, bf16[512,1024]{1,0:T(8,128)(2,1)} %fusion.6.refs_14_.hidden_t, bf16[128,3584]{1,0:T(8,128)(2,1)} %get-tuple-element.15.last, f32[512,3584]{1,0:T(8,128)} %get-tuple-element.19.merged, f32[32,3584]{1,0:T(8,128)} %mul.50.q), custom_call_target="tpu_custom_call" | custom-call | flops 1000000000 | bytes 12000000 | tf_op jit(solution)/shard_map/new_error/pallas_call | solution.py:265
  (43 shorter events, 0.3 us)
Async XLA Ops:
  0.6 44.1 %copy-start = (bf16[2,1024,512]{2,1,0:T(8,128)(2,1)S(1)}, bf16[2,1024,512]{2,1,0:T(8,128)(2,1)}, u32[]{:S(2)}) copy-start(bf16[2,1024,512]{2,1,0:T(8,128)(2,1)} %pre.1) | copy-start | bytes 6291460
  0.6 13.3 %collective-permute-start.1 = (bf16[64,3584]{1,0:T(8,128)(2,1)}, bf16[64,3584]{1,0:T(8,128)(2,1)S(1)}, u32[]{:S(2)}, u32[]{:S(2)}) collective-permute-start(bf16[64,3584]{1,0:T(8,128)(2,1)} %refs_0_.1), channel_id=1, source_target_pairs={{0,2},{1,3},{2,4},{3,5},{4,6},{5,7},{6,8},{7,9},{8,10},{9,11},{10,... | collective-permute-start | bytes 1376264 | tf_op jit(solution)/shard_map/ppermute | solution.py:59
  3.8 13.7 %collective-permute-start.2 = (bf16[64,3584]{1,0:T(8,128)(2,1)}, bf16[64,3584]{1,0:T(8,128)(2,1)}, u32[]{:S(2)}, u32[]{:S(2)}) collective-permute-start(bf16[64,3584]{1,0:T(8,128)(2,1)} %refs_0_.1), channel_id=1, source_target_pairs={{0,14},{1,15},{2,0},{3,1},{4,2},{5,3},{6,4},{7,5},{8,6},{9,7},{10,... | collective-permute-start | bytes 1376264 | tf_op jit(solution)/shard_map/ppermute | solution.py:59
  3.9 26.4 %collective-permute-start = (bf16[64,3584]{1,0:T(8,128)(2,1)}, bf16[64,3584]{1,0:T(8,128)(2,1)}, u32[]{:S(2)}, u32[]{:S(2)}) collective-permute-start(bf16[64,3584]{1,0:T(8,128)(2,1)} %refs_0_.1), channel_id=1, source_target_pairs={{0,1},{1,0},{2,3},{3,2},{4,5},{5,4},{6,7},{7,6},{8,9},{9,8},{10,11... | collective-permute-start | bytes 1376264 | tf_op jit(solution)/shard_map/ppermute | solution.py:63
  13.9 30.8 %copy-start.9 = (bf16[64,3584]{1,0:T(8,128)(2,1)}, bf16[64,3584]{1,0:T(8,128)(2,1)S(1)}, u32[]{:S(2)}) copy-start(bf16[64,3584]{1,0:T(8,128)(2,1)S(1)} %collective-permute-done.1.refs_2_) | copy-start | bytes 1376260
  13.9 12.5 %collective-permute-start.5 = (bf16[64,3584]{1,0:T(8,128)(2,1)S(1)}, bf16[64,3584]{1,0:T(8,128)(2,1)}, u32[]{:S(2)}, u32[]{:S(2)}) collective-permute-start(bf16[64,3584]{1,0:T(8,128)(2,1)S(1)} %collective-permute-done.1.refs_2_), channel_id=1, source_target_pairs={{0,2},{1,3},{2,4},{3,5},{4,6},{5,7},{6,8},{7,9},{8,10},{9,11},{10,... | collective-permute-start | bytes 1376264 | tf_op jit(solution)/shard_map/ppermute | solution.py:59
  17.5 12.7 %collective-permute-start.6 = (bf16[64,3584]{1,0:T(8,128)(2,1)}, bf16[64,3584]{1,0:T(8,128)(2,1)}, u32[]{:S(2)}, u32[]{:S(2)}) collective-permute-start(bf16[64,3584]{1,0:T(8,128)(2,1)} %collective-permute-done.2.refs_3_), channel_id=1, source_target_pairs={{0,14},{1,15},{2,0},{3,1},{4,2},{5,3},{6,4},{7,5},{8,6},{9,7},{10,... | collective-permute-start | bytes 1376264 | tf_op jit(solution)/shard_map/ppermute | solution.py:59
  18.8 12.5 %collective-permute-start.3 = (bf16[64,3584]{1,0:T(8,128)(2,1)S(1)}, bf16[64,3584]{1,0:T(8,128)(2,1)S(1)}, u32[]{:S(2)}, u32[]{:S(2)}) collective-permute-start(bf16[64,3584]{1,0:T(8,128)(2,1)S(1)} %collective-permute-done.1.refs_2_), channel_id=1, source_target_pairs={{0,1},{1,0},{2,3},{3,2},{4,5},{5,4},{6,7},{7,6},{8,9},{9,8},{10,11... | collective-permute-start | bytes 1376264 | tf_op jit(solution)/shard_map/ppermute | solution.py:63
  18.9 29.6 %collective-permute-start.4 = (bf16[64,3584]{1,0:T(8,128)(2,1)}, bf16[64,3584]{1,0:T(8,128)(2,1)}, u32[]{:S(2)}, u32[]{:S(2)}) collective-permute-start(bf16[64,3584]{1,0:T(8,128)(2,1)} %collective-permute-done.2.refs_3_), channel_id=1, source_target_pairs={{0,1},{1,0},{2,3},{3,2},{4,5},{5,4},{6,7},{7,6},{8,9},{9,8},{10,11... | collective-permute-start | bytes 1376264 | tf_op jit(solution)/shard_map/ppermute | solution.py:63
  26.4 12.1 %collective-permute-start.9 = (bf16[64,3584]{1,0:T(8,128)(2,1)}, bf16[64,3584]{1,0:T(8,128)(2,1)}, u32[]{:S(2)}, u32[]{:S(2)}) collective-permute-start(bf16[64,3584]{1,0:T(8,128)(2,1)} %collective-permute-done.5.refs_6_), channel_id=1, source_target_pairs={{0,2},{1,3},{2,4},{3,5},{4,6},{5,7},{6,8},{7,9},{8,10},{9,11},{10,... | collective-permute-start | bytes 1376264 | tf_op jit(solution)/shard_map/ppermute | solution.py:59
  30.2 18.4 %collective-permute-start.7 = (bf16[64,3584]{1,0:T(8,128)(2,1)}, bf16[64,3584]{1,0:T(8,128)(2,1)}, u32[]{:S(2)}, u32[]{:S(2)}) collective-permute-start(bf16[64,3584]{1,0:T(8,128)(2,1)} %collective-permute-done.5.refs_6_), channel_id=1, source_target_pairs={{0,1},{1,0},{2,3},{3,2},{4,5},{5,4},{6,7},{7,6},{8,9},{9,8},{10,11... | collective-permute-start | bytes 1376264 | tf_op jit(solution)/shard_map/ppermute | solution.py:63
  30.2 14.5 %collective-permute-start.10 = (bf16[64,3584]{1,0:T(8,128)(2,1)}, bf16[64,3584]{1,0:T(8,128)(2,1)}, u32[]{:S(2)}, u32[]{:S(2)}) collective-permute-start(bf16[64,3584]{1,0:T(8,128)(2,1)} %collective-permute-done.6.refs_7_), channel_id=1, source_target_pairs={{0,14},{1,15},{2,0},{3,1},{4,2},{5,3},{6,4},{7,5},{8,6},{9,7},{10,... | collective-permute-start | bytes 1376264 | tf_op jit(solution)/shard_map/ppermute | solution.py:59
  31.2 13.5 %copy-start.10 = (bf16[64,3584]{1,0:T(8,128)(2,1)}, bf16[64,3584]{1,0:T(8,128)(2,1)S(1)}, u32[]{:S(2)}) copy-start(bf16[64,3584]{1,0:T(8,128)(2,1)S(1)} %collective-permute-done.3.refs_4_) | copy-start | bytes 1376260
  31.2 26.7 %collective-permute-start.8 = (bf16[64,3584]{1,0:T(8,128)(2,1)}, bf16[64,3584]{1,0:T(8,128)(2,1)}, u32[]{:S(2)}, u32[]{:S(2)}) collective-permute-start(bf16[64,3584]{1,0:T(8,128)(2,1)} %collective-permute-done.6.refs_7_), channel_id=1, source_target_pairs={{0,1},{1,0},{2,3},{3,2},{4,5},{5,4},{6,7},{7,6},{8,9},{9,8},{10,11... | collective-permute-start | bytes 1376264 | tf_op jit(solution)/shard_map/ppermute | solution.py:63
  38.5 19.4 %collective-permute-start.11 = (bf16[64,3584]{1,0:T(8,128)(2,1)}, bf16[64,3584]{1,0:T(8,128)(2,1)}, u32[]{:S(2)}, u32[]{:S(2)}) collective-permute-start(bf16[64,3584]{1,0:T(8,128)(2,1)} %collective-permute-done.9.refs_10_), channel_id=1, source_target_pairs={{0,1},{1,0},{2,3},{3,2},{4,5},{5,4},{6,7},{7,6},{8,9},{9,8},{10,11... | collective-permute-start | bytes 1376264 | tf_op jit(solution)/shard_map/ppermute | solution.py:63
  44.7 13.2 %collective-permute-start.12 = (bf16[64,3584]{1,0:T(8,128)(2,1)}, bf16[64,3584]{1,0:T(8,128)(2,1)}, u32[]{:S(2)}, u32[]{:S(2)}) collective-permute-start(bf16[64,3584]{1,0:T(8,128)(2,1)} %collective-permute-done.10.refs_11_), channel_id=1, source_target_pairs={{0,1},{1,0},{2,3},{3,2},{4,5},{5,4},{6,7},{7,6},{8,9},{9,8},{10,11... | collective-permute-start | bytes 1376264 | tf_op jit(solution)/shard_map/ppermute | solution.py:63
  48.5 8.1 %collective-permute-start.13 = (bf16[32,3584]{1,0:T(8,128)(2,1)S(1)}, bf16[32,3584]{1,0:T(8,128)(2,1)S(1)}, u32[]{:S(2)}, u32[]{:S(2)}) collective-permute-start(bf16[32,3584]{1,0:T(8,128)(2,1)S(1)} %slice.16), channel_id=1, source_target_pairs={{0,2},{1,3},{2,4},{3,5},{4,6},{5,7},{6,8},{7,9},{8,10},{9,11},{10,... | collective-permute-start | bytes 688136 | tf_op jit(solution)/shard_map/ppermute | solution.py:59
  48.6 9.3 %collective-permute-start.14 = (bf16[32,3584]{1,0:T(8,128)(2,1)S(1)}, bf16[32,3584]{1,0:T(8,128)(2,1)S(1)}, u32[]{:S(2)}, u32[]{:S(2)}) collective-permute-start(bf16[32,3584]{1,0:T(8,128)(2,1)S(1)} %slice.17), channel_id=1, source_target_pairs={{0,14},{1,15},{2,0},{3,1},{4,2},{5,3},{6,4},{7,5},{8,6},{9,7},{10,... | collective-permute-start | bytes 688136 | tf_op jit(solution)/shard_map/ppermute | solution.py:59
  56.6 18.1 %copy-start.2 = (bf16[32,3584]{1,0:T(8,128)(2,1)}, bf16[32,3584]{1,0:T(8,128)(2,1)S(1)}, u32[]{:S(2)}) copy-start(bf16[32,3584]{1,0:T(8,128)(2,1)S(1)} %collective-permute-done.13.f4) | copy-start | bytes 688132
  56.6 18.1 %collective-permute-start.15 = (bf16[32,3584]{1,0:T(8,128)(2,1)S(1)}, bf16[32,3584]{1,0:T(8,128)(2,1)S(1)}, u32[]{:S(2)}, u32[]{:S(2)}) collective-permute-start(bf16[32,3584]{1,0:T(8,128)(2,1)S(1)} %collective-permute-done.13.f4), channel_id=1, source_target_pairs={{0,1},{1,0},{2,3},{3,2},{4,5},{5,4},{6,7},{7,6},{8,9},{9,8},{10,11... | collective-permute-start | bytes 688136 | tf_op jit(solution)/shard_map/ppermute | solution.py:63
  57.9 16.8 %copy-start.3 = (bf16[32,3584]{1,0:T(8,128)(2,1)}, bf16[32,3584]{1,0:T(8,128)(2,1)S(1)}, u32[]{:S(2)}) copy-start(bf16[32,3584]{1,0:T(8,128)(2,1)S(1)} %collective-permute-done.14.b4) | copy-start | bytes 688132
  57.9 16.8 %collective-permute-start.16 = (bf16[32,3584]{1,0:T(8,128)(2,1)S(1)}, bf16[32,3584]{1,0:T(8,128)(2,1)S(1)}, u32[]{:S(2)}, u32[]{:S(2)}) collective-permute-start(bf16[32,3584]{1,0:T(8,128)(2,1)S(1)} %collective-permute-done.14.b4), channel_id=1, source_target_pairs={{0,1},{1,0},{2,3},{3,2},{4,5},{5,4},{6,7},{7,6},{8,9},{9,8},{10,11... | collective-permute-start | bytes 688136 | tf_op jit(solution)/shard_map/ppermute | solution.py:63
  74.7 0.7 copy-start.4
  74.8 0.7 copy-start.5
  78.6 6.3 %collective-permute-start.17 = (f32[32,512]{1,0:T(8,128)}, f32[32,512]{1,0:T(8,128)S(1)}, u32[]{:S(2)}, u32[]{:S(2)}) collective-permute-start(f32[32,512]{1,0:T(8,128)} %get-tuple-element.16), channel_id=1, source_target_pairs={{0,128},{16,144},{32,160},{48,176},{64,192},{80,208},{96,224},{112... | collective-permute-start | bytes 196616 | tf_op jit(solution)/shard_map/ppermute | solution.py:67
  81.6 5.7 %collective-permute-start.18 = (f32[32,512]{1,0:T(8,128)}, f32[32,512]{1,0:T(8,128)S(1)}, u32[]{:S(2)}, u32[]{:S(2)}) collective-permute-start(f32[32,512]{1,0:T(8,128)} %get-tuple-element.16), channel_id=1, source_target_pairs={{0,64},{16,80},{32,96},{48,112},{64,128},{80,144},{96,160},{112,17... | collective-permute-start | bytes 196616 | tf_op jit(solution)/shard_map/ppermute | solution.py:67
  82.2 5.1 %collective-permute-start.19 = (f32[32,512]{1,0:T(8,128)}, f32[32,512]{1,0:T(8,128)S(1)}, u32[]{:S(2)}, u32[]{:S(2)}) collective-permute-start(f32[32,512]{1,0:T(8,128)} %get-tuple-element.16), channel_id=1, source_target_pairs={{0,192},{16,208},{32,224},{48,240},{64,0},{80,16},{96,32},{112,48}... | collective-permute-start | bytes 196616 | tf_op jit(solution)/shard_map/ppermute | solution.py:67
  88.2 8.8 %copy-start.1 = (f32[32,512]{1,0:T(8,128)}, f32[32,512]{1,0:T(8,128)S(1)}, u32[]{:S(2)}) copy-start(f32[32,512]{1,0:T(8,128)S(1)} %add_add_fusion.l0) | copy-start | bytes 196612
  88.2 6.3 %collective-permute-start.20 = (f32[32,512]{1,0:T(8,128)S(1)}, f32[32,512]{1,0:T(8,128)S(1)}, u32[]{:S(2)}, u32[]{:S(2)}) collective-permute-start(f32[32,512]{1,0:T(8,128)S(1)} %add_add_fusion.l0), channel_id=1, source_target_pairs={{0,16},{16,32},{32,48},{48,0},{64,80},{80,96},{96,112},{112,64},{1... | collective-permute-start | bytes 196616 | tf_op jit(solution)/shard_map/ppermute | solution.py:67
  89.9 5.8 %collective-permute-start.21 = (f32[32,512]{1,0:T(8,128)S(1)}, f32[32,512]{1,0:T(8,128)S(1)}, u32[]{:S(2)}, u32[]{:S(2)}) collective-permute-start(f32[32,512]{1,0:T(8,128)S(1)} %add_add_fusion.l0), channel_id=1, source_target_pairs={{0,32},{16,48},{32,0},{48,16},{64,96},{80,112},{96,64},{112,80},{1... | collective-permute-start | bytes 196616 | tf_op jit(solution)/shard_map/ppermute | solution.py:67
  92.8 4.3 %collective-permute-start.22 = (f32[32,512]{1,0:T(8,128)S(1)}, f32[32,512]{1,0:T(8,128)S(1)}, u32[]{:S(2)}, u32[]{:S(2)}) collective-permute-start(f32[32,512]{1,0:T(8,128)S(1)} %add_add_fusion.l0), channel_id=1, source_target_pairs={{0,48},{16,0},{32,16},{48,32},{64,112},{80,64},{96,80},{112,96},{1... | collective-permute-start | bytes 196616 | tf_op jit(solution)/shard_map/ppermute | solution.py:67
  94.5 2.6 %copy-start.6 = (f32[32,512]{1,0:T(8,128)}, f32[32,512]{1,0:T(8,128)S(1)}, u32[]{:S(2)}) copy-start(f32[32,512]{1,0:T(8,128)S(1)} %collective-permute-done.20.l1) | copy-start | bytes 196612
  95.7 1.3 copy-start.7
  97.0 0.6 copy-start.8
  124.8 16.2 %all-to-all-start.1 = ((bf16[16,2,3584]{2,1,0:T(2,128)(2,1)}), bf16[16,2,3584]{2,1,0:T(2,128)(2,1)S(1)}, u32[]{:S(2)}, u32[]{:S(2)}) async-start(bf16[16,2,3584]{2,1,0:T(2,128)(2,1)} %broadcast_in_dim.2), calls=%async_computation.1 | async-start | bytes 458752 | tf_op jit(solution)/shard_map/all_to_all | solution.py:363

commit v2 on v0

v2 whole, which is shorter than its diff:
```python
import functools

import jax
import jax.numpy as jnp
from jax import lax
from jax.experimental import pallas as pl
from jax.experimental.pallas import tpu as pltpu
from jax.sharding import PartitionSpec as P

BF = jnp.bfloat16
F32 = jnp.float32
HI = lax.Precision.HIGHEST
DP = 16
NZ = 8
TOK = 64
CHIP = 2 * TOK
D = 3584
UNITS = 512
ROWS = 1024
EARLY = 5 * CHIP
RANK = 32
BLK = 512
NBLK = D // BLK
MIB = 1024 * 1024


def gelu_pair(value):
    coeff = 0.7978845608028654
    tanh_val = jnp.tanh(coeff * (value + 0.044715 * value * value * value))
    gelu_value = 0.5 * value * (1.0 + tanh_val)
    gelu_slope = 0.5 * (1.0 + tanh_val) + 0.5 * value * (1.0 - tanh_val * tanh_val) * coeff * (
        1.0 + 3.0 * 0.044715 * value * value
    )
    return (gelu_value, gelu_slope)


def split(value, terms):
    parts = []
    for _ in range(terms):
        part = value.astype(BF)
        parts.append(part)
        value = value - part.astype(F32)
    return parts


def split_exactly(value, terms):
    parts = []
    for _ in range(terms):
        part = lax.reduce_precision(value, 8, 7)
        parts.append(part.astype(BF))
        value = value - part
    return parts


def dot(a, b, ca, cb, precision=None):
    return lax.dot_general(
        a, b, (((ca,), (cb,)), ((), ())), preferred_element_type=F32, precision=precision
    )


def fold(stacked, terms):
    total = stacked[0:RANK]
    for k in range(1, terms):
        total = total + stacked[k * RANK : (k + 1) * RANK]
    return total


def chip_of(slot, z):
    return lax.rem(z + jnp.where(slot % 2 == 1, 2 * NZ - (slot + 1) // 2, NZ + slot // 2), NZ)


def rows_of_step(s, core):
    if s == 0:
        return [core * TOK, (1 - core) * TOK]
    if s == 4:
        return [(14 + core) * TOK, (15 - core) * TOK]
    return [
        (4 * s - 2 + 3 * core) * TOK,
        (4 * s - 1 + core) * TOK,
        (4 * s + 1 - 3 * core) * TOK,
        (4 * s - core) * TOK,
    ]


def after(value, *others):
    return lax.optimization_barrier((value,) + others)[0]


def other_core(value):
    return lax.ppermute(value, "tensor", [(i, i ^ 1) for i in range(2 * NZ)])


def along_z(value):
    return lax.ppermute(
        value, "tensor", [(i, (i + 2 - 4 * (i % 2)) % (2 * NZ)) for i in range(2 * NZ)]
    )


def sum_over_ring(value, turn):
    def pairs(k):
        for i in range(DP * 2 * NZ):
            dp, t = divmod(i, 2 * NZ)
            x, y = divmod(dp, 4)
            if (t + turn) % 2 == 0:
                x = (x + k) % 4
            else:
                y = (y + k) % 4
            yield (i, (4 * x + y) * 2 * NZ + t)

    return [value] + [lax.ppermute(value, ("dp", "tensor"), list(pairs(k))) for k in (1, 2, 3)]


def sum_of_four(a, b, c, d):
    return (a + c) + (b + d)


SMEM = pl.BlockSpec(memory_space=pltpu.SMEM)
WHOLE = pl.BlockSpec(memory_space=pltpu.VMEM)


def kept(shape, dtype):
    return pltpu.VMEM(shape, dtype)


def held(value):
    return pltpu.with_memory_space_constraint(value, pltpu.VMEM)


def kept_out(shape, dtype):
    return pltpu.HBM(shape, dtype)


def from_hbm(value):
    return pltpu.with_memory_space_constraint(value, pltpu.HBM)


def params(mib):
    return pltpu.CompilerParams(vmem_limit_bytes=mib * MIB)


def cost(flops, moved):
    return pl.CostEstimate(flops=flops, bytes_accessed=moved, transcendentals=0)


def hidden_kernel(place, pre, hidden_t):
    value, _ = gelu_pair(pre[0].astype(F32))
    hidden = (value * pre[1].astype(F32)).astype(BF).astype(F32)
    hidden_t[...] = jnp.transpose(hidden).astype(BF)


def hidden_call(place, pre):
    return pl.pallas_call(
        hidden_kernel,
        grid_spec=pltpu.PrefetchScalarGridSpec(
            num_scalar_prefetch=1,
            grid=(NZ,),
            in_specs=[pl.BlockSpec((2, CHIP, UNITS), lambda i, p: (0, chip_of(i, p[0]), 0))],
            out_specs=pl.BlockSpec((UNITS, CHIP), lambda i, p: (0, i)),
        ),
        out_shape=kept((UNITS, ROWS), BF),
        compiler_params=params(8),
        cost_estimate=cost(10**7, 3_000_000),
        name="hidden",
    )(place, pre)


def main_kernel(place, *refs):
    pieces = refs[:10]
    hidden_t, error, q3, merged, left, tokens, g_acc, e_acc = refs[10:]
    i = pl.program_id(0)
    rows = [r for s in range(3) for r in rows_of_step(s, place[1])]
    for piece, row in zip(pieces, rows):
        tokens[pl.ds(pl.multiple_of(row, TOK), TOK), :] = piece[...]

    @pl.when(i == 0)
    def _():
        g_acc[...] = jnp.zeros_like(g_acc)
        e_acc[...] = jnp.zeros_like(e_acc)

    block = tokens[...]
    err = error[...]
    merged[...] = (dot(hidden_t[:, :EARLY], block, 1, 0) + err.astype(F32)).astype(BF)
    q = q3[...]
    g_acc[...] += dot(q, block, 1, 1)
    e_acc[...] += dot(q, err, 1, 1)

    @pl.when(i == NBLK - 1)
    def _():
        g = jnp.concatenate(split(fold(g_acc[...], 3), 2), axis=0)
        left[...] = fold(e_acc[...], 3) + fold(dot(g, hidden_t[:, :EARLY], 1, 1), 2)


def main_call(place, pieces, hidden_t, error, q3):
    whole = lambda shape: pl.BlockSpec(shape, lambda i, p: (0, 0))
    cols = lambda rows: pl.BlockSpec((rows, BLK), lambda i, p: (0, i))
    return pl.pallas_call(
        main_kernel,
        grid_spec=pltpu.PrefetchScalarGridSpec(
            num_scalar_prefetch=1,
            grid=(NBLK,),
            in_specs=[cols(TOK)] * 10
            + [whole((UNITS, ROWS)), cols(UNITS), cols(3 * RANK)],
            out_specs=[cols(UNITS), whole((RANK, UNITS))],
            scratch_shapes=[
                pltpu.VMEM((EARLY, BLK), BF),
                pltpu.VMEM((3 * RANK, EARLY), F32),
                pltpu.VMEM((3 * RANK, UNITS), F32),
            ],
        ),
        out_shape=[
            kept((UNITS, D), BF),
            jax.ShapeDtypeStruct((RANK, UNITS), F32),
        ],
        compiler_params=params(14),
        cost_estimate=cost(2 * EARLY * UNITS * D, 14_000_000),
        name="weight_grad",
    )(place, *map(held, pieces), held(hidden_t), error, q3)


def left_kernel(step, place, *refs):
    pieces = refs[:-5]
    hidden_t, q3, left_in, left, last = refs[-5:]
    base = (5 if step == 3 else 7) * CHIP
    for piece, row in zip(pieces, rows_of_step(step, place[1])):
        last[pl.ds(pl.multiple_of(row - base, TOK), TOK), :] = piece[...]
    g = fold(dot(q3[...], last[...], 1, 1), 3)
    g = jnp.concatenate(split(g, 2), axis=0)
    here = hidden_t[:, base : base + last.shape[0]]
    left[...] = left_in[...] + fold(dot(g, here, 1, 1), 2)


def left_call(step, place, pieces, hidden_t, q3, left_in):
    rows = TOK * len(pieces)
    return pl.pallas_call(
        functools.partial(left_kernel, step),
        in_specs=[SMEM] + [WHOLE] * (len(pieces) + 3),
        out_specs=[WHOLE] * 2,
        out_shape=[
            jax.ShapeDtypeStruct((RANK, UNITS), F32),
            kept((rows, D), BF),
        ],
        compiler_params=params(12),
        cost_estimate=cost(2 * rows * D * 96, 4_000_000),
        name="left_of_step",
    )(place, *map(held, pieces), held(hidden_t), held(q3), left_in)


def right_kernel(l0, l1, l2, l3, hidden_t, last_a, last_b, merged, p_out, right):
    left = ((l0[...] + l2[...]) + (l1[...] + l3[...])) * (1.0 / DP)
    rest = dot(left, left, 1, 1, HI)
    rows = lax.broadcasted_iota(jnp.int32, (RANK, RANK), 0)
    inverse = (rows == lax.broadcasted_iota(jnp.int32, (RANK, RANK), 1)).astype(F32)
    for k in range(RANK):
        scale = lax.rsqrt(rest[k : k + 1, k : k + 1])
        column = jnp.where(rows[:, 0:1] > k, rest[:, k : k + 1] * scale, 0.0)
        rest_row = rest[k : k + 1, :] * scale
        inverse_row = inverse[k : k + 1, :] * scale
        rest = rest - column * rest_row
        inverse = jnp.where(rows == k, inverse_row, inverse - column * inverse_row)
    factor = dot(inverse, left, 1, 0, HI)
    p_out[...] = factor
    high, low = split(factor, 2)
    p2 = jnp.concatenate([high, low], axis=0)
    mine = fold(dot(p2, hidden_t[:, EARLY:], 1, 0), 2)
    h2 = jnp.concatenate(split(mine, 2), axis=0)
    for i in range(NBLK):
        c = slice(i * BLK, (i + 1) * BLK)
        total = dot(p2, merged[:, c], 1, 0)
        total += dot(h2[:, : 2 * CHIP], last_a[:, c], 1, 0)
        total += dot(h2[:, 2 * CHIP :], last_b[:, c], 1, 0)
        right[:, c] = fold(total, 2).astype(BF)


def right_call(lefts, hidden_t, last_a, last_b, merged):
    return pl.pallas_call(
        right_kernel,
        in_specs=[WHOLE] * 8,
        out_specs=[WHOLE] * 2,
        out_shape=[
            jax.ShapeDtypeStruct((RANK, UNITS), F32),
            jax.ShapeDtypeStruct((RANK, D), BF),
        ],
        compiler_params=params(14),
        cost_estimate=cost(10**8, 8_000_000),
        name="right_factor",
    )(*lefts, held(hidden_t), held(last_a), held(last_b), held(merged))


def sum_kernel(parts, out):
    total = jnp.sum(parts[...].astype(F32), axis=0, keepdims=True)
    out[...] = jnp.broadcast_to(total.astype(BF), out.shape)


def sum_call(parts):
    return pl.pallas_call(
        sum_kernel,
        in_specs=[WHOLE],
        out_specs=WHOLE,
        out_shape=jax.ShapeDtypeStruct(parts.shape, BF),
        compiler_params=params(8),
        cost_estimate=cost(10**6, 500_000),
        name="sum_of_ranks",
    )(parts)


HALF = D // 2
WIDE = HALF // 2


def merge_kernel(hidden_t, last_a, last_b, merged, total):
    part = merged[...].astype(F32)
    part += dot(hidden_t[:, EARLY : EARLY + 2 * CHIP], last_a[...], 1, 0)
    part += dot(hidden_t[:, EARLY + 2 * CHIP :], last_b[...], 1, 0)
    total[...] = part.astype(BF)


def merge_call(half, hidden_t, last_a, last_b, merged):
    first = half * (HALF // WIDE)
    cols = lambda rows: pl.BlockSpec((rows, WIDE), lambda i: (0, first + i))
    return pl.pallas_call(
        merge_kernel,
        grid=(HALF // WIDE,),
        in_specs=[
            pl.BlockSpec((UNITS, ROWS), lambda i: (0, 0)),
            cols(2 * CHIP),
            cols(CHIP),
            cols(UNITS),
        ],
        out_specs=pl.BlockSpec((UNITS, WIDE), lambda i: (0, i)),
        out_shape=kept_out((UNITS, HALF), BF),
        compiler_params=params(14),
        cost_estimate=cost(3 * CHIP * UNITS * D, 6_000_000),
        name="weight_grad_rest",
    )(*map(from_hbm, (hidden_t, last_a, last_b, merged)))


def error_kernel(factor, lower, upper, q, out, p2_t):
    i = pl.program_id(0)

    @pl.when(i == 0)
    def _():
        p2_t[...] = jnp.concatenate(split(jnp.transpose(factor[...]), 2), axis=1)

    rounded = q[...].astype(BF)
    rounded = jnp.concatenate([rounded, rounded], axis=0)
    estimate = dot(p2_t[...], rounded, 1, 0)

    @pl.when(i < HALF // WIDE)
    def _():
        out[...] = (lower[...].astype(F32) - estimate).astype(BF)

    @pl.when(i >= HALF // WIDE)
    def _():
        out[...] = (upper[...].astype(F32) - estimate).astype(BF)


def error_call(factor, lower, upper, q):
    per = HALF // WIDE
    cols = lambda rows: pl.BlockSpec((rows, WIDE), lambda i: (0, i))
    return pl.pallas_call(
        error_kernel,
        grid=(D // WIDE,),
        in_specs=[
            pl.BlockSpec((RANK, UNITS), lambda i: (0, 0)),
            pl.BlockSpec((UNITS, WIDE), lambda i: (0, jnp.minimum(i, per - 1))),
            pl.BlockSpec((UNITS, WIDE), lambda i: (0, jnp.maximum(i - per, 0))),
            cols(RANK),
        ],
        out_specs=cols(UNITS),
        scratch_shapes=[pltpu.VMEM((UNITS, 2 * RANK), BF)],
        out_shape=jax.ShapeDtypeStruct((UNITS, D), BF),
        compiler_params=params(12),
        cost_estimate=cost(2 * 64 * UNITS * D, 8_000_000),
        name="new_error",
    )(factor, from_hbm(lower), from_hbm(upper), q)


def slots_of_step(s):
    return {0: [0], 4: [7]}.get(s, [2 * s - 1, 2 * s])


def finish_pre(grad, pre, stage):
    value, slope = gelu_pair(pre[0].astype(F32))
    stage[0] = (grad * pre[1].astype(F32) * slope).astype(BF)
    stage[1] = (grad * value).astype(BF)


def pre_kernel(s, place, *refs):
    slots = slots_of_step(s)
    count = 2 * len(slots) if s < 3 else 1
    pieces, refs = refs[:count], refs[count:]
    pres, refs = refs[: len(slots)], refs[len(slots) :]
    weight, (out, tokens, stage, sems) = refs[0], refs[-4:]
    if s < 3:
        for piece, row in zip(pieces, rows_of_step(s, place[1])):
            row = pl.multiple_of(row - slots[0] * CHIP, TOK)
            tokens[pl.ds(row, TOK), :] = piece[...]
        here = tokens[...]
    else:
        here = pieces[0][...]
    grad = dot(here, weight[...], 1, 1)
    copies = []
    for k, slot in enumerate(slots):
        finish_pre(grad[k * CHIP : (k + 1) * CHIP], pres[k], stage.at[k])
        row = pl.multiple_of(chip_of(slot, place[0]) * CHIP, CHIP)
        copies.append(
            pltpu.make_async_copy(stage.at[k], out.at[:, pl.ds(row, CHIP), :], sems.at[k])
        )
        copies[-1].start()
    for copy in copies:
        copy.wait()


def pre_call(s, place, pieces, pre, weight, so_far=None):
    slots = slots_of_step(s)
    chip = lambda slot: pl.BlockSpec((2, CHIP, UNITS), lambda i, p: (0, chip_of(slot, p[0]), 0))
    any_space = pl.BlockSpec(memory_space=pl.ANY)
    specs = [WHOLE] * len(pieces) + [chip(k) for k in slots] + [WHOLE]
    args = [place, *map(held, pieces), *([pre] * len(slots)), held(weight)]
    aliases = {}
    if so_far is not None:
        aliases = {len(args): 0}
        specs.append(any_space)
        args.append(so_far)
    rows = CHIP * len(slots)
    return pl.pallas_call(
        functools.partial(pre_kernel, s),
        grid_spec=pltpu.PrefetchScalarGridSpec(
            num_scalar_prefetch=1,
            grid=(1,),
            in_specs=specs,
            out_specs=any_space,
            scratch_shapes=[
                pltpu.VMEM((rows, D), BF),
                pltpu.VMEM((len(slots), 2, CHIP, UNITS), BF),
                pltpu.SemaphoreType.DMA((len(slots),)),
            ],
        ),
        out_shape=jax.ShapeDtypeStruct((2, ROWS, UNITS), BF),
        input_output_aliases=aliases,
        compiler_params=params(10),
        cost_estimate=cost(2 * rows * UNITS * D, 2 * rows * D + 8 * rows * UNITS),
        name="grad_pre",
    )(*args)


def on_device(grad_out, pre_act, down_weight, error, q_start):
    index = lax.axis_index("tensor").astype(jnp.int32)
    place = jnp.stack([index >> 1, index & 1])
    hidden_t = hidden_call(place, pre_act)
    q3 = jnp.concatenate(split_exactly(q_start, 3), axis=0)


    def pre_of(step, pieces, so_far=None):
        return pre_call(step, place, pieces, pre_act, down_weight, so_far)

    a0, b0 = grad_out, other_core(grad_out)
    a1, b1 = along_z(a0), along_z(after(b0, hidden_t))
    a2 = along_z(a1)
    grad_pre = pre_of(0, [a0, after(b0, a1)])
    b2 = along_z(after(b1, a1, grad_pre))
    xa1, xb1 = other_core(after(a1, b1, grad_pre)), other_core(after(b1, a1, grad_pre))
    grad_pre = pre_of(1, [a1, b1, xa1, xb1], grad_pre)
    a3 = along_z(after(a2, b1, grad_pre))
    b3 = along_z(after(b2, a2, grad_pre))
    xa2, xb2 = other_core(after(a2, b2, grad_pre)), other_core(after(b2, a2, grad_pre))
    grad_pre = pre_of(2, [a2, b2, xa2, xb2], grad_pre)
    a4 = along_z(after(a3, b2, grad_pre))
    early = [a0, b0, a1, b1, xa1, xb1, a2, b2, xa2, after(xb2, a3)]
    merged, left = main_call(place, early, hidden_t, error, q3)
    xa3, xb3 = other_core(after(a3, b3, left)), other_core(after(b3, a3, left))
    left, last_a = left_call(3, place, [a3, b3, xa3, xb3], hidden_t, q3, left)
    xa4 = other_core(after(a4, b3))
    left, last_b = left_call(4, place, [a4, xa4], hidden_t, q3, left)

    grad_pre = pre_of(3, [after(last_a, left)], grad_pre)
    lefts = sum_over_ring(left, 0)
    left = sum_of_four(lefts[0], lefts[1], lefts[2], after(lefts[3], grad_pre))
    grad_pre = pre_of(4, [after(last_b, left)], grad_pre)
    lefts = sum_over_ring(left, 1)
    lefts[3] = after(lefts[3], grad_pre)
    p_factor, right = right_call(lefts, hidden_t, last_a, last_b, merged)

    parts = lax.all_to_all(right.reshape(DP, RANK // DP, D), "dp", 0, 0, tiled=True)
    lower = merge_call(0, after(hidden_t, right), last_a, last_b, merged)
    summed = sum_call(after(parts, lower))
    right = lax.all_to_all(summed, "dp", 0, 0, tiled=True).reshape(RANK, D)
    upper = merge_call(1, after(hidden_t, summed), last_a, last_b, merged)
    q_factor = right.astype(F32) * (1.0 / DP)
    new_error = error_call(p_factor, lower, upper, q_factor)
    return (grad_pre, new_error, p_factor, q_factor)


def solution(mesh):
    placed = (
        P(("dp", "tensor"), None),
        P(None, "dp", "tensor"),
        P("tensor", None),
        P(("dp", "tensor"), None),
        P("tensor", None),
    )
    return jax.shard_map(
        on_device,
        mesh=mesh,
        in_specs=placed,
        out_specs=(
            P(None, "dp", "tensor"),
            P(("dp", "tensor"), None),
            P(None, "tensor"),
            P("tensor", None),
        ),
        check_vma=False,
    )
```

time: 300 us -> 115 us (0.38)
  waiting for transfers between devices: 228 us -> 26.8 us
  Pallas kernels: 0 us -> 47.5 us
  matrix products: 45.2 us -> 0 us
  starting transfers between devices: 0.3 us -> 34.1 us
  between operations: 13.9 us -> 0.91 us
  other arithmetic: 9.17 us -> 0.43 us
    psum x2 -> x0, waiting for transfers between devices: 173 us -> none  [the longest x1 90.2 us: on_device(): left_mean = lax.psum(left_local, 'dp') / dp_count]
    all_gather x1 -> x0, waiting for transfers between devices: 54.2 us -> none  [on_device(): collected_factors = lax.all_gather(grad_out, 'tensor', axis=0, tiled=True)]
    pallas_call x0 -> x14, Pallas kernels: none -> 47.5 us  [the longest x5 13.6 us: pre_call(): pl.pallas_call(functools.partial(pre_kernel, s), grid_spec=pltpu.Prefetch...]
    dot_general x6 -> x0, matrix products: 44.1 us -> none  [the longest x1 9.64 us: on_device(): lax.dot_general(orthonormal_left, right_average, (((0,), (0,)), ((), ()))...]
    ppermute x0 -> x21, starting transfers between devices: none -> 25.4 us  [the longest x7 13.8 us: along_z(): lax.ppermute(value, 'tensor', [(i, (i + 2 - 4 * (i % 2)) % (2 * NZ)) for...]
    ppermute x0 -> x21, waiting for transfers between devices: none -> 18.8 us  [the longest x7 11.8 us: along_z(): lax.ppermute(value, 'tensor', [(i, (i + 2 - 4 * (i % 2)) % (2 * NZ)) for...]
    all_to_all x0 -> x2, starting transfers between devices: none -> 8.66 us  [the longest x1 4.97 us: on_device(): lax.all_to_all(right.reshape(DP, RANK // DP, D), 'dp', 0, 0, tiled=True)]
    another operation x6 -> x1, other arithmetic: 8.19 us -> 0.07 us  [on_device(): place = jnp.stack([index >> 1, index & 1])]
  transfers between devices with their start and end apart: 3 -> 23, of which waited for: 3 -> 14; matrix products, arithmetic and copies ran while one was open for 4% -> 0% of each run, Pallas kernels for 0% -> 31%
where the time goes in v2:
time: 115 us
  Pallas kernels  47.5 us (41%)
  starting transfers between devices  34.1 us (30%)
  waiting for transfers between devices  26.8 us (23%)
  local copies, waits for them, and re-layouts  4.84 us (4%)
    ppermute x7, starting transfers between devices, along_z(): lax.ppermute(value, 'tensor', [(i, (i + 2 - 4 * (i % 2)) % (2 * NZ)) for...  13.8 us
    pallas_call x5, Pallas kernels, pre_call(): pl.pallas_call(functools.partial(pre_kernel, s), grid_spec=pltpu.Prefetch...  13.6 us
    ppermute x7, waiting for transfers between devices, along_z(): lax.ppermute(value, 'tensor', [(i, (i + 2 - 4 * (i % 2)) % (2 * NZ)) for...  11.8 us
    ppermute x6, starting transfers between devices, sum_over_ring(): lax.ppermute(value, ('dp', 'tensor'), list(pairs(k)))  9.81 us
    pallas_call x1, Pallas kernels, main_call(): pl.pallas_call(main_kernel, grid_spec=pltpu.PrefetchScalarGridSpec(num_sc...  8.81 us
    pallas_call x2, Pallas kernels, merge_call(): pl.pallas_call(merge_kernel, grid=(HALF // WIDE,), in_specs=[pl.BlockSpec...  8.56 us
    pallas_call x1, Pallas kernels, error_call(): pl.pallas_call(error_kernel, grid=(D // WIDE,), in_specs=[pl.BlockSpec((R...  5.93 us
    all_to_all x1, starting transfers between devices, on_device(): lax.all_to_all(right.reshape(DP, RANK // DP, D), 'dp', 0, 0, tiled=True)  4.97 us
  transfers between devices with their start and end apart: 23, of which 14 were waited for; matrix products, arithmetic and copies ran while one was open for 0% of the time, Pallas kernels for 31%

profile of v2, /device:TPU:96, one launch (start us, length us, event | category | flops | bytes accessed | tf_op | source)
XLA Modules:
  0.0 114.6 jit_solution(15159378275349797075)
XLA Ops:
  0.7 3.2 %collective-permute-start = (bf16[64,3584]{1,0:T(8,128)(2,1)}, bf16[64,3584]{1,0:T(8,128)(2,1)S(1)}, u32[]{:S(2)}, u32[]{:S(2)}) collective-permute-start(bf16[64,3584]{1,0:T(8,128)(2,1)} %refs_0_.3), channel_id=1, source_target_pairs={{0,2},{1,15},{2,4},{3,1},{4,6},{5,3},{6,8},{7,5},{8,10},{9,7},{10,... | collective-permute-start | bytes 1376264 | tf_op jit(solution)/shard_map/ppermute | solution.py:94
  4.0 1.6 %copy-done = bf16[2,1024,512]{2,1,0:T(8,128)(2,1)S(1)} copy-done((bf16[2,1024,512]{2,1,0:T(8,128)(2,1)S(1)}, bf16[2,1024,512]{2,1,0:T(8,128)(2,1)}, u32[]{:S(2)}) %copy-start) | copy-done | bytes 2097176
  5.6 2.7 %hidden.1.refs_10_.refs_4_.refs_2_.hidden_t = bf16[512,1024]{1,0:T(8,128)(2,1)S(1)} custom-call(s32[2]{0:T(128)S(1)} %pad_add_fusion.place, bf16[2,1024,512]{2,1,0:T(8,128)(2,1)S(1)} %copy-done), custom_call_target="tpu_custom_call" | custom-call | flops 10000000 | bytes 3000000 | tf_op jit(solution)/shard_map/hidden/pallas_call | solution.py:152
  8.3 1.1 collective-permute-start.3
  9.4 0.8 collective-permute-done.refs_0_.refs_2_
  10.3 2.0 %copy-done.2 = bf16[512,3584]{1,0:T(8,128)(2,1)S(1)} copy-done((bf16[512,3584]{1,0:T(8,128)(2,1)S(1)}, bf16[512,3584]{1,0:T(8,128)(2,1)}, u32[]{:S(2)}) %copy-start.2) | copy-done | bytes 3670040
  12.3 2.7 %grad_pre.5.refs_7_ = bf16[2,1024,512]{2,1,0:T(8,128)(2,1)} custom-call(s32[2]{0:T(128)S(1)} %pad_add_fusion.place, bf16[64,3584]{1,0:T(8,128)(2,1)S(1)} %copy-done.9, bf16[64,3584]{1,0:T(8,128)(2,1)S(1)} %collective-permute-done.2.refs_1_, bf16[2,1024,512]{2,1,0:T(8,128)(2,1)S(1)} %copy-done.1, bf16[512,3584]{1,0:T(8,128)(2,1)S(1)} %copy-done.2), custom_call_target="tpu_custom_call" | custom-call | flops 469762048 | bytes 1441792 | tf_op jit(solution)/shard_map/grad_pre/pallas_call | solution.py:426
  15.0 1.9 %collective-permute-done.3.refs_1_.refs_3_ = bf16[64,3584]{1,0:T(8,128)(2,1)S(1)} collective-permute-done((bf16[64,3584]{1,0:T(8,128)(2,1)S(1)}, bf16[64,3584]{1,0:T(8,128)(2,1)S(1)}, u32[]{:S(2)}, u32[]{:S(2)}) %collective-permute-start.3) | collective-permute-done | bytes 458784 | tf_op jit(solution)/shard_map/ppermute | solution.py:94
  16.9 0.5 collective-permute-start.5
  17.4 2.2 %collective-permute-start.1 = (bf16[64,3584]{1,0:T(8,128)(2,1)S(1)}, bf16[64,3584]{1,0:T(8,128)(2,1)S(1)}, u32[]{:S(2)}, u32[]{:S(2)}) collective-permute-start(bf16[64,3584]{1,0:T(8,128)(2,1)S(1)} %collective-permute-done.refs_0_.refs_2_), channel_id=1, source_target_pairs={{0,2},{1,15},{2,4},{3,1},{4,6},{5,3},{6,8},{7,5},{8,10},{9,7},{10,... | collective-permute-start | bytes 1376264 | tf_op jit(solution)/shard_map/ppermute | solution.py:94
  19.7 2.8 %grad_pre.6.refs_7_ = bf16[2,1024,512]{2,1,0:T(8,128)(2,1)} custom-call(s32[2]{0:T(128)S(1)} %pad_add_fusion.place, bf16[64,3584]{1,0:T(8,128)(2,1)S(1)} %collective-permute-done.refs_0_.refs_2_, bf16[64,3584]{1,0:T(8,128)(2,1)S(1)} %collective-permute-done.3.refs_1_.refs_3_, ...), custom_call_target="tpu_custom_call", output_to_operand_aliasing={{}: (8, {})} | custom-call | flops 939524096 | bytes 2883584 | tf_op jit(solution)/shard_map/grad_pre/pallas_call | solution.py:426
  22.4 3.4 %collective-permute-done.1.refs_0_.refs_6_ = bf16[64,3584]{1,0:T(8,128)(2,1)S(1)} collective-permute-done((bf16[64,3584]{1,0:T(8,128)(2,1)S(1)}, bf16[64,3584]{1,0:T(8,128)(2,1)S(1)}, u32[]{:S(2)}, u32[]{:S(2)}) %collective-permute-start.1) | collective-permute-done | bytes 458784 | tf_op jit(solution)/shard_map/ppermute | solution.py:94
  25.9 4.9 %collective-permute-done.7.refs_1_.refs_7_ = bf16[64,3584]{1,0:T(8,128)(2,1)S(1)} collective-permute-done((bf16[64,3584]{1,0:T(8,128)(2,1)S(1)}, bf16[64,3584]{1,0:T(8,128)(2,1)S(1)}, u32[]{:S(2)}, u32[]{:S(2)}) %collective-permute-start.7) | collective-permute-done | bytes 458784 | tf_op jit(solution)/shard_map/ppermute | solution.py:94
  30.8 3.4 %collective-permute-start.6 = (bf16[64,3584]{1,0:T(8,128)(2,1)S(1)}, bf16[64,3584]{1,0:T(8,128)(2,1)S(1)}, u32[]{:S(2)}, u32[]{:S(2)}) collective-permute-start(bf16[64,3584]{1,0:T(8,128)(2,1)S(1)} %collective-permute-done.1.refs_0_.refs_6_), channel_id=1, source_target_pairs={{0,2},{1,15},{2,4},{3,1},{4,6},{5,3},{6,8},{7,5},{8,10},{9,7},{10,... | collective-permute-start | bytes 1376264 | tf_op jit(solution)/shard_map/ppermute | solution.py:94
  34.2 0.5 collective-permute-start.9
  34.9 1.1 collective-permute-done.8.refs_2_.refs_8_
  36.0 0.7 collective-permute-done.9.refs_3_.refs_9_
  36.7 2.8 %grad_pre.7.refs_4_ = bf16[2,1024,512]{2,1,0:T(8,128)(2,1)} custom-call(s32[2]{0:T(128)S(1)} %pad_add_fusion.place, bf16[64,3584]{1,0:T(8,128)(2,1)S(1)} %collective-permute-done.1.refs_0_.refs_6_, bf16[64,3584]{1,0:T(8,128)(2,1)S(1)} %collective-permute-done.7.refs_1_.refs_7_, ...), custom_call_target="tpu_custom_call", output_to_operand_aliasing={{}: (8, {})} | custom-call | flops 939524096 | bytes 2883584 | tf_op jit(solution)/shard_map/grad_pre/pallas_call | solution.py:426
  39.5 0.7 collective-permute-done.6.refs_0_
  40.2 3.7 %collective-permute-start.10 = (bf16[64,3584]{1,0:T(8,128)(2,1)S(1)}, bf16[64,3584]{1,0:T(8,128)(2,1)S(1)}, u32[]{:S(2)}, u32[]{:S(2)}) collective-permute-start(bf16[64,3584]{1,0:T(8,128)(2,1)S(1)} %collective-permute-done.6.refs_0_), channel_id=1, source_target_pairs={{0,2},{1,15},{2,4},{3,1},{4,6},{5,3},{6,8},{7,5},{8,10},{9,7},{10,... | collective-permute-start | bytes 1376264 | tf_op jit(solution)/shard_map/ppermute | solution.py:94
  44.0 8.8 %weight_grad.1 = (bf16[512,3584]{1,0:T(8,128)(2,1)S(1)}, f32[32,512]{1,0:T(8,128)S(1)}) custom-call(s32[2]{0:T(128)S(1)} %pad_add_fusion.place, bf16[64,3584]{1,0:T(8,128)(2,1)S(1)} %copy-done.9, bf16[64,3584]{1,0:T(8,128)(2,1)S(1)} %collective-permute-done.2.refs_1_, bf16[64,3584]{1,0:T(8,128)(2,1)S(1)} %collective-permute-done.refs_0_.refs_2_, ...), custom_call_target="tpu_custom_call" | custom-call | flops 2348810240 | bytes 14000000 | tf_op jit(solution)/shard_map/weight_grad/pallas_call | solution.py:196
  52.9 0.5 collective-permute-start.14
  53.5 1.2 %collective-permute-done.13.refs_2_ = bf16[64,3584]{1,0:T(8,128)(2,1)S(1)} collective-permute-done((bf16[64,3584]{1,0:T(8,128)(2,1)S(1)}, bf16[64,3584]{1,0:T(8,128)(2,1)S(1)}, u32[]{:S(2)}, u32[]{:S(2)}) %collective-permute-start.13) | collective-permute-done | bytes 458784 | tf_op jit(solution)/shard_map/ppermute | solution.py:90
  54.7 0.7 collective-permute-done.14.refs_3_
  55.4 1.6 %left_of_step.2 = (f32[32,512]{1,0:T(8,128)S(1)}, bf16[256,3584]{1,0:T(8,128)(2,1)S(1)}) custom-call(s32[2]{0:T(128)S(1)} %pad_add_fusion.place, bf16[64,3584]{1,0:T(8,128)(2,1)S(1)} %collective-permute-done.6.refs_0_, bf16[64,3584]{1,0:T(8,128)(2,1)S(1)} %collective-permute-done.11.refs_1_, bf16[64,3584]{1,0:T(8,128)(2,1)S(1)} %collective-permute-done.13.refs_2_, ...), custom_call_target="tpu_custom_call" | custom-call | flops 176160768 | bytes 4000000 | tf_op jit(solution)/shard_map/left_of_step/pallas_call | solution.py:234
  57.0 1.2 %left_of_step.3 = (f32[32,512]{1,0:T(8,128)S(1)}, bf16[128,3584]{1,0:T(8,128)(2,1)S(1)}) custom-call(s32[2]{0:T(128)S(1)} %pad_add_fusion.place, bf16[64,3584]{1,0:T(8,128)(2,1)S(1)} %collective-permute-done.10.refs_0_, bf16[64,3584]{1,0:T(8,128)(2,1)S(1)} %collective-permute-done.12.refs_1_, bf16[512,1024]{1,0:T(8,128)(2,1)S(1)} %hidden.1.refs_10_.refs_4_.refs_2_.hidden_t, ...), custom_call_target="tpu_custom_call" | custom-call | flops 88080384 | bytes 4000000 | tf_op jit(solution)/shard_map/left_of_step/pallas_call | solution.py:234
  58.2 2.8 %collective-permute-start.17 = (f32[32,512]{1,0:T(8,128)S(1)}, f32[32,512]{1,0:T(8,128)S(1)}, u32[]{:S(2)}, u32[]{:S(2)}) collective-permute-start(f32[32,512]{1,0:T(8,128)S(1)} %get-tuple-element.46), channel_id=1, source_target_pairs={{0,192},{1,49},{2,194},{3,51},{4,196},{5,53},{6,198},{7,55},{8,200... | collective-permute-start | bytes 196616 | tf_op jit(solution)/shard_map/ppermute | solution.py:110
  61.1 2.3 %collective-permute-start.15 = (f32[32,512]{1,0:T(8,128)S(1)}, f32[32,512]{1,0:T(8,128)S(1)}, u32[]{:S(2)}, u32[]{:S(2)}) collective-permute-start(f32[32,512]{1,0:T(8,128)S(1)} %get-tuple-element.46), channel_id=1, source_target_pairs={{0,128},{1,33},{2,130},{3,35},{4,132},{5,37},{6,134},{7,39},{8,136... | collective-permute-start | bytes 196616 | tf_op jit(solution)/shard_map/ppermute | solution.py:110
  63.4 2.7 %grad_pre.8.refs_3_ = bf16[2,1024,512]{2,1,0:T(8,128)(2,1)} custom-call(s32[2]{0:T(128)S(1)} %pad_add_fusion.place, bf16[256,3584]{1,0:T(8,128)(2,1)S(1)} %get-tuple-element.48.refs_0_.last_a, bf16[2,1024,512]{2,1,0:T(8,128)(2,1)S(1)} %copy-done.1, bf16[2,1024,512]{2,1,0:T(8,128)(2,1)S(1)} %copy-done.1, ...), custom_call_target="tpu_custom_call", output_to_operand_aliasing={{}: (5, {})} | custom-call | flops 939524096 | bytes 2883584 | tf_op jit(solution)/shard_map/grad_pre/pallas_call | solution.py:426
  66.1 1.2 %collective-permute-done.16 = f32[32,512]{1,0:T(8,128)S(1)} collective-permute-done((f32[32,512]{1,0:T(8,128)S(1)}, f32[32,512]{1,0:T(8,128)S(1)}, u32[]{:S(2)}, u32[]{:S(2)}) %collective-permute-start.16) | collective-permute-done | bytes 65568 | tf_op jit(solution)/shard_map/ppermute | solution.py:110
  67.3 3.1 %collective-permute-start.20 = (f32[32,512]{1,0:T(8,128)S(1)}, f32[32,512]{1,0:T(8,128)S(1)}, u32[]{:S(2)}, u32[]{:S(2)}) collective-permute-start(f32[32,512]{1,0:T(8,128)S(1)} %add_add_fusion.l0), channel_id=1, source_target_pairs={{0,48},{1,193},{2,50},{3,195},{4,52},{5,197},{6,54},{7,199},{8,56}... | collective-permute-start | bytes 196616 | tf_op jit(solution)/shard_map/ppermute | solution.py:110
  70.4 0.6 collective-permute-start.19
  71.0 1.0 collective-permute-start.18
  72.0 2.7 %grad_pre.9 = bf16[2,1024,512]{2,1,0:T(8,128)(2,1)} custom-call(s32[2]{0:T(128)S(1)} %pad_add_fusion.place, bf16[128,3584]{1,0:T(8,128)(2,1)S(1)} %get-tuple-element.50.refs_0_.last_b, bf16[2,1024,512]{2,1,0:T(8,128)(2,1)S(1)} %copy-done.1, bf16[512,3584]{1,0:T(8,128)(2,1)S(1)} %copy-done.3, ...), custom_call_target="tpu_custom_call", output_to_operand_aliasing={{}: (4, {})} | custom-call | flops 469762048 | bytes 1441792 | tf_op jit(solution)/shard_map/grad_pre/pallas_call | solution.py:426
  74.6 1.5 %collective-permute-done.19.l2 = f32[32,512]{1,0:T(8,128)S(1)} collective-permute-done((f32[32,512]{1,0:T(8,128)S(1)}, f32[32,512]{1,0:T(8,128)S(1)}, u32[]{:S(2)}, u32[]{:S(2)}) %collective-permute-start.19) | collective-permute-done | bytes 65568 | tf_op jit(solution)/shard_map/ppermute | solution.py:110
  76.2 0.7 collective-permute-done.18.l1
  76.9 4.3 %right_factor.1 = (f32[32,512]{1,0:T(8,128)}, bf16[32,3584]{1,0:T(8,128)(2,1)S(1)}) custom-call(f32[32,512]{1,0:T(8,128)S(1)} %add_add_fusion.l0, f32[32,512]{1,0:T(8,128)S(1)} %collective-permute-done.18.l1, f32[32,512]{1,0:T(8,128)S(1)} %collective-permute-done.19.l2, f32[32,512]{1,0:T(8,128)S(1)} %collective-permute-done.20.l3, ...), custom_call_target="tpu_custom_call" | custom-call | flops 100000000 | bytes 8000000 | tf_op jit(solution)/shard_map/right_factor/pallas_call | solution.py:275
  81.2 0.8 reshape.15
  82.0 5.0 %all-to-all-start = ((bf16[16,2,3584]{2,1,0:T(2,128)(2,1)}), bf16[16,2,3584]{2,1,0:T(2,128)(2,1)S(1)}, u32[]{:S(2)}, u32[]{:S(2)}) async-start(bf16[16,2,3584]{2,1,0:T(2,128)(2,1)} %reshape.15), calls=%async_computation | async-start | bytes 458752 | tf_op jit(solution)/shard_map/all_to_all | solution.py:484
  86.9 4.2 %weight_grad_rest.2.lower = bf16[512,1792]{1,0:T(8,128)(2,1)} custom-call(bf16[512,1024]{1,0:T(8,128)(2,1)} %copy-done.4, bf16[256,3584]{1,0:T(8,128)(2,1)} %copy-done.6, bf16[128,3584]{1,0:T(8,128)(2,1)} %copy-done.7, bf16[512,3584]{1,0:T(8,128)(2,1)} %copy-done.5), custom_call_target="tpu_custom_call" | custom-call | flops 704643072 | bytes 6000000 | tf_op jit(solution)/shard_map/weight_grad_rest/pallas_call | solution.py:320
  91.2 4.0 %all-to-all-done.parts = bf16[16,2,3584]{2,1,0:T(2,128)(2,1)S(1)} async-done(((bf16[16,2,3584]{2,1,0:T(2,128)(2,1)}), bf16[16,2,3584]{2,1,0:T(2,128)(2,1)S(1)}, u32[]{:S(2)}, u32[]{:S(2)}) %all-to-all-start) | async-done | bytes 229408 | tf_op jit(solution)/shard_map/all_to_all | solution.py:484
  95.2 0.9 sum_of_ranks.1
  96.1 3.7 %all-to-all-start.1 = ((bf16[16,2,3584]{2,1,0:T(2,128)(2,1)}), bf16[16,2,3584]{2,1,0:T(2,128)(2,1)S(1)}, u32[]{:S(2)}, u32[]{:S(2)}) async-start(bf16[16,2,3584]{2,1,0:T(2,128)(2,1)} %sum_of_ranks.1), calls=%async_computation.1 | async-start | bytes 458752 | tf_op jit(solution)/shard_map/all_to_all | solution.py:487
  99.8 4.3 %weight_grad_rest.3.upper = bf16[512,1792]{1,0:T(8,128)(2,1)} custom-call(bf16[512,1024]{1,0:T(8,128)(2,1)} %copy-done.4, bf16[256,3584]{1,0:T(8,128)(2,1)} %copy-done.6, bf16[128,3584]{1,0:T(8,128)(2,1)} %copy-done.7, bf16[512,3584]{1,0:T(8,128)(2,1)} %copy-done.5), custom_call_target="tpu_custom_call" | custom-call | flops 704643072 | bytes 6000000 | tf_op jit(solution)/shard_map/weight_grad_rest/pallas_call | solution.py:320
  104.2 3.9 %all-to-all-done.1 = bf16[16,2,3584]{2,1,0:T(2,128)(2,1)S(1)} async-done(((bf16[16,2,3584]{2,1,0:T(2,128)(2,1)}), bf16[16,2,3584]{2,1,0:T(2,128)(2,1)S(1)}, u32[]{:S(2)}, u32[]{:S(2)}) %all-to-all-start.1) | async-done | bytes 229408 | tf_op jit(solution)/shard_map/all_to_all | solution.py:487
  108.1 0.2 convert_multiply_fusion
  108.3 0.3 mul.10.q
  108.6 5.9 %new_error.1 = bf16[512,3584]{1,0:T(8,128)(2,1)} custom-call(f32[32,512]{1,0:T(8,128)S(1)} %copy-done.11, bf16[512,1792]{1,0:T(8,128)(2,1)} %weight_grad_rest.2.lower, bf16[512,1792]{1,0:T(8,128)(2,1)} %weight_grad_rest.3.upper, f32[32,3584]{1,0:T(8,128)S(1)} %mul.10.q), custom_call_target="tpu_custom_call" | custom-call | flops 234881024 | bytes 8000000 | tf_op jit(solution)/shard_map/new_error/pallas_call | solution.py:360
  (45 shorter events, 0.8 us)
Async XLA Ops:
  0.6 7.7 %collective-permute-start.2 = (bf16[64,3584]{1,0:T(8,128)(2,1)}, bf16[64,3584]{1,0:T(8,128)(2,1)S(1)}, u32[]{:S(2)}, u32[]{:S(2)}) collective-permute-start(bf16[64,3584]{1,0:T(8,128)(2,1)} %refs_0_.3), channel_id=1, source_target_pairs={{0,1},{1,0},{2,3},{3,2},{4,5},{5,4},{6,7},{7,6},{8,9},{9,8},{10,11... | collective-permute-start | bytes 1376264 | tf_op jit(solution)/shard_map/ppermute | solution.py:90
  0.7 9.5 %collective-permute-start = (bf16[64,3584]{1,0:T(8,128)(2,1)}, bf16[64,3584]{1,0:T(8,128)(2,1)S(1)}, u32[]{:S(2)}, u32[]{:S(2)}) collective-permute-start(bf16[64,3584]{1,0:T(8,128)(2,1)} %refs_0_.3), channel_id=1, source_target_pairs={{0,2},{1,15},{2,4},{3,1},{4,6},{5,3},{6,8},{7,5},{8,10},{9,7},{10,... | collective-permute-start | bytes 1376264 | tf_op jit(solution)/shard_map/ppermute | solution.py:94
  4.0 1.6 %copy-start = (bf16[2,1024,512]{2,1,0:T(8,128)(2,1)S(1)}, bf16[2,1024,512]{2,1,0:T(8,128)(2,1)}, u32[]{:S(2)}) copy-start(bf16[2,1024,512]{2,1,0:T(8,128)(2,1)} %refs_1_.3) | copy-start | bytes 6291460
  5.6 4.6 %copy-start.1 = (bf16[2,1024,512]{2,1,0:T(8,128)(2,1)S(1)}, bf16[2,1024,512]{2,1,0:T(8,128)(2,1)}, u32[]{:S(2)}) copy-start(bf16[2,1024,512]{2,1,0:T(8,128)(2,1)} %refs_1_.3) | copy-start | bytes 6291460
  5.6 4.6 %copy-start.9 = (bf16[64,3584]{1,0:T(8,128)(2,1)S(1)}, bf16[64,3584]{1,0:T(8,128)(2,1)}, u32[]{:S(2)}) copy-start(bf16[64,3584]{1,0:T(8,128)(2,1)} %refs_0_.3) | copy-start | bytes 1376260
  8.3 68.5 %copy-start.4 = (bf16[512,1024]{1,0:T(8,128)(2,1)}, bf16[512,1024]{1,0:T(8,128)(2,1)S(1)}, u32[]{:S(2)}) copy-start(bf16[512,1024]{1,0:T(8,128)(2,1)S(1)} %hidden.1.refs_10_.refs_4_.refs_2_.hidden_t) | copy-start | bytes 3145732
  8.3 8.6 %collective-permute-start.3 = (bf16[64,3584]{1,0:T(8,128)(2,1)S(1)}, bf16[64,3584]{1,0:T(8,128)(2,1)S(1)}, u32[]{:S(2)}, u32[]{:S(2)}) collective-permute-start(bf16[64,3584]{1,0:T(8,128)(2,1)S(1)} %collective-permute-done.2.refs_1_), channel_id=1, source_target_pairs={{0,2},{1,15},{2,4},{3,1},{4,6},{5,3},{6,8},{7,5},{8,10},{9,7},{10,... | collective-permute-start | bytes 1376264 | tf_op jit(solution)/shard_map/ppermute | solution.py:94
  10.3 2.0 %copy-start.2 = (bf16[512,3584]{1,0:T(8,128)(2,1)S(1)}, bf16[512,3584]{1,0:T(8,128)(2,1)}, u32[]{:S(2)}) copy-start(bf16[512,3584]{1,0:T(8,128)(2,1)} %refs_2_.5) | copy-start | bytes 11010052
  12.3 7.4 %copy-start.3 = (bf16[512,3584]{1,0:T(8,128)(2,1)S(1)}, bf16[512,3584]{1,0:T(8,128)(2,1)}, u32[]{:S(2)}) copy-start(bf16[512,3584]{1,0:T(8,128)(2,1)} %refs_2_.5) | copy-start | bytes 11010052
  15.0 19.8 %copy-start.12 = (f32[32,3584]{1,0:T(8,128)S(1)}, f32[32,3584]{1,0:T(8,128)}, u32[]{:S(2)}) copy-start(f32[32,3584]{1,0:T(8,128)} %param.9) | copy-start | bytes 1376260
  16.9 2.8 %collective-permute-start.4 = (bf16[64,3584]{1,0:T(8,128)(2,1)S(1)}, bf16[64,3584]{1,0:T(8,128)(2,1)S(1)}, u32[]{:S(2)}, u32[]{:S(2)}) collective-permute-start(bf16[64,3584]{1,0:T(8,128)(2,1)S(1)} %collective-permute-done.refs_0_.refs_2_), channel_id=1, source_target_pairs={{0,1},{1,0},{2,3},{3,2},{4,5},{5,4},{6,7},{7,6},{8,9},{9,8},{10,11... | collective-permute-start | bytes 1376264 | tf_op jit(solution)/shard_map/ppermute | solution.py:90
  16.9 2.8 %collective-permute-start.5 = (bf16[64,3584]{1,0:T(8,128)(2,1)S(1)}, bf16[64,3584]{1,0:T(8,128)(2,1)S(1)}, u32[]{:S(2)}, u32[]{:S(2)}) collective-permute-start(bf16[64,3584]{1,0:T(8,128)(2,1)S(1)} %collective-permute-done.3.refs_1_.refs_3_), channel_id=1, source_target_pairs={{0,1},{1,0},{2,3},{3,2},{4,5},{5,4},{6,7},{7,6},{8,9},{9,8},{10,11... | collective-permute-start | bytes 1376264 | tf_op jit(solution)/shard_map/ppermute | solution.py:90
  17.4 8.5 %collective-permute-start.1 = (bf16[64,3584]{1,0:T(8,128)(2,1)S(1)}, bf16[64,3584]{1,0:T(8,128)(2,1)S(1)}, u32[]{:S(2)}, u32[]{:S(2)}) collective-permute-start(bf16[64,3584]{1,0:T(8,128)(2,1)S(1)} %collective-permute-done.refs_0_.refs_2_), channel_id=1, source_target_pairs={{0,2},{1,15},{2,4},{3,1},{4,6},{5,3},{6,8},{7,5},{8,10},{9,7},{10,... | collective-permute-start | bytes 1376264 | tf_op jit(solution)/shard_map/ppermute | solution.py:94
  19.6 11.2 %collective-permute-start.7 = (bf16[64,3584]{1,0:T(8,128)(2,1)S(1)}, bf16[64,3584]{1,0:T(8,128)(2,1)S(1)}, u32[]{:S(2)}, u32[]{:S(2)}) collective-permute-start(bf16[64,3584]{1,0:T(8,128)(2,1)S(1)} %collective-permute-done.3.refs_1_.refs_3_), channel_id=1, source_target_pairs={{0,2},{1,15},{2,4},{3,1},{4,6},{5,3},{6,8},{7,5},{8,10},{9,7},{10,... | collective-permute-start | bytes 1376264 | tf_op jit(solution)/shard_map/ppermute | solution.py:94
  30.8 9.4 %collective-permute-start.6 = (bf16[64,3584]{1,0:T(8,128)(2,1)S(1)}, bf16[64,3584]{1,0:T(8,128)(2,1)S(1)}, u32[]{:S(2)}, u32[]{:S(2)}) collective-permute-start(bf16[64,3584]{1,0:T(8,128)(2,1)S(1)} %collective-permute-done.1.refs_0_.refs_6_), channel_id=1, source_target_pairs={{0,2},{1,15},{2,4},{3,1},{4,6},{5,3},{6,8},{7,5},{8,10},{9,7},{10,... | collective-permute-start | bytes 1376264 | tf_op jit(solution)/shard_map/ppermute | solution.py:94
  34.2 1.8 %collective-permute-start.8 = (bf16[64,3584]{1,0:T(8,128)(2,1)S(1)}, bf16[64,3584]{1,0:T(8,128)(2,1)S(1)}, u32[]{:S(2)}, u32[]{:S(2)}) collective-permute-start(bf16[64,3584]{1,0:T(8,128)(2,1)S(1)} %collective-permute-done.1.refs_0_.refs_6_), channel_id=1, source_target_pairs={{0,1},{1,0},{2,3},{3,2},{4,5},{5,4},{6,7},{7,6},{8,9},{9,8},{10,11... | collective-permute-start | bytes 1376264 | tf_op jit(solution)/shard_map/ppermute | solution.py:90
  34.2 2.5 %collective-permute-start.9 = (bf16[64,3584]{1,0:T(8,128)(2,1)S(1)}, bf16[64,3584]{1,0:T(8,128)(2,1)S(1)}, u32[]{:S(2)}, u32[]{:S(2)}) collective-permute-start(bf16[64,3584]{1,0:T(8,128)(2,1)S(1)} %collective-permute-done.7.refs_1_.refs_7_), channel_id=1, source_target_pairs={{0,1},{1,0},{2,3},{3,2},{4,5},{5,4},{6,7},{7,6},{8,9},{9,8},{10,11... | collective-permute-start | bytes 1376264 | tf_op jit(solution)/shard_map/ppermute | solution.py:90
  34.8 18.0 %collective-permute-start.11 = (bf16[64,3584]{1,0:T(8,128)(2,1)S(1)}, bf16[64,3584]{1,0:T(8,128)(2,1)S(1)}, u32[]{:S(2)}, u32[]{:S(2)}) collective-permute-start(bf16[64,3584]{1,0:T(8,128)(2,1)S(1)} %collective-permute-done.7.refs_1_.refs_7_), channel_id=1, source_target_pairs={{0,2},{1,15},{2,4},{3,1},{4,6},{5,3},{6,8},{7,5},{8,10},{9,7},{10,... | collective-permute-start | bytes 1376264 | tf_op jit(solution)/shard_map/ppermute | solution.py:94
  36.7 7.3 %copy-start.8 = (bf16[512,3584]{1,0:T(8,128)(2,1)S(1)}, bf16[512,3584]{1,0:T(8,128)(2,1)}, u32[]{:S(2)}) copy-start(bf16[512,3584]{1,0:T(8,128)(2,1)} %refs_11_.1) | copy-start | bytes 11010052
  40.2 13.2 %collective-permute-start.10 = (bf16[64,3584]{1,0:T(8,128)(2,1)S(1)}, bf16[64,3584]{1,0:T(8,128)(2,1)S(1)}, u32[]{:S(2)}, u32[]{:S(2)}) collective-permute-start(bf16[64,3584]{1,0:T(8,128)(2,1)S(1)} %collective-permute-done.6.refs_0_), channel_id=1, source_target_pairs={{0,2},{1,15},{2,4},{3,1},{4,6},{5,3},{6,8},{7,5},{8,10},{9,7},{10,... | collective-permute-start | bytes 1376264 | tf_op jit(solution)/shard_map/ppermute | solution.py:94
  52.8 24.1 %copy-start.5 = (bf16[512,3584]{1,0:T(8,128)(2,1)}, bf16[512,3584]{1,0:T(8,128)(2,1)S(1)}, u32[]{:S(2)}) copy-start(bf16[512,3584]{1,0:T(8,128)(2,1)S(1)} %get-tuple-element.52.merged) | copy-start | bytes 11010052
  52.8 1.9 %collective-permute-start.13 = (bf16[64,3584]{1,0:T(8,128)(2,1)S(1)}, bf16[64,3584]{1,0:T(8,128)(2,1)S(1)}, u32[]{:S(2)}, u32[]{:S(2)}) collective-permute-start(bf16[64,3584]{1,0:T(8,128)(2,1)S(1)} %collective-permute-done.6.refs_0_), channel_id=1, source_target_pairs={{0,1},{1,0},{2,3},{3,2},{4,5},{5,4},{6,7},{7,6},{8,9},{9,8},{10,11... | collective-permute-start | bytes 1376264 | tf_op jit(solution)/shard_map/ppermute | solution.py:90
  52.9 2.5 %collective-permute-start.14 = (bf16[64,3584]{1,0:T(8,128)(2,1)S(1)}, bf16[64,3584]{1,0:T(8,128)(2,1)S(1)}, u32[]{:S(2)}, u32[]{:S(2)}) collective-permute-start(bf16[64,3584]{1,0:T(8,128)(2,1)S(1)} %collective-permute-done.11.refs_1_), channel_id=1, source_target_pairs={{0,1},{1,0},{2,3},{3,2},{4,5},{5,4},{6,7},{7,6},{8,9},{9,8},{10,11... | collective-permute-start | bytes 1376264 | tf_op jit(solution)/shard_map/ppermute | solution.py:90
  53.4 3.6 %collective-permute-start.12 = (bf16[64,3584]{1,0:T(8,128)(2,1)S(1)}, bf16[64,3584]{1,0:T(8,128)(2,1)S(1)}, u32[]{:S(2)}, u32[]{:S(2)}) collective-permute-start(bf16[64,3584]{1,0:T(8,128)(2,1)S(1)} %collective-permute-done.10.refs_0_), channel_id=1, source_target_pairs={{0,1},{1,0},{2,3},{3,2},{4,5},{5,4},{6,7},{7,6},{8,9},{9,8},{10,11... | collective-permute-start | bytes 1376264 | tf_op jit(solution)/shard_map/ppermute | solution.py:90
  57.0 19.9 %copy-start.6 = (bf16[256,3584]{1,0:T(8,128)(2,1)}, bf16[256,3584]{1,0:T(8,128)(2,1)S(1)}, u32[]{:S(2)}) copy-start(bf16[256,3584]{1,0:T(8,128)(2,1)S(1)} %get-tuple-element.48.refs_0_.last_a) | copy-start | bytes 5505028
  58.2 18.6 %copy-start.7 = (bf16[128,3584]{1,0:T(8,128)(2,1)}, bf16[128,3584]{1,0:T(8,128)(2,1)S(1)}, u32[]{:S(2)}) copy-start(bf16[128,3584]{1,0:T(8,128)(2,1)S(1)} %get-tuple-element.50.refs_0_.last_b) | copy-start | bytes 2752516
  58.2 7.8 %collective-permute-start.17 = (f32[32,512]{1,0:T(8,128)S(1)}, f32[32,512]{1,0:T(8,128)S(1)}, u32[]{:S(2)}, u32[]{:S(2)}) collective-permute-start(f32[32,512]{1,0:T(8,128)S(1)} %get-tuple-element.46), channel_id=1, source_target_pairs={{0,192},{1,49},{2,194},{3,51},{4,196},{5,53},{6,198},{7,55},{8,200... | collective-permute-start | bytes 196616 | tf_op jit(solution)/shard_map/ppermute | solution.py:110
  61.1 6.2 %collective-permute-start.16 = (f32[32,512]{1,0:T(8,128)S(1)}, f32[32,512]{1,0:T(8,128)S(1)}, u32[]{:S(2)}, u32[]{:S(2)}) collective-permute-start(f32[32,512]{1,0:T(8,128)S(1)} %get-tuple-element.46), channel_id=1, source_target_pairs={{0,64},{1,17},{2,66},{3,19},{4,68},{5,21},{6,70},{7,23},{8,72},{9,... | collective-permute-start | bytes 196616 | tf_op jit(solution)/shard_map/ppermute | solution.py:110
  61.1 6.2 %collective-permute-start.15 = (f32[32,512]{1,0:T(8,128)S(1)}, f32[32,512]{1,0:T(8,128)S(1)}, u32[]{:S(2)}, u32[]{:S(2)}) collective-permute-start(f32[32,512]{1,0:T(8,128)S(1)} %get-tuple-element.46), channel_id=1, source_target_pairs={{0,128},{1,33},{2,130},{3,35},{4,132},{5,37},{6,134},{7,39},{8,136... | collective-permute-start | bytes 196616 | tf_op jit(solution)/shard_map/ppermute | solution.py:110
  67.3 7.4 %collective-permute-start.20 = (f32[32,512]{1,0:T(8,128)S(1)}, f32[32,512]{1,0:T(8,128)S(1)}, u32[]{:S(2)}, u32[]{:S(2)}) collective-permute-start(f32[32,512]{1,0:T(8,128)S(1)} %add_add_fusion.l0), channel_id=1, source_target_pairs={{0,48},{1,193},{2,50},{3,195},{4,52},{5,197},{6,54},{7,199},{8,56}... | collective-permute-start | bytes 196616 | tf_op jit(solution)/shard_map/ppermute | solution.py:110
  70.4 5.8 %collective-permute-start.19 = (f32[32,512]{1,0:T(8,128)S(1)}, f32[32,512]{1,0:T(8,128)S(1)}, u32[]{:S(2)}, u32[]{:S(2)}) collective-permute-start(f32[32,512]{1,0:T(8,128)S(1)} %add_add_fusion.l0), channel_id=1, source_target_pairs={{0,32},{1,129},{2,34},{3,131},{4,36},{5,133},{6,38},{7,135},{8,40}... | collective-permute-start | bytes 196616 | tf_op jit(solution)/shard_map/ppermute | solution.py:110
  71.0 5.8 %collective-permute-start.18 = (f32[32,512]{1,0:T(8,128)S(1)}, f32[32,512]{1,0:T(8,128)S(1)}, u32[]{:S(2)}, u32[]{:S(2)}) collective-permute-start(f32[32,512]{1,0:T(8,128)S(1)} %add_add_fusion.l0), channel_id=1, source_target_pairs={{0,16},{1,65},{2,18},{3,67},{4,20},{5,69},{6,22},{7,71},{8,24},{9,... | collective-permute-start | bytes 196616 | tf_op jit(solution)/shard_map/ppermute | solution.py:110
  82.0 13.2 %all-to-all-start = ((bf16[16,2,3584]{2,1,0:T(2,128)(2,1)}), bf16[16,2,3584]{2,1,0:T(2,128)(2,1)S(1)}, u32[]{:S(2)}, u32[]{:S(2)}) async-start(bf16[16,2,3584]{2,1,0:T(2,128)(2,1)} %reshape.15), calls=%async_computation | async-start | bytes 458752 | tf_op jit(solution)/shard_map/all_to_all | solution.py:484
  96.1 12.0 %all-to-all-start.1 = ((bf16[16,2,3584]{2,1,0:T(2,128)(2,1)}), bf16[16,2,3584]{2,1,0:T(2,128)(2,1)S(1)}, u32[]{:S(2)}, u32[]{:S(2)}) async-start(bf16[16,2,3584]{2,1,0:T(2,128)(2,1)} %sum_of_ranks.1), calls=%async_computation.1 | async-start | bytes 458752 | tf_op jit(solution)/shard_map/all_to_all | solution.py:487
  99.8 8.8 %copy-start.11 = (f32[32,512]{1,0:T(8,128)S(1)}, f32[32,512]{1,0:T(8,128)}, u32[]{:S(2)}) copy-start(f32[32,512]{1,0:T(8,128)} %get-tuple-element.29.factor) | copy-start | bytes 196612
  108.6 6.0 %copy-start.10 = (f32[32,3584]{1,0:T(8,128)}, f32[32,3584]{1,0:T(8,128)S(1)}, u32[]{:S(2)}) copy-start(f32[32,3584]{1,0:T(8,128)S(1)} %mul.10.q) | copy-start | bytes 1376260

commit v3 on v2

--- a/solution.py
+++ b/solution.py
@@ -142,6 +142,9 @@
     return pl.CostEstimate(flops=flops, bytes_accessed=moved, transcendentals=0)
 
 
+SHORT = cost(10**6, 10**5)
+
+
 def hidden_kernel(place, pre, hidden_t):
     value, _ = gelu_pair(pre[0].astype(F32))
     hidden = (value * pre[1].astype(F32)).astype(BF).astype(F32)
@@ -159,7 +162,7 @@
         ),
         out_shape=kept((UNITS, ROWS), BF),
         compiler_params=params(8),
-        cost_estimate=cost(10**7, 3_000_000),
+        cost_estimate=SHORT,
         name="hidden",
     )(place, pre)
 
@@ -212,7 +215,7 @@
             jax.ShapeDtypeStruct((RANK, UNITS), F32),
         ],
         compiler_params=params(14),
-        cost_estimate=cost(2 * EARLY * UNITS * D, 14_000_000),
+        cost_estimate=SHORT,
         name="weight_grad",
     )(place, *map(held, pieces), held(hidden_t), error, q3)
 
@@ -240,7 +243,7 @@
             kept((rows, D), BF),
         ],
         compiler_params=params(12),
-        cost_estimate=cost(2 * rows * D * 96, 4_000_000),
+        cost_estimate=SHORT,
         name="left_of_step",
     )(place, *map(held, pieces), held(hidden_t), held(q3), left_in)
 
@@ -268,7 +271,7 @@
         total = dot(p2, merged[:, c], 1, 0)
         total += dot(h2[:, : 2 * CHIP], last_a[:, c], 1, 0)
         total += dot(h2[:, 2 * CHIP :], last_b[:, c], 1, 0)
-        right[:, c] = fold(total, 2).astype(BF)
+        right[:, :, c] = fold(total, 2).astype(BF).reshape(DP, RANK // DP, BLK)
 
 
 def right_call(lefts, hidden_t, last_a, last_b, merged):
@@ -278,7 +281,7 @@
         out_specs=[WHOLE] * 2,
         out_shape=[
             jax.ShapeDtypeStruct((RANK, UNITS), F32),
-            jax.ShapeDtypeStruct((RANK, D), BF),
+            jax.ShapeDtypeStruct((DP, RANK // DP, D), BF),
         ],
         compiler_params=params(14),
         cost_estimate=cost(10**8, 8_000_000),
@@ -327,52 +330,56 @@
             cols(UNITS),
         ],
         out_specs=pl.BlockSpec((UNITS, WIDE), lambda i: (0, i)),
-        out_shape=kept_out((UNITS, HALF), BF),
+        out_shape=kept((UNITS, HALF), BF),
         compiler_params=params(14),
         cost_estimate=cost(3 * CHIP * UNITS * D, 6_000_000),
         name="weight_grad_rest",
     )(*map(from_hbm, (hidden_t, last_a, last_b, merged)))
 
 
-def error_kernel(factor, lower, upper, q, out, p2_t):
+def error_kernel(factor, lower, upper, summed, out, q, p2_t):
     i = pl.program_id(0)
 
     @pl.when(i == 0)
     def _():
         p2_t[...] = jnp.concatenate(split(jnp.transpose(factor[...]), 2), axis=1)
 
-    rounded = q[...].astype(BF)
+    mean = summed[...].astype(F32).reshape(RANK, WIDE) * (1.0 / DP)
+    q[...] = mean
+    rounded = mean.astype(BF)
     rounded = jnp.concatenate([rounded, rounded], axis=0)
     estimate = dot(p2_t[...], rounded, 1, 0)
 
-    @pl.when(i < HALF // WIDE)
-    def _():
-        out[...] = (lower[...].astype(F32) - estimate).astype(BF)
-
-    @pl.when(i >= HALF // WIDE)
-    def _():
-        out[...] = (upper[...].astype(F32) - estimate).astype(BF)
-
-
-def error_call(factor, lower, upper, q):
     per = HALF // WIDE
+    for k in range(2 * per):
+
+        @pl.when(i == k)
+        def _():
+            part = (lower, upper)[k // per][:, k % per * WIDE : (k % per + 1) * WIDE]
+            out[...] = (part.astype(F32) - estimate).astype(BF)
+
+
+def error_call(factor, lower, upper, summed):
     cols = lambda rows: pl.BlockSpec((rows, WIDE), lambda i: (0, i))
     return pl.pallas_call(
         error_kernel,
         grid=(D // WIDE,),
         in_specs=[
             pl.BlockSpec((RANK, UNITS), lambda i: (0, 0)),
-            pl.BlockSpec((UNITS, WIDE), lambda i: (0, jnp.minimum(i, per - 1))),
-            pl.BlockSpec((UNITS, WIDE), lambda i: (0, jnp.maximum(i - per, 0))),
-            cols(RANK),
+            WHOLE,
+            WHOLE,
+            pl.BlockSpec((DP, RANK // DP, WIDE), lambda i: (0, 0, i)),
         ],
-        out_specs=cols(UNITS),
+        out_specs=[cols(UNITS), cols(RANK)],
         scratch_shapes=[pltpu.VMEM((UNITS, 2 * RANK), BF)],
-        out_shape=jax.ShapeDtypeStruct((UNITS, D), BF),
-        compiler_params=params(12),
+        out_shape=[
+            jax.ShapeDtypeStruct((UNITS, D), BF),
+            jax.ShapeDtypeStruct((RANK, D), F32),
+        ],
+        compiler_params=params(8),
         cost_estimate=cost(2 * 64 * UNITS * D, 8_000_000),
         name="new_error",
-    )(factor, from_hbm(lower), from_hbm(upper), q)
+    )(factor, held(lower), held(upper), summed)
 
 
 def slots_of_step(s):
@@ -439,7 +446,7 @@
         out_shape=jax.ShapeDtypeStruct((2, ROWS, UNITS), BF),
         input_output_aliases=aliases,
         compiler_params=params(10),
-        cost_estimate=cost(2 * rows * UNITS * D, 2 * rows * D + 8 * rows * UNITS),
+        cost_estimate=SHORT,
         name="grad_pre",
     )(*args)
 
@@ -450,27 +457,28 @@
     hidden_t = hidden_call(place, pre_act)
     q3 = jnp.concatenate(split_exactly(q_start, 3), axis=0)
 
-
     def pre_of(step, pieces, so_far=None):
         return pre_call(step, place, pieces, pre_act, down_weight, so_far)
 
     a0, b0 = grad_out, other_core(grad_out)
     a1, b1 = along_z(a0), along_z(after(b0, hidden_t))
-    a2 = along_z(a1)
-    grad_pre = pre_of(0, [a0, after(b0, a1)])
-    b2 = along_z(after(b1, a1, grad_pre))
-    xa1, xb1 = other_core(after(a1, b1, grad_pre)), other_core(after(b1, a1, grad_pre))
+    grad_pre = pre_of(0, [a0, b0])
+    a2 = along_z(after(a1, grad_pre))
+    b2 = along_z(after(b1, a1))
+    xa1, xb1 = other_core(after(a1, b1)), other_core(after(b1, a1))
+    a3 = along_z(after(a2, b1))
+    xb1 = after(xb1, a2)
     grad_pre = pre_of(1, [a1, b1, xa1, xb1], grad_pre)
-    a3 = along_z(after(a2, b1, grad_pre))
     b3 = along_z(after(b2, a2, grad_pre))
     xa2, xb2 = other_core(after(a2, b2, grad_pre)), other_core(after(b2, a2, grad_pre))
+    a4 = along_z(after(a3, b2))
     grad_pre = pre_of(2, [a2, b2, xa2, xb2], grad_pre)
-    a4 = along_z(after(a3, b2, grad_pre))
-    early = [a0, b0, a1, b1, xa1, xb1, a2, b2, xa2, after(xb2, a3)]
+    xa2, xb2, _ = lax.optimization_barrier((xa2, xb2, a3))
+    early = [a0, b0, a1, b1, xa1, xb1, a2, b2, xa2, xb2]
     merged, left = main_call(place, early, hidden_t, error, q3)
     xa3, xb3 = other_core(after(a3, b3, left)), other_core(after(b3, a3, left))
+    xa4 = other_core(after(a4, b3, left))
     left, last_a = left_call(3, place, [a3, b3, xa3, xb3], hidden_t, q3, left)
-    xa4 = other_core(after(a4, b3))
     left, last_b = left_call(4, place, [a4, xa4], hidden_t, q3, left)
 
     grad_pre = pre_of(3, [after(last_a, left)], grad_pre)
@@ -481,13 +489,12 @@
     lefts[3] = after(lefts[3], grad_pre)
     p_factor, right = right_call(lefts, hidden_t, last_a, last_b, merged)
 
-    parts = lax.all_to_all(right.reshape(DP, RANK // DP, D), "dp", 0, 0, tiled=True)
+    parts = lax.all_to_all(right, "dp", 0, 0, tiled=True)
     lower = merge_call(0, after(hidden_t, right), last_a, last_b, merged)
     summed = sum_call(after(parts, lower))
-    right = lax.all_to_all(summed, "dp", 0, 0, tiled=True).reshape(RANK, D)
+    right = lax.all_to_all(summed, "dp", 0, 0, tiled=True)
     upper = merge_call(1, after(hidden_t, summed), last_a, last_b, merged)
-    q_factor = right.astype(F32) * (1.0 / DP)
-    new_error = error_call(p_factor, lower, upper, q_factor)
+    new_error, q_factor = error_call(p_factor, lower, upper, right)
     return (grad_pre, new_error, p_factor, q_factor)
 
 

time: 115 us -> 107 us (0.930)
  waiting for transfers between devices: 26.8 us -> 22 us
  Pallas kernels: 47.5 us -> 44.4 us
  local copies, waits for them, and re-layouts: 4.84 us -> 6.45 us
  starting transfers between devices: 34.1 us -> 32.5 us
    ppermute x7, waiting for transfers between devices: 11.8 us -> 7.92 us  [along_z(): lax.ppermute(value, 'tensor', [(i, (i + 2 - 4 * (i % 2)) % (2 * NZ)) for...]
    unnamed x26 -> x28, local copies, waits for them, and re-layouts: 3.73 us -> 6.45 us
    pallas_call x1, Pallas kernels: 5.93 us -> 3.84 us  [error_call(): pl.pallas_call(error_kernel, grid=(D // WIDE,), in_specs=[pl.BlockSpec((R...]
    pallas_call x2, Pallas kernels: 8.56 us -> 6.88 us  [merge_call(): pl.pallas_call(merge_kernel, grid=(HALF // WIDE,), in_specs=[pl.BlockSpec...]
    ppermute x6, waiting for transfers between devices: 3.39 us -> 2.22 us  [sum_over_ring(): lax.ppermute(value, ('dp', 'tensor'), list(pairs(k)))]
  transfers between devices with their start and end apart: 23 -> 23, of which waited for: 14 -> 10; matrix products, arithmetic and copies ran while one was open for 0% -> 0% of each run, Pallas kernels for 31% -> 31%
where the time goes in v3:
time: 107 us
  Pallas kernels  44.4 us (41%)
  starting transfers between devices  32.5 us (30%)
  waiting for transfers between devices  22 us (21%)
  local copies, waits for them, and re-layouts  6.45 us (6%)
    ppermute x7, starting transfers between devices, along_z(): lax.ppermute(value, 'tensor', [(i, (i + 2 - 4 * (i % 2)) % (2 * NZ)) for...  14 us
    pallas_call x5, Pallas kernels, pre_call(): pl.pallas_call(functools.partial(pre_kernel, s), grid_spec=pltpu.Prefetch...  13.5 us
    ppermute x6, starting transfers between devices, sum_over_ring(): lax.ppermute(value, ('dp', 'tensor'), list(pairs(k)))  9.82 us
    pallas_call x1, Pallas kernels, main_call(): pl.pallas_call(main_kernel, grid_spec=pltpu.PrefetchScalarGridSpec(num_sc...  8.8 us
    ppermute x7, waiting for transfers between devices, along_z(): lax.ppermute(value, 'tensor', [(i, (i + 2 - 4 * (i % 2)) % (2 * NZ)) for...  7.92 us
    pallas_call x2, Pallas kernels, merge_call(): pl.pallas_call(merge_kernel, grid=(HALF // WIDE,), in_specs=[pl.BlockSpec...  6.88 us
    unnamed x28, local copies, waits for them, and re-layouts  6.45 us
    pallas_call x1, Pallas kernels, right_call(): pl.pallas_call(right_kernel, in_specs=[WHOLE] * 8, out_specs=[WHOLE] * 2,...  5.01 us
  transfers between devices with their start and end apart: 23, of which 10 were waited for; matrix products, arithmetic and copies ran while one was open for 0% of the time, Pallas kernels for 31%

profile of v3, /device:TPU:96, one launch (start us, length us, event | category | flops | bytes accessed | tf_op | source)
XLA Modules:
  0.0 106.5 jit_solution(3821705422849575508)
XLA Ops:
  0.6 0.1 collective-permute-start.1
  0.7 3.2 %collective-permute-start = (bf16[64,3584]{1,0:T(8,128)(2,1)}, bf16[64,3584]{1,0:T(8,128)(2,1)S(1)}, u32[]{:S(2)}, u32[]{:S(2)}) collective-permute-start(bf16[64,3584]{1,0:T(8,128)(2,1)} %refs_0_.3), channel_id=1, source_target_pairs={{0,2},{1,15},{2,4},{3,1},{4,6},{5,3},{6,8},{7,5},{8,10},{9,7},{10,... | collective-permute-start | bytes 1376264 | tf_op jit(solution)/shard_map/ppermute | solution.py:94
  4.0 1.6 %copy-done = bf16[2,1024,512]{2,1,0:T(8,128)(2,1)S(1)} copy-done((bf16[2,1024,512]{2,1,0:T(8,128)(2,1)S(1)}, bf16[2,1024,512]{2,1,0:T(8,128)(2,1)}, u32[]{:S(2)}) %copy-start) | copy-done | bytes 2097176
  5.6 2.7 %hidden.1.refs_10_.refs_4_.refs_2_.hidden_t = bf16[512,1024]{1,0:T(8,128)(2,1)S(1)} custom-call(s32[2]{0:T(128)S(1)} %pad_add_fusion.place, bf16[2,1024,512]{2,1,0:T(8,128)(2,1)S(1)} %copy-done), custom_call_target="tpu_custom_call" | custom-call | flops 1000000 | bytes 100000 | tf_op jit(solution)/shard_map/hidden/pallas_call | solution.py:155
  8.3 1.1 %collective-permute-start.3 = (bf16[64,3584]{1,0:T(8,128)(2,1)S(1)}, bf16[64,3584]{1,0:T(8,128)(2,1)S(1)}, u32[]{:S(2)}, u32[]{:S(2)}) collective-permute-start(bf16[64,3584]{1,0:T(8,128)(2,1)S(1)} %collective-permute-done.1.refs_1_), channel_id=1, source_target_pairs={{0,2},{1,15},{2,4},{3,1},{4,6},{5,3},{6,8},{7,5},{8,10},{9,7},{10,... | collective-permute-start | bytes 1376264 | tf_op jit(solution)/shard_map/ppermute | solution.py:94
  9.4 2.0 %copy-done.2 = bf16[512,3584]{1,0:T(8,128)(2,1)S(1)} copy-done((bf16[512,3584]{1,0:T(8,128)(2,1)S(1)}, bf16[512,3584]{1,0:T(8,128)(2,1)}, u32[]{:S(2)}) %copy-start.2) | copy-done | bytes 3670040
  11.5 2.7 %grad_pre.5.refs_7_ = bf16[2,1024,512]{2,1,0:T(8,128)(2,1)} custom-call(s32[2]{0:T(128)S(1)} %pad_add_fusion.place, bf16[64,3584]{1,0:T(8,128)(2,1)S(1)} %copy-done.11, bf16[64,3584]{1,0:T(8,128)(2,1)S(1)} %collective-permute-done.1.refs_1_, bf16[2,1024,512]{2,1,0:T(8,128)(2,1)S(1)} %copy-done.1, bf16[512,3584]{1,0:T(8,128)(2,1)S(1)} %copy-done.2), custom_call_target="tpu_custom_call" | custom-call | flops 1000000 | bytes 100000 | tf_op jit(solution)/shard_map/grad_pre/pallas_call | solution.py:433
  14.1 1.1 %collective-permute-start.2 = (bf16[64,3584]{1,0:T(8,128)(2,1)S(1)}, bf16[64,3584]{1,0:T(8,128)(2,1)S(1)}, u32[]{:S(2)}, u32[]{:S(2)}) collective-permute-start(bf16[64,3584]{1,0:T(8,128)(2,1)S(1)} %collective-permute-done.refs_0_.refs_2_), channel_id=1, source_target_pairs={{0,2},{1,15},{2,4},{3,1},{4,6},{5,3},{6,8},{7,5},{8,10},{9,7},{10,... | collective-permute-start | bytes 1376264 | tf_op jit(solution)/shard_map/ppermute | solution.py:94
  15.2 1.6 %collective-permute-done.3.refs_1_.refs_3_ = bf16[64,3584]{1,0:T(8,128)(2,1)S(1)} collective-permute-done((bf16[64,3584]{1,0:T(8,128)(2,1)S(1)}, bf16[64,3584]{1,0:T(8,128)(2,1)S(1)}, u32[]{:S(2)}, u32[]{:S(2)}) %collective-permute-start.3) | collective-permute-done | bytes 458784 | tf_op jit(solution)/shard_map/ppermute | solution.py:94
  16.9 2.2 %collective-permute-start.5 = (bf16[64,3584]{1,0:T(8,128)(2,1)S(1)}, bf16[64,3584]{1,0:T(8,128)(2,1)S(1)}, u32[]{:S(2)}, u32[]{:S(2)}) collective-permute-start(bf16[64,3584]{1,0:T(8,128)(2,1)S(1)} %collective-permute-done.3.refs_1_.refs_3_), channel_id=1, source_target_pairs={{0,2},{1,15},{2,4},{3,1},{4,6},{5,3},{6,8},{7,5},{8,10},{9,7},{10,... | collective-permute-start | bytes 1376264 | tf_op jit(solution)/shard_map/ppermute | solution.py:94
  19.1 3.6 %collective-permute-done.2.refs_6_.refs_0_ = bf16[64,3584]{1,0:T(8,128)(2,1)S(1)} collective-permute-done((bf16[64,3584]{1,0:T(8,128)(2,1)S(1)}, bf16[64,3584]{1,0:T(8,128)(2,1)S(1)}, u32[]{:S(2)}, u32[]{:S(2)}) %collective-permute-start.2) | collective-permute-done | bytes 458784 | tf_op jit(solution)/shard_map/ppermute | solution.py:94
  22.7 2.2 %collective-permute-start.4 = (bf16[64,3584]{1,0:T(8,128)(2,1)S(1)}, bf16[64,3584]{1,0:T(8,128)(2,1)S(1)}, u32[]{:S(2)}, u32[]{:S(2)}) collective-permute-start(bf16[64,3584]{1,0:T(8,128)(2,1)S(1)} %collective-permute-done.2.refs_6_.refs_0_), channel_id=1, source_target_pairs={{0,2},{1,15},{2,4},{3,1},{4,6},{5,3},{6,8},{7,5},{8,10},{9,7},{10,... | collective-permute-start | bytes 1376264 | tf_op jit(solution)/shard_map/ppermute | solution.py:94
  24.9 0.1 reduce-precision_convert_fusion.1
  25.1 2.8 %grad_pre.6.refs_7_ = bf16[2,1024,512]{2,1,0:T(8,128)(2,1)} custom-call(s32[2]{0:T(128)S(1)} %pad_add_fusion.place, bf16[64,3584]{1,0:T(8,128)(2,1)S(1)} %collective-permute-done.refs_0_.refs_2_, bf16[64,3584]{1,0:T(8,128)(2,1)S(1)} %collective-permute-done.3.refs_1_.refs_3_, ...), custom_call_target="tpu_custom_call", output_to_operand_aliasing={{}: (8, {})} | custom-call | flops 1000000 | bytes 100000 | tf_op jit(solution)/shard_map/grad_pre/pallas_call | solution.py:433
  27.9 0.1 collective-permute-start.11
  28.0 1.9 %collective-permute-start.9 = (bf16[64,3584]{1,0:T(8,128)(2,1)S(1)}, bf16[64,3584]{1,0:T(8,128)(2,1)S(1)}, u32[]{:S(2)}, u32[]{:S(2)}) collective-permute-start(bf16[64,3584]{1,0:T(8,128)(2,1)S(1)} %collective-permute-done.5.refs_7_.refs_1_), channel_id=1, source_target_pairs={{0,2},{1,15},{2,4},{3,1},{4,6},{5,3},{6,8},{7,5},{8,10},{9,7},{10,... | collective-permute-start | bytes 1376264 | tf_op jit(solution)/shard_map/ppermute | solution.py:94
  29.8 2.7 %collective-permute-done.4.refs_0_ = bf16[64,3584]{1,0:T(8,128)(2,1)S(1)} collective-permute-done((bf16[64,3584]{1,0:T(8,128)(2,1)S(1)}, bf16[64,3584]{1,0:T(8,128)(2,1)S(1)}, u32[]{:S(2)}, u32[]{:S(2)}) %collective-permute-start.4) | collective-permute-done | bytes 458784 | tf_op jit(solution)/shard_map/ppermute | solution.py:94
  32.5 2.2 %collective-permute-start.6 = (bf16[64,3584]{1,0:T(8,128)(2,1)S(1)}, bf16[64,3584]{1,0:T(8,128)(2,1)S(1)}, u32[]{:S(2)}, u32[]{:S(2)}) collective-permute-start(bf16[64,3584]{1,0:T(8,128)(2,1)S(1)} %collective-permute-done.4.refs_0_), channel_id=1, source_target_pairs={{0,2},{1,15},{2,4},{3,1},{4,6},{5,3},{6,8},{7,5},{8,10},{9,7},{10,... | collective-permute-start | bytes 1376264 | tf_op jit(solution)/shard_map/ppermute | solution.py:94
  34.8 1.7 %collective-permute-done.10.refs_8_.refs_2_ = bf16[64,3584]{1,0:T(8,128)(2,1)S(1)} collective-permute-done((bf16[64,3584]{1,0:T(8,128)(2,1)S(1)}, bf16[64,3584]{1,0:T(8,128)(2,1)S(1)}, u32[]{:S(2)}, u32[]{:S(2)}) %collective-permute-start.10) | collective-permute-done | bytes 458784 | tf_op jit(solution)/shard_map/ppermute | solution.py:90
  36.6 8.8 %weight_grad.1 = (bf16[512,3584]{1,0:T(8,128)(2,1)S(1)}, f32[32,512]{1,0:T(8,128)S(1)}) custom-call(s32[2]{0:T(128)S(1)} %pad_add_fusion.place, bf16[64,3584]{1,0:T(8,128)(2,1)S(1)} %copy-done.11, bf16[64,3584]{1,0:T(8,128)(2,1)S(1)} %collective-permute-done.1.refs_1_, bf16[64,3584]{1,0:T(8,128)(2,1)S(1)} %collective-permute-done.refs_0_.refs_2_, ...), custom_call_target="tpu_custom_call" | custom-call | flops 1000000 | bytes 100000 | tf_op jit(solution)/shard_map/weight_grad/pallas_call | solution.py:199
  45.4 0.2 collective-permute-start.13
  45.6 0.4 collective-permute-start.14
  46.0 0.3 collective-permute-start.12
  46.3 1.0 collective-permute-done.13.refs_2_
  47.3 0.7 collective-permute-done.14.refs_3_
  48.0 1.6 %left_of_step.2 = (f32[32,512]{1,0:T(8,128)S(1)}, bf16[256,3584]{1,0:T(8,128)(2,1)S(1)}) custom-call(s32[2]{0:T(128)S(1)} %pad_add_fusion.place, bf16[64,3584]{1,0:T(8,128)(2,1)S(1)} %collective-permute-done.4.refs_0_, bf16[64,3584]{1,0:T(8,128)(2,1)S(1)} %collective-permute-done.9.refs_1_, bf16[64,3584]{1,0:T(8,128)(2,1)S(1)} %collective-permute-done.13.refs_2_, ...), custom_call_target="tpu_custom_call" | custom-call | flops 1000000 | bytes 100000 | tf_op jit(solution)/shard_map/left_of_step/pallas_call | solution.py:237
  49.6 1.2 %left_of_step.3 = (f32[32,512]{1,0:T(8,128)S(1)}, bf16[128,3584]{1,0:T(8,128)(2,1)S(1)}) custom-call(s32[2]{0:T(128)S(1)} %pad_add_fusion.place, bf16[64,3584]{1,0:T(8,128)(2,1)S(1)} %collective-permute-done.6.refs_0_, bf16[64,3584]{1,0:T(8,128)(2,1)S(1)} %collective-permute-done.12.refs_1_, bf16[512,1024]{1,0:T(8,128)(2,1)S(1)} %hidden.1.refs_10_.refs_4_.refs_2_.hidden_t, ...), custom_call_target="tpu_custom_call" | custom-call | flops 1000000 | bytes 100000 | tf_op jit(solution)/shard_map/left_of_step/pallas_call | solution.py:237
  50.8 2.8 %collective-permute-start.17 = (f32[32,512]{1,0:T(8,128)S(1)}, f32[32,512]{1,0:T(8,128)S(1)}, u32[]{:S(2)}, u32[]{:S(2)}) collective-permute-start(f32[32,512]{1,0:T(8,128)S(1)} %get-tuple-element.52), channel_id=1, source_target_pairs={{0,192},{1,49},{2,194},{3,51},{4,196},{5,53},{6,198},{7,55},{8,200... | collective-permute-start | bytes 196616 | tf_op jit(solution)/shard_map/ppermute | solution.py:110
  53.7 2.3 %collective-permute-start.15 = (f32[32,512]{1,0:T(8,128)S(1)}, f32[32,512]{1,0:T(8,128)S(1)}, u32[]{:S(2)}, u32[]{:S(2)}) collective-permute-start(f32[32,512]{1,0:T(8,128)S(1)} %get-tuple-element.52), channel_id=1, source_target_pairs={{0,128},{1,33},{2,130},{3,35},{4,132},{5,37},{6,134},{7,39},{8,136... | collective-permute-start | bytes 196616 | tf_op jit(solution)/shard_map/ppermute | solution.py:110
  56.0 2.8 %grad_pre.7.refs_4_ = bf16[2,1024,512]{2,1,0:T(8,128)(2,1)} custom-call(s32[2]{0:T(128)S(1)} %pad_add_fusion.place, bf16[64,3584]{1,0:T(8,128)(2,1)S(1)} %collective-permute-done.2.refs_6_.refs_0_, bf16[64,3584]{1,0:T(8,128)(2,1)S(1)} %collective-permute-done.5.refs_7_.refs_1_, ...), custom_call_target="tpu_custom_call", output_to_operand_aliasing={{}: (8, {})} | custom-call | flops 1000000 | bytes 100000 | tf_op jit(solution)/shard_map/grad_pre/pallas_call | solution.py:433
  58.7 2.7 %grad_pre.8.refs_3_ = bf16[2,1024,512]{2,1,0:T(8,128)(2,1)} custom-call(s32[2]{0:T(128)S(1)} %pad_add_fusion.place, bf16[256,3584]{1,0:T(8,128)(2,1)S(1)} %get-tuple-element.54.refs_0_.last_a, bf16[2,1024,512]{2,1,0:T(8,128)(2,1)S(1)} %copy-done.1, bf16[2,1024,512]{2,1,0:T(8,128)(2,1)S(1)} %copy-done.1, ...), custom_call_target="tpu_custom_call", output_to_operand_aliasing={{}: (5, {})} | custom-call | flops 1000000 | bytes 100000 | tf_op jit(solution)/shard_map/grad_pre/pallas_call | solution.py:433
  61.5 3.1 %collective-permute-start.20 = (f32[32,512]{1,0:T(8,128)S(1)}, f32[32,512]{1,0:T(8,128)S(1)}, u32[]{:S(2)}, u32[]{:S(2)}) collective-permute-start(f32[32,512]{1,0:T(8,128)S(1)} %add_add_fusion.l0), channel_id=1, source_target_pairs={{0,48},{1,193},{2,50},{3,195},{4,52},{5,197},{6,54},{7,199},{8,56}... | collective-permute-start | bytes 196616 | tf_op jit(solution)/shard_map/ppermute | solution.py:110
  64.6 0.6 collective-permute-start.19
  65.2 1.0 collective-permute-start.18
  66.2 2.6 %grad_pre.9 = bf16[2,1024,512]{2,1,0:T(8,128)(2,1)} custom-call(s32[2]{0:T(128)S(1)} %pad_add_fusion.place, bf16[128,3584]{1,0:T(8,128)(2,1)S(1)} %get-tuple-element.56.refs_0_.last_b, bf16[2,1024,512]{2,1,0:T(8,128)(2,1)S(1)} %copy-done.1, bf16[512,3584]{1,0:T(8,128)(2,1)S(1)} %copy-done.3, ...), custom_call_target="tpu_custom_call", output_to_operand_aliasing={{}: (4, {})} | custom-call | flops 1000000 | bytes 100000 | tf_op jit(solution)/shard_map/grad_pre/pallas_call | solution.py:433
  68.8 1.5 %collective-permute-done.19.l2 = f32[32,512]{1,0:T(8,128)S(1)} collective-permute-done((f32[32,512]{1,0:T(8,128)S(1)}, f32[32,512]{1,0:T(8,128)S(1)}, u32[]{:S(2)}, u32[]{:S(2)}) %collective-permute-start.19) | collective-permute-done | bytes 65568 | tf_op jit(solution)/shard_map/ppermute | solution.py:110
  70.4 0.7 collective-permute-done.18.l1
  71.1 5.0 %right_factor.1 = (f32[32,512]{1,0:T(8,128)}, bf16[16,2,3584]{2,1,0:T(2,128)(2,1)}) custom-call(f32[32,512]{1,0:T(8,128)S(1)} %add_add_fusion.l0, f32[32,512]{1,0:T(8,128)S(1)} %collective-permute-done.18.l1, f32[32,512]{1,0:T(8,128)S(1)} %collective-permute-done.19.l2, f32[32,512]{1,0:T(8,128)S(1)} %collective-permute-done.20.l3, ...), custom_call_target="tpu_custom_call" | custom-call | flops 100000000 | bytes 8000000 | tf_op jit(solution)/shard_map/right_factor/pallas_call | solution.py:278
  76.1 3.9 %all-to-all-start = ((bf16[16,2,3584]{2,1,0:T(2,128)(2,1)}), bf16[16,2,3584]{2,1,0:T(2,128)(2,1)S(1)}, u32[]{:S(2)}, u32[]{:S(2)}) async-start(bf16[16,2,3584]{2,1,0:T(2,128)(2,1)} %get-tuple-element.60), calls=%async_computation | async-start | bytes 458752 | tf_op jit(solution)/shard_map/all_to_all | solution.py:492
  80.0 3.4 %weight_grad_rest.2.lower = bf16[512,1792]{1,0:T(8,128)(2,1)S(1)} custom-call(bf16[512,1024]{1,0:T(8,128)(2,1)} %copy-done.4, bf16[256,3584]{1,0:T(8,128)(2,1)} %copy-done.6, bf16[128,3584]{1,0:T(8,128)(2,1)} %copy-done.7, bf16[512,3584]{1,0:T(8,128)(2,1)} %copy-done.5), custom_call_target="tpu_custom_call" | custom-call | flops 704643072 | bytes 6000000 | tf_op jit(solution)/shard_map/weight_grad_rest/pallas_call | solution.py:323
  83.5 4.8 %all-to-all-done.parts = bf16[16,2,3584]{2,1,0:T(2,128)(2,1)S(1)} async-done(((bf16[16,2,3584]{2,1,0:T(2,128)(2,1)}), bf16[16,2,3584]{2,1,0:T(2,128)(2,1)S(1)}, u32[]{:S(2)}, u32[]{:S(2)}) %all-to-all-start) | async-done | bytes 229408 | tf_op jit(solution)/shard_map/all_to_all | solution.py:492
  88.3 0.9 sum_of_ranks.1
  89.2 3.7 %all-to-all-start.1 = ((bf16[16,2,3584]{2,1,0:T(2,128)(2,1)}), bf16[16,2,3584]{2,1,0:T(2,128)(2,1)S(1)}, u32[]{:S(2)}, u32[]{:S(2)}) async-start(bf16[16,2,3584]{2,1,0:T(2,128)(2,1)} %sum_of_ranks.1), calls=%async_computation.1 | async-start | bytes 458752 | tf_op jit(solution)/shard_map/all_to_all | solution.py:495
  92.9 3.5 %weight_grad_rest.3.upper = bf16[512,1792]{1,0:T(8,128)(2,1)S(1)} custom-call(bf16[512,1024]{1,0:T(8,128)(2,1)} %copy-done.4, bf16[256,3584]{1,0:T(8,128)(2,1)} %copy-done.6, bf16[128,3584]{1,0:T(8,128)(2,1)} %copy-done.7, bf16[512,3584]{1,0:T(8,128)(2,1)} %copy-done.5), custom_call_target="tpu_custom_call" | custom-call | flops 704643072 | bytes 6000000 | tf_op jit(solution)/shard_map/weight_grad_rest/pallas_call | solution.py:323
  96.4 1.2 %copy-done.8 = bf16[512,1792]{1,0:T(8,128)(2,1)} copy-done((bf16[512,1792]{1,0:T(8,128)(2,1)}, bf16[512,1792]{1,0:T(8,128)(2,1)S(1)}, u32[]{:S(2)}) %copy-start.8) | copy-done | bytes 1835032
  97.6 3.6 %all-to-all-done.1.summed = bf16[16,2,3584]{2,1,0:T(2,128)(2,1)S(1)} async-done(((bf16[16,2,3584]{2,1,0:T(2,128)(2,1)}), bf16[16,2,3584]{2,1,0:T(2,128)(2,1)S(1)}, u32[]{:S(2)}, u32[]{:S(2)}) %all-to-all-start.1) | async-done | bytes 229408 | tf_op jit(solution)/shard_map/all_to_all | solution.py:495
  101.2 1.5 %copy-done.9 = bf16[512,1792]{1,0:T(8,128)(2,1)S(1)} copy-done((bf16[512,1792]{1,0:T(8,128)(2,1)S(1)}, bf16[512,1792]{1,0:T(8,128)(2,1)}, u32[]{:S(2)}) %copy-start.9) | copy-done | bytes 1835032
  102.7 3.8 %new_error.1 = (bf16[512,3584]{1,0:T(8,128)(2,1)}, f32[32,3584]{1,0:T(8,128)}) custom-call(f32[32,512]{1,0:T(8,128)S(1)} %copy-done.12, bf16[512,1792]{1,0:T(8,128)(2,1)S(1)} %weight_grad_rest.2.lower, bf16[512,1792]{1,0:T(8,128)(2,1)S(1)} %copy-done.9, bf16[16,2,3584]{2,1,0:T(2,128)(2,1)S(1)} %all-to-all-done.1.summed), custom_call_target="tpu_custom_call" | custom-call | flops 234881024 | bytes 8000000 | tf_op jit(solution)/shard_map/new_error/pallas_call | solution.py:364
  (44 shorter events, 0.3 us)
Async XLA Ops:
  0.6 7.7 %collective-permute-start.1 = (bf16[64,3584]{1,0:T(8,128)(2,1)}, bf16[64,3584]{1,0:T(8,128)(2,1)S(1)}, u32[]{:S(2)}, u32[]{:S(2)}) collective-permute-start(bf16[64,3584]{1,0:T(8,128)(2,1)} %refs_0_.3), channel_id=1, source_target_pairs={{0,1},{1,0},{2,3},{3,2},{4,5},{5,4},{6,7},{7,6},{8,9},{9,8},{10,11... | collective-permute-start | bytes 1376264 | tf_op jit(solution)/shard_map/ppermute | solution.py:90
  0.7 13.4 %collective-permute-start = (bf16[64,3584]{1,0:T(8,128)(2,1)}, bf16[64,3584]{1,0:T(8,128)(2,1)S(1)}, u32[]{:S(2)}, u32[]{:S(2)}) collective-permute-start(bf16[64,3584]{1,0:T(8,128)(2,1)} %refs_0_.3), channel_id=1, source_target_pairs={{0,2},{1,15},{2,4},{3,1},{4,6},{5,3},{6,8},{7,5},{8,10},{9,7},{10,... | collective-permute-start | bytes 1376264 | tf_op jit(solution)/shard_map/ppermute | solution.py:94
  4.0 1.6 %copy-start = (bf16[2,1024,512]{2,1,0:T(8,128)(2,1)S(1)}, bf16[2,1024,512]{2,1,0:T(8,128)(2,1)}, u32[]{:S(2)}) copy-start(bf16[2,1024,512]{2,1,0:T(8,128)(2,1)} %refs_1_.3) | copy-start | bytes 6291460
  5.6 3.8 %copy-start.1 = (bf16[2,1024,512]{2,1,0:T(8,128)(2,1)S(1)}, bf16[2,1024,512]{2,1,0:T(8,128)(2,1)}, u32[]{:S(2)}) copy-start(bf16[2,1024,512]{2,1,0:T(8,128)(2,1)} %refs_1_.3) | copy-start | bytes 6291460
  5.6 3.8 %copy-start.11 = (bf16[64,3584]{1,0:T(8,128)(2,1)S(1)}, bf16[64,3584]{1,0:T(8,128)(2,1)}, u32[]{:S(2)}) copy-start(bf16[64,3584]{1,0:T(8,128)(2,1)} %refs_0_.3) | copy-start | bytes 1376260
  5.6 19.3 %copy-start.13 = (f32[32,3584]{1,0:T(8,128)S(1)}, f32[32,3584]{1,0:T(8,128)}, u32[]{:S(2)}) copy-start(f32[32,3584]{1,0:T(8,128)} %param.9) | copy-start | bytes 1376260
  8.3 62.8 %copy-start.4 = (bf16[512,1024]{1,0:T(8,128)(2,1)}, bf16[512,1024]{1,0:T(8,128)(2,1)S(1)}, u32[]{:S(2)}) copy-start(bf16[512,1024]{1,0:T(8,128)(2,1)S(1)} %hidden.1.refs_10_.refs_4_.refs_2_.hidden_t) | copy-start | bytes 3145732
  8.3 8.6 %collective-permute-start.3 = (bf16[64,3584]{1,0:T(8,128)(2,1)S(1)}, bf16[64,3584]{1,0:T(8,128)(2,1)S(1)}, u32[]{:S(2)}, u32[]{:S(2)}) collective-permute-start(bf16[64,3584]{1,0:T(8,128)(2,1)S(1)} %collective-permute-done.1.refs_1_), channel_id=1, source_target_pairs={{0,2},{1,15},{2,4},{3,1},{4,6},{5,3},{6,8},{7,5},{8,10},{9,7},{10,... | collective-permute-start | bytes 1376264 | tf_op jit(solution)/shard_map/ppermute | solution.py:94
  9.4 2.0 %copy-start.2 = (bf16[512,3584]{1,0:T(8,128)(2,1)S(1)}, bf16[512,3584]{1,0:T(8,128)(2,1)}, u32[]{:S(2)}) copy-start(bf16[512,3584]{1,0:T(8,128)(2,1)} %refs_2_.5) | copy-start | bytes 11010052
  11.5 13.6 %copy-start.3 = (bf16[512,3584]{1,0:T(8,128)(2,1)S(1)}, bf16[512,3584]{1,0:T(8,128)(2,1)}, u32[]{:S(2)}) copy-start(bf16[512,3584]{1,0:T(8,128)(2,1)} %refs_2_.5) | copy-start | bytes 11010052
  14.1 8.6 %collective-permute-start.2 = (bf16[64,3584]{1,0:T(8,128)(2,1)S(1)}, bf16[64,3584]{1,0:T(8,128)(2,1)S(1)}, u32[]{:S(2)}, u32[]{:S(2)}) collective-permute-start(bf16[64,3584]{1,0:T(8,128)(2,1)S(1)} %collective-permute-done.refs_0_.refs_2_), channel_id=1, source_target_pairs={{0,2},{1,15},{2,4},{3,1},{4,6},{5,3},{6,8},{7,5},{8,10},{9,7},{10,... | collective-permute-start | bytes 1376264 | tf_op jit(solution)/shard_map/ppermute | solution.py:94
  16.9 8.1 %collective-permute-start.8 = (bf16[64,3584]{1,0:T(8,128)(2,1)S(1)}, bf16[64,3584]{1,0:T(8,128)(2,1)S(1)}, u32[]{:S(2)}, u32[]{:S(2)}) collective-permute-start(bf16[64,3584]{1,0:T(8,128)(2,1)S(1)} %collective-permute-done.3.refs_1_.refs_3_), channel_id=1, source_target_pairs={{0,1},{1,0},{2,3},{3,2},{4,5},{5,4},{6,7},{7,6},{8,9},{9,8},{10,11... | collective-permute-start | bytes 1376264 | tf_op jit(solution)/shard_map/ppermute | solution.py:90
  16.9 11.0 %collective-permute-start.5 = (bf16[64,3584]{1,0:T(8,128)(2,1)S(1)}, bf16[64,3584]{1,0:T(8,128)(2,1)S(1)}, u32[]{:S(2)}, u32[]{:S(2)}) collective-permute-start(bf16[64,3584]{1,0:T(8,128)(2,1)S(1)} %collective-permute-done.3.refs_1_.refs_3_), channel_id=1, source_target_pairs={{0,2},{1,15},{2,4},{3,1},{4,6},{5,3},{6,8},{7,5},{8,10},{9,7},{10,... | collective-permute-start | bytes 1376264 | tf_op jit(solution)/shard_map/ppermute | solution.py:94
  19.1 5.9 %collective-permute-start.7 = (bf16[64,3584]{1,0:T(8,128)(2,1)S(1)}, bf16[64,3584]{1,0:T(8,128)(2,1)S(1)}, u32[]{:S(2)}, u32[]{:S(2)}) collective-permute-start(bf16[64,3584]{1,0:T(8,128)(2,1)S(1)} %collective-permute-done.refs_0_.refs_2_), channel_id=1, source_target_pairs={{0,1},{1,0},{2,3},{3,2},{4,5},{5,4},{6,7},{7,6},{8,9},{9,8},{10,11... | collective-permute-start | bytes 1376264 | tf_op jit(solution)/shard_map/ppermute | solution.py:90
  22.7 9.8 %collective-permute-start.4 = (bf16[64,3584]{1,0:T(8,128)(2,1)S(1)}, bf16[64,3584]{1,0:T(8,128)(2,1)S(1)}, u32[]{:S(2)}, u32[]{:S(2)}) collective-permute-start(bf16[64,3584]{1,0:T(8,128)(2,1)S(1)} %collective-permute-done.2.refs_6_.refs_0_), channel_id=1, source_target_pairs={{0,2},{1,15},{2,4},{3,1},{4,6},{5,3},{6,8},{7,5},{8,10},{9,7},{10,... | collective-permute-start | bytes 1376264 | tf_op jit(solution)/shard_map/ppermute | solution.py:94
  25.1 11.5 %copy-start.10 = (bf16[512,3584]{1,0:T(8,128)(2,1)S(1)}, bf16[512,3584]{1,0:T(8,128)(2,1)}, u32[]{:S(2)}) copy-start(bf16[512,3584]{1,0:T(8,128)(2,1)} %refs_11_.1) | copy-start | bytes 11010052
  27.9 7.0 %collective-permute-start.11 = (bf16[64,3584]{1,0:T(8,128)(2,1)S(1)}, bf16[64,3584]{1,0:T(8,128)(2,1)S(1)}, u32[]{:S(2)}, u32[]{:S(2)}) collective-permute-start(bf16[64,3584]{1,0:T(8,128)(2,1)S(1)} %collective-permute-done.5.refs_7_.refs_1_), channel_id=1, source_target_pairs={{0,1},{1,0},{2,3},{3,2},{4,5},{5,4},{6,7},{7,6},{8,9},{9,8},{10,11... | collective-permute-start | bytes 1376264 | tf_op jit(solution)/shard_map/ppermute | solution.py:90
  28.0 17.4 %collective-permute-start.9 = (bf16[64,3584]{1,0:T(8,128)(2,1)S(1)}, bf16[64,3584]{1,0:T(8,128)(2,1)S(1)}, u32[]{:S(2)}, u32[]{:S(2)}) collective-permute-start(bf16[64,3584]{1,0:T(8,128)(2,1)S(1)} %collective-permute-done.5.refs_7_.refs_1_), channel_id=1, source_target_pairs={{0,2},{1,15},{2,4},{3,1},{4,6},{5,3},{6,8},{7,5},{8,10},{9,7},{10,... | collective-permute-start | bytes 1376264 | tf_op jit(solution)/shard_map/ppermute | solution.py:94
  32.5 13.5 %collective-permute-start.6 = (bf16[64,3584]{1,0:T(8,128)(2,1)S(1)}, bf16[64,3584]{1,0:T(8,128)(2,1)S(1)}, u32[]{:S(2)}, u32[]{:S(2)}) collective-permute-start(bf16[64,3584]{1,0:T(8,128)(2,1)S(1)} %collective-permute-done.4.refs_0_), channel_id=1, source_target_pairs={{0,2},{1,15},{2,4},{3,1},{4,6},{5,3},{6,8},{7,5},{8,10},{9,7},{10,... | collective-permute-start | bytes 1376264 | tf_op jit(solution)/shard_map/ppermute | solution.py:94
  34.8 1.8 %collective-permute-start.10 = (bf16[64,3584]{1,0:T(8,128)(2,1)S(1)}, bf16[64,3584]{1,0:T(8,128)(2,1)S(1)}, u32[]{:S(2)}, u32[]{:S(2)}) collective-permute-start(bf16[64,3584]{1,0:T(8,128)(2,1)S(1)} %collective-permute-done.2.refs_6_.refs_0_), channel_id=1, source_target_pairs={{0,1},{1,0},{2,3},{3,2},{4,5},{5,4},{6,7},{7,6},{8,9},{9,8},{10,11... | collective-permute-start | bytes 1376264 | tf_op jit(solution)/shard_map/ppermute | solution.py:90
  45.4 25.7 %copy-start.5 = (bf16[512,3584]{1,0:T(8,128)(2,1)}, bf16[512,3584]{1,0:T(8,128)(2,1)S(1)}, u32[]{:S(2)}) copy-start(bf16[512,3584]{1,0:T(8,128)(2,1)S(1)} %get-tuple-element.58.merged) | copy-start | bytes 11010052
  45.4 1.9 %collective-permute-start.13 = (bf16[64,3584]{1,0:T(8,128)(2,1)S(1)}, bf16[64,3584]{1,0:T(8,128)(2,1)S(1)}, u32[]{:S(2)}, u32[]{:S(2)}) collective-permute-start(bf16[64,3584]{1,0:T(8,128)(2,1)S(1)} %collective-permute-done.4.refs_0_), channel_id=1, source_target_pairs={{0,1},{1,0},{2,3},{3,2},{4,5},{5,4},{6,7},{7,6},{8,9},{9,8},{10,11... | collective-permute-start | bytes 1376264 | tf_op jit(solution)/shard_map/ppermute | solution.py:90
  45.6 2.3 %collective-permute-start.14 = (bf16[64,3584]{1,0:T(8,128)(2,1)S(1)}, bf16[64,3584]{1,0:T(8,128)(2,1)S(1)}, u32[]{:S(2)}, u32[]{:S(2)}) collective-permute-start(bf16[64,3584]{1,0:T(8,128)(2,1)S(1)} %collective-permute-done.9.refs_1_), channel_id=1, source_target_pairs={{0,1},{1,0},{2,3},{3,2},{4,5},{5,4},{6,7},{7,6},{8,9},{9,8},{10,11... | collective-permute-start | bytes 1376264 | tf_op jit(solution)/shard_map/ppermute | solution.py:90
  46.0 3.6 %collective-permute-start.12 = (bf16[64,3584]{1,0:T(8,128)(2,1)S(1)}, bf16[64,3584]{1,0:T(8,128)(2,1)S(1)}, u32[]{:S(2)}, u32[]{:S(2)}) collective-permute-start(bf16[64,3584]{1,0:T(8,128)(2,1)S(1)} %collective-permute-done.6.refs_0_), channel_id=1, source_target_pairs={{0,1},{1,0},{2,3},{3,2},{4,5},{5,4},{6,7},{7,6},{8,9},{9,8},{10,11... | collective-permute-start | bytes 1376264 | tf_op jit(solution)/shard_map/ppermute | solution.py:90
  49.5 21.5 %copy-start.6 = (bf16[256,3584]{1,0:T(8,128)(2,1)}, bf16[256,3584]{1,0:T(8,128)(2,1)S(1)}, u32[]{:S(2)}) copy-start(bf16[256,3584]{1,0:T(8,128)(2,1)S(1)} %get-tuple-element.54.refs_0_.last_a) | copy-start | bytes 5505028
  50.8 20.3 %copy-start.7 = (bf16[128,3584]{1,0:T(8,128)(2,1)}, bf16[128,3584]{1,0:T(8,128)(2,1)S(1)}, u32[]{:S(2)}) copy-start(bf16[128,3584]{1,0:T(8,128)(2,1)S(1)} %get-tuple-element.56.refs_0_.last_b) | copy-start | bytes 2752516
  50.8 10.6 %collective-permute-start.17 = (f32[32,512]{1,0:T(8,128)S(1)}, f32[32,512]{1,0:T(8,128)S(1)}, u32[]{:S(2)}, u32[]{:S(2)}) collective-permute-start(f32[32,512]{1,0:T(8,128)S(1)} %get-tuple-element.52), channel_id=1, source_target_pairs={{0,192},{1,49},{2,194},{3,51},{4,196},{5,53},{6,198},{7,55},{8,200... | collective-permute-start | bytes 196616 | tf_op jit(solution)/shard_map/ppermute | solution.py:110
  53.7 7.8 %collective-permute-start.16 = (f32[32,512]{1,0:T(8,128)S(1)}, f32[32,512]{1,0:T(8,128)S(1)}, u32[]{:S(2)}, u32[]{:S(2)}) collective-permute-start(f32[32,512]{1,0:T(8,128)S(1)} %get-tuple-element.52), channel_id=1, source_target_pairs={{0,64},{1,17},{2,66},{3,19},{4,68},{5,21},{6,70},{7,23},{8,72},{9,... | collective-permute-start | bytes 196616 | tf_op jit(solution)/shard_map/ppermute | solution.py:110
  53.7 7.8 %collective-permute-start.15 = (f32[32,512]{1,0:T(8,128)S(1)}, f32[32,512]{1,0:T(8,128)S(1)}, u32[]{:S(2)}, u32[]{:S(2)}) collective-permute-start(f32[32,512]{1,0:T(8,128)S(1)} %get-tuple-element.52), channel_id=1, source_target_pairs={{0,128},{1,33},{2,130},{3,35},{4,132},{5,37},{6,134},{7,39},{8,136... | collective-permute-start | bytes 196616 | tf_op jit(solution)/shard_map/ppermute | solution.py:110
  61.5 7.3 %collective-permute-start.20 = (f32[32,512]{1,0:T(8,128)S(1)}, f32[32,512]{1,0:T(8,128)S(1)}, u32[]{:S(2)}, u32[]{:S(2)}) collective-permute-start(f32[32,512]{1,0:T(8,128)S(1)} %add_add_fusion.l0), channel_id=1, source_target_pairs={{0,48},{1,193},{2,50},{3,195},{4,52},{5,197},{6,54},{7,199},{8,56}... | collective-permute-start | bytes 196616 | tf_op jit(solution)/shard_map/ppermute | solution.py:110
  64.6 5.8 %collective-permute-start.19 = (f32[32,512]{1,0:T(8,128)S(1)}, f32[32,512]{1,0:T(8,128)S(1)}, u32[]{:S(2)}, u32[]{:S(2)}) collective-permute-start(f32[32,512]{1,0:T(8,128)S(1)} %add_add_fusion.l0), channel_id=1, source_target_pairs={{0,32},{1,129},{2,34},{3,131},{4,36},{5,133},{6,38},{7,135},{8,40}... | collective-permute-start | bytes 196616 | tf_op jit(solution)/shard_map/ppermute | solution.py:110
  65.2 5.8 %collective-permute-start.18 = (f32[32,512]{1,0:T(8,128)S(1)}, f32[32,512]{1,0:T(8,128)S(1)}, u32[]{:S(2)}, u32[]{:S(2)}) collective-permute-start(f32[32,512]{1,0:T(8,128)S(1)} %add_add_fusion.l0), channel_id=1, source_target_pairs={{0,16},{1,65},{2,18},{3,67},{4,20},{5,69},{6,22},{7,71},{8,24},{9,... | collective-permute-start | bytes 196616 | tf_op jit(solution)/shard_map/ppermute | solution.py:110
  76.1 12.2 %all-to-all-start = ((bf16[16,2,3584]{2,1,0:T(2,128)(2,1)}), bf16[16,2,3584]{2,1,0:T(2,128)(2,1)S(1)}, u32[]{:S(2)}, u32[]{:S(2)}) async-start(bf16[16,2,3584]{2,1,0:T(2,128)(2,1)} %get-tuple-element.60), calls=%async_computation | async-start | bytes 458752 | tf_op jit(solution)/shard_map/all_to_all | solution.py:492
  89.2 12.0 %all-to-all-start.1 = ((bf16[16,2,3584]{2,1,0:T(2,128)(2,1)}), bf16[16,2,3584]{2,1,0:T(2,128)(2,1)S(1)}, u32[]{:S(2)}, u32[]{:S(2)}) async-start(bf16[16,2,3584]{2,1,0:T(2,128)(2,1)} %sum_of_ranks.1), calls=%async_computation.1 | async-start | bytes 458752 | tf_op jit(solution)/shard_map/all_to_all | solution.py:495
  92.9 8.3 %copy-start.12 = (f32[32,512]{1,0:T(8,128)S(1)}, f32[32,512]{1,0:T(8,128)}, u32[]{:S(2)}) copy-start(f32[32,512]{1,0:T(8,128)} %get-tuple-element.33.factor) | copy-start | bytes 196612
  96.4 1.2 %copy-start.8 = (bf16[512,1792]{1,0:T(8,128)(2,1)}, bf16[512,1792]{1,0:T(8,128)(2,1)S(1)}, u32[]{:S(2)}) copy-start(bf16[512,1792]{1,0:T(8,128)(2,1)S(1)} %weight_grad_rest.3.upper) | copy-start | bytes 5505028
  101.2 1.5 %copy-start.9 = (bf16[512,1792]{1,0:T(8,128)(2,1)S(1)}, bf16[512,1792]{1,0:T(8,128)(2,1)}, u32[]{:S(2)}) copy-start(bf16[512,1792]{1,0:T(8,128)(2,1)} %copy-done.8) | copy-start | bytes 5505028

commit v4 on v3

--- a/solution.py
+++ b/solution.py
@@ -383,7 +383,7 @@
 
 
 def slots_of_step(s):
-    return {0: [0], 4: [7]}.get(s, [2 * s - 1, 2 * s])
+    return {0: [0], 3: [5, 6, 7]}.get(s, [2 * s - 1, 2 * s])
 
 
 def finish_pre(grad, pre, stage):
@@ -394,7 +394,7 @@
 
 def pre_kernel(s, place, *refs):
     slots = slots_of_step(s)
-    count = 2 * len(slots) if s < 3 else 1
+    count = 2 if s == 3 else 2 * len(slots)
     pieces, refs = refs[:count], refs[count:]
     pres, refs = refs[: len(slots)], refs[len(slots) :]
     weight, (out, tokens, stage, sems) = refs[0], refs[-4:]
@@ -402,10 +402,9 @@
         for piece, row in zip(pieces, rows_of_step(s, place[1])):
             row = pl.multiple_of(row - slots[0] * CHIP, TOK)
             tokens[pl.ds(row, TOK), :] = piece[...]
-        here = tokens[...]
+        grad = dot(tokens[...], weight[...], 1, 1)
     else:
-        here = pieces[0][...]
-    grad = dot(here, weight[...], 1, 1)
+        grad = jnp.concatenate([dot(here[...], weight[...], 1, 1) for here in pieces], axis=0)
     copies = []
     for k, slot in enumerate(slots):
         finish_pre(grad[k * CHIP : (k + 1) * CHIP], pres[k], stage.at[k])
@@ -445,7 +444,7 @@
         ),
         out_shape=jax.ShapeDtypeStruct((2, ROWS, UNITS), BF),
         input_output_aliases=aliases,
-        compiler_params=params(10),
+        compiler_params=params(14),
         cost_estimate=SHORT,
         name="grad_pre",
     )(*args)
@@ -481,10 +480,9 @@
     left, last_a = left_call(3, place, [a3, b3, xa3, xb3], hidden_t, q3, left)
     left, last_b = left_call(4, place, [a4, xa4], hidden_t, q3, left)
 
-    grad_pre = pre_of(3, [after(last_a, left)], grad_pre)
     lefts = sum_over_ring(left, 0)
     left = sum_of_four(lefts[0], lefts[1], lefts[2], after(lefts[3], grad_pre))
-    grad_pre = pre_of(4, [after(last_b, left)], grad_pre)
+    grad_pre = pre_of(3, [after(last_a, left), last_b], grad_pre)
     lefts = sum_over_ring(left, 1)
     lefts[3] = after(lefts[3], grad_pre)
     p_factor, right = right_call(lefts, hidden_t, last_a, last_b, merged)

time: 107 us -> 107 us (level)
  Pallas kernels: 44.4 us -> 43 us
    pallas_call x5 -> x4, Pallas kernels: 13.5 us -> 12.1 us  [pre_call(): pl.pallas_call(functools.partial(pre_kernel, s), grid_spec=pltpu.Prefetch...]
  transfers between devices with their start and end apart: 23 -> 23, of which waited for: 10 -> 11; matrix products, arithmetic and copies ran while one was open for 0% -> 0% of each run, Pallas kernels for 31% -> 30%
where the time goes in v4:
time: 107 us; the launch traced here: 106 us
  Pallas kernels  43 us (40%)
  starting transfers between devices  33.5 us (31%)
  waiting for transfers between devices  21.9 us (20%)
  local copies, waits for them, and re-layouts  6.45 us (6%)
    ppermute x7, starting transfers between devices, along_z(): lax.ppermute(value, 'tensor', [(i, (i + 2 - 4 * (i % 2)) % (2 * NZ)) for...  13.9 us
    pallas_call x4, Pallas kernels, pre_call(): pl.pallas_call(functools.partial(pre_kernel, s), grid_spec=pltpu.Prefetch...  12.1 us
    ppermute x6, starting transfers between devices, sum_over_ring(): lax.ppermute(value, ('dp', 'tensor'), list(pairs(k)))  9.81 us
    pallas_call x1, Pallas kernels, main_call(): pl.pallas_call(main_kernel, grid_spec=pltpu.PrefetchScalarGridSpec(num_sc...  8.8 us
    ppermute x7, waiting for transfers between devices, along_z(): lax.ppermute(value, 'tensor', [(i, (i + 2 - 4 * (i % 2)) % (2 * NZ)) for...  7.92 us
    pallas_call x2, Pallas kernels, merge_call(): pl.pallas_call(merge_kernel, grid=(HALF // WIDE,), in_specs=[pl.BlockSpec...  6.89 us
    unnamed x28, local copies, waits for them, and re-layouts  6.45 us
    pallas_call x1, Pallas kernels, right_call(): pl.pallas_call(right_kernel, in_specs=[WHOLE] * 8, out_specs=[WHOLE] * 2,...  5.01 us
  transfers between devices with their start and end apart: 23, of which 11 were waited for; matrix products, arithmetic and copies ran while one was open for 0% of the time, Pallas kernels for 30%

profile of v4, /device:TPU:96, one launch (start us, length us, event | category | flops | bytes accessed | tf_op | source)
XLA Modules:
  0.0 105.9 jit_solution(5727063708786997082)
XLA Ops:
  0.6 0.1 collective-permute-start.1
  0.7 3.2 %collective-permute-start = (bf16[64,3584]{1,0:T(8,128)(2,1)}, bf16[64,3584]{1,0:T(8,128)(2,1)S(1)}, u32[]{:S(2)}, u32[]{:S(2)}) collective-permute-start(bf16[64,3584]{1,0:T(8,128)(2,1)} %refs_0_.3), channel_id=1, source_target_pairs={{0,2},{1,15},{2,4},{3,1},{4,6},{5,3},{6,8},{7,5},{8,10},{9,7},{10,... | collective-permute-start | bytes 1376264 | tf_op jit(solution)/shard_map/ppermute | solution.py:94
  4.0 1.6 %copy-done = bf16[2,1024,512]{2,1,0:T(8,128)(2,1)S(1)} copy-done((bf16[2,1024,512]{2,1,0:T(8,128)(2,1)S(1)}, bf16[2,1024,512]{2,1,0:T(8,128)(2,1)}, u32[]{:S(2)}) %copy-start) | copy-done | bytes 2097176
  5.6 2.7 %hidden.1.refs_10_.refs_4_.refs_2_.hidden_t = bf16[512,1024]{1,0:T(8,128)(2,1)S(1)} custom-call(s32[2]{0:T(128)S(1)} %pad_add_fusion.place, bf16[2,1024,512]{2,1,0:T(8,128)(2,1)S(1)} %copy-done), custom_call_target="tpu_custom_call" | custom-call | flops 1000000 | bytes 100000 | tf_op jit(solution)/shard_map/hidden/pallas_call | solution.py:155
  8.3 1.1 %collective-permute-start.3 = (bf16[64,3584]{1,0:T(8,128)(2,1)S(1)}, bf16[64,3584]{1,0:T(8,128)(2,1)S(1)}, u32[]{:S(2)}, u32[]{:S(2)}) collective-permute-start(bf16[64,3584]{1,0:T(8,128)(2,1)S(1)} %collective-permute-done.1.refs_1_), channel_id=1, source_target_pairs={{0,2},{1,15},{2,4},{3,1},{4,6},{5,3},{6,8},{7,5},{8,10},{9,7},{10,... | collective-permute-start | bytes 1376264 | tf_op jit(solution)/shard_map/ppermute | solution.py:94
  9.4 2.0 %copy-done.2 = bf16[512,3584]{1,0:T(8,128)(2,1)S(1)} copy-done((bf16[512,3584]{1,0:T(8,128)(2,1)S(1)}, bf16[512,3584]{1,0:T(8,128)(2,1)}, u32[]{:S(2)}) %copy-start.2) | copy-done | bytes 3670040
  11.5 2.7 %grad_pre.4.refs_7_ = bf16[2,1024,512]{2,1,0:T(8,128)(2,1)} custom-call(s32[2]{0:T(128)S(1)} %pad_add_fusion.place, bf16[64,3584]{1,0:T(8,128)(2,1)S(1)} %copy-done.11, bf16[64,3584]{1,0:T(8,128)(2,1)S(1)} %collective-permute-done.1.refs_1_, bf16[2,1024,512]{2,1,0:T(8,128)(2,1)S(1)} %copy-done.1, bf16[512,3584]{1,0:T(8,128)(2,1)S(1)} %copy-done.2), custom_call_target="tpu_custom_call" | custom-call | flops 1000000 | bytes 100000 | tf_op jit(solution)/shard_map/grad_pre/pallas_call | solution.py:432
  14.1 1.1 %collective-permute-start.2 = (bf16[64,3584]{1,0:T(8,128)(2,1)S(1)}, bf16[64,3584]{1,0:T(8,128)(2,1)S(1)}, u32[]{:S(2)}, u32[]{:S(2)}) collective-permute-start(bf16[64,3584]{1,0:T(8,128)(2,1)S(1)} %collective-permute-done.refs_0_.refs_2_), channel_id=1, source_target_pairs={{0,2},{1,15},{2,4},{3,1},{4,6},{5,3},{6,8},{7,5},{8,10},{9,7},{10,... | collective-permute-start | bytes 1376264 | tf_op jit(solution)/shard_map/ppermute | solution.py:94
  15.2 1.6 %collective-permute-done.3.refs_1_.refs_3_ = bf16[64,3584]{1,0:T(8,128)(2,1)S(1)} collective-permute-done((bf16[64,3584]{1,0:T(8,128)(2,1)S(1)}, bf16[64,3584]{1,0:T(8,128)(2,1)S(1)}, u32[]{:S(2)}, u32[]{:S(2)}) %collective-permute-start.3) | collective-permute-done | bytes 458784 | tf_op jit(solution)/shard_map/ppermute | solution.py:94
  16.9 2.2 %collective-permute-start.5 = (bf16[64,3584]{1,0:T(8,128)(2,1)S(1)}, bf16[64,3584]{1,0:T(8,128)(2,1)S(1)}, u32[]{:S(2)}, u32[]{:S(2)}) collective-permute-start(bf16[64,3584]{1,0:T(8,128)(2,1)S(1)} %collective-permute-done.3.refs_1_.refs_3_), channel_id=1, source_target_pairs={{0,2},{1,15},{2,4},{3,1},{4,6},{5,3},{6,8},{7,5},{8,10},{9,7},{10,... | collective-permute-start | bytes 1376264 | tf_op jit(solution)/shard_map/ppermute | solution.py:94
  19.1 3.6 %collective-permute-done.2.refs_6_.refs_0_ = bf16[64,3584]{1,0:T(8,128)(2,1)S(1)} collective-permute-done((bf16[64,3584]{1,0:T(8,128)(2,1)S(1)}, bf16[64,3584]{1,0:T(8,128)(2,1)S(1)}, u32[]{:S(2)}, u32[]{:S(2)}) %collective-permute-start.2) | collective-permute-done | bytes 458784 | tf_op jit(solution)/shard_map/ppermute | solution.py:94
  22.7 2.2 %collective-permute-start.4 = (bf16[64,3584]{1,0:T(8,128)(2,1)S(1)}, bf16[64,3584]{1,0:T(8,128)(2,1)S(1)}, u32[]{:S(2)}, u32[]{:S(2)}) collective-permute-start(bf16[64,3584]{1,0:T(8,128)(2,1)S(1)} %collective-permute-done.2.refs_6_.refs_0_), channel_id=1, source_target_pairs={{0,2},{1,15},{2,4},{3,1},{4,6},{5,3},{6,8},{7,5},{8,10},{9,7},{10,... | collective-permute-start | bytes 1376264 | tf_op jit(solution)/shard_map/ppermute | solution.py:94
  24.9 0.1 reduce-precision_convert_fusion.1
  25.1 2.8 %grad_pre.5.refs_7_ = bf16[2,1024,512]{2,1,0:T(8,128)(2,1)} custom-call(s32[2]{0:T(128)S(1)} %pad_add_fusion.place, bf16[64,3584]{1,0:T(8,128)(2,1)S(1)} %collective-permute-done.refs_0_.refs_2_, bf16[64,3584]{1,0:T(8,128)(2,1)S(1)} %collective-permute-done.3.refs_1_.refs_3_, ...), custom_call_target="tpu_custom_call", output_to_operand_aliasing={{}: (8, {})} | custom-call | flops 1000000 | bytes 100000 | tf_op jit(solution)/shard_map/grad_pre/pallas_call | solution.py:432
  27.9 0.1 collective-permute-start.10
  28.0 1.9 %collective-permute-start.8 = (bf16[64,3584]{1,0:T(8,128)(2,1)S(1)}, bf16[64,3584]{1,0:T(8,128)(2,1)S(1)}, u32[]{:S(2)}, u32[]{:S(2)}) collective-permute-start(bf16[64,3584]{1,0:T(8,128)(2,1)S(1)} %collective-permute-done.5.refs_7_.refs_1_), channel_id=1, source_target_pairs={{0,2},{1,15},{2,4},{3,1},{4,6},{5,3},{6,8},{7,5},{8,10},{9,7},{10,... | collective-permute-start | bytes 1376264 | tf_op jit(solution)/shard_map/ppermute | solution.py:94
  29.8 2.7 %collective-permute-done.4.refs_0_ = bf16[64,3584]{1,0:T(8,128)(2,1)S(1)} collective-permute-done((bf16[64,3584]{1,0:T(8,128)(2,1)S(1)}, bf16[64,3584]{1,0:T(8,128)(2,1)S(1)}, u32[]{:S(2)}, u32[]{:S(2)}) %collective-permute-start.4) | collective-permute-done | bytes 458784 | tf_op jit(solution)/shard_map/ppermute | solution.py:94
  32.5 2.2 %collective-permute-start.13 = (bf16[64,3584]{1,0:T(8,128)(2,1)S(1)}, bf16[64,3584]{1,0:T(8,128)(2,1)S(1)}, u32[]{:S(2)}, u32[]{:S(2)}) collective-permute-start(bf16[64,3584]{1,0:T(8,128)(2,1)S(1)} %collective-permute-done.4.refs_0_), channel_id=1, source_target_pairs={{0,2},{1,15},{2,4},{3,1},{4,6},{5,3},{6,8},{7,5},{8,10},{9,7},{10,... | collective-permute-start | bytes 1376264 | tf_op jit(solution)/shard_map/ppermute | solution.py:94
  34.8 1.7 %collective-permute-done.9.refs_8_.refs_2_ = bf16[64,3584]{1,0:T(8,128)(2,1)S(1)} collective-permute-done((bf16[64,3584]{1,0:T(8,128)(2,1)S(1)}, bf16[64,3584]{1,0:T(8,128)(2,1)S(1)}, u32[]{:S(2)}, u32[]{:S(2)}) %collective-permute-start.9) | collective-permute-done | bytes 458784 | tf_op jit(solution)/shard_map/ppermute | solution.py:90
  36.6 8.8 %weight_grad.1 = (bf16[512,3584]{1,0:T(8,128)(2,1)S(1)}, f32[32,512]{1,0:T(8,128)S(1)}) custom-call(s32[2]{0:T(128)S(1)} %pad_add_fusion.place, bf16[64,3584]{1,0:T(8,128)(2,1)S(1)} %copy-done.11, bf16[64,3584]{1,0:T(8,128)(2,1)S(1)} %collective-permute-done.1.refs_1_, bf16[64,3584]{1,0:T(8,128)(2,1)S(1)} %collective-permute-done.refs_0_.refs_2_, ...), custom_call_target="tpu_custom_call" | custom-call | flops 1000000 | bytes 100000 | tf_op jit(solution)/shard_map/weight_grad/pallas_call | solution.py:199
  45.4 0.2 collective-permute-start.11
  45.6 0.4 collective-permute-start.12
  46.0 0.3 collective-permute-start.14
  46.3 1.0 collective-permute-done.11.refs_2_
  47.3 0.7 collective-permute-done.12.refs_3_
  48.0 1.6 %left_of_step.2 = (f32[32,512]{1,0:T(8,128)S(1)}, bf16[256,3584]{1,0:T(8,128)(2,1)S(1)}) custom-call(s32[2]{0:T(128)S(1)} %pad_add_fusion.place, bf16[64,3584]{1,0:T(8,128)(2,1)S(1)} %collective-permute-done.4.refs_0_, bf16[64,3584]{1,0:T(8,128)(2,1)S(1)} %collective-permute-done.8.refs_1_, bf16[64,3584]{1,0:T(8,128)(2,1)S(1)} %collective-permute-done.11.refs_2_, ...), custom_call_target="tpu_custom_call" | custom-call | flops 1000000 | bytes 100000 | tf_op jit(solution)/shard_map/left_of_step/pallas_call | solution.py:237
  49.6 1.2 %left_of_step.3 = (f32[32,512]{1,0:T(8,128)S(1)}, bf16[128,3584]{1,0:T(8,128)(2,1)S(1)}) custom-call(s32[2]{0:T(128)S(1)} %pad_add_fusion.place, bf16[64,3584]{1,0:T(8,128)(2,1)S(1)} %collective-permute-done.13.refs_0_, bf16[64,3584]{1,0:T(8,128)(2,1)S(1)} %collective-permute-done.14.refs_1_, bf16[512,1024]{1,0:T(8,128)(2,1)S(1)} %hidden.1.refs_10_.refs_4_.refs_2_.hidden_t, ...), custom_call_target="tpu_custom_call" | custom-call | flops 1000000 | bytes 100000 | tf_op jit(solution)/shard_map/left_of_step/pallas_call | solution.py:237
  50.8 2.8 %collective-permute-start.17 = (f32[32,512]{1,0:T(8,128)S(1)}, f32[32,512]{1,0:T(8,128)S(1)}, u32[]{:S(2)}, u32[]{:S(2)}) collective-permute-start(f32[32,512]{1,0:T(8,128)S(1)} %get-tuple-element.51), channel_id=1, source_target_pairs={{0,192},{1,49},{2,194},{3,51},{4,196},{5,53},{6,198},{7,55},{8,200... | collective-permute-start | bytes 196616 | tf_op jit(solution)/shard_map/ppermute | solution.py:110
  53.7 2.3 %collective-permute-start.15 = (f32[32,512]{1,0:T(8,128)S(1)}, f32[32,512]{1,0:T(8,128)S(1)}, u32[]{:S(2)}, u32[]{:S(2)}) collective-permute-start(f32[32,512]{1,0:T(8,128)S(1)} %get-tuple-element.51), channel_id=1, source_target_pairs={{0,128},{1,33},{2,130},{3,35},{4,132},{5,37},{6,134},{7,39},{8,136... | collective-permute-start | bytes 196616 | tf_op jit(solution)/shard_map/ppermute | solution.py:110
  56.0 2.8 %grad_pre.6.refs_6_ = bf16[2,1024,512]{2,1,0:T(8,128)(2,1)} custom-call(s32[2]{0:T(128)S(1)} %pad_add_fusion.place, bf16[64,3584]{1,0:T(8,128)(2,1)S(1)} %collective-permute-done.2.refs_6_.refs_0_, bf16[64,3584]{1,0:T(8,128)(2,1)S(1)} %collective-permute-done.5.refs_7_.refs_1_, ...), custom_call_target="tpu_custom_call", output_to_operand_aliasing={{}: (8, {})} | custom-call | flops 1000000 | bytes 100000 | tf_op jit(solution)/shard_map/grad_pre/pallas_call | solution.py:432
  58.7 1.1 %collective-permute-done.16 = f32[32,512]{1,0:T(8,128)S(1)} collective-permute-done((f32[32,512]{1,0:T(8,128)S(1)}, f32[32,512]{1,0:T(8,128)S(1)}, u32[]{:S(2)}, u32[]{:S(2)}) %collective-permute-start.16) | collective-permute-done | bytes 65568 | tf_op jit(solution)/shard_map/ppermute | solution.py:110
  59.9 3.1 %collective-permute-start.20 = (f32[32,512]{1,0:T(8,128)S(1)}, f32[32,512]{1,0:T(8,128)S(1)}, u32[]{:S(2)}, u32[]{:S(2)}) collective-permute-start(f32[32,512]{1,0:T(8,128)S(1)} %add_add_fusion.l0), channel_id=1, source_target_pairs={{0,48},{1,193},{2,50},{3,195},{4,52},{5,197},{6,54},{7,199},{8,56}... | collective-permute-start | bytes 196616 | tf_op jit(solution)/shard_map/ppermute | solution.py:110
  63.0 0.6 collective-permute-start.19
  63.6 1.0 collective-permute-start.18
  64.6 3.9 %grad_pre.7 = bf16[2,1024,512]{2,1,0:T(8,128)(2,1)} custom-call(s32[2]{0:T(128)S(1)} %pad_add_fusion.place, bf16[256,3584]{1,0:T(8,128)(2,1)S(1)} %get-tuple-element.53.refs_0_.last_a, bf16[128,3584]{1,0:T(8,128)(2,1)S(1)} %get-tuple-element.54.refs_1_.last_b, bf16[2,1024,512]{2,1,0:T(8,128)(2,1)S(1)} %copy-done.1, ...), custom_call_target="tpu_custom_call", output_to_operand_aliasing={{}: (7, {})} | custom-call | flops 1000000 | bytes 100000 | tf_op jit(solution)/shard_map/grad_pre/pallas_call | solution.py:432
  68.4 0.3 collective-permute-done.19.l2
  68.8 0.7 collective-permute-done.18.l1
  69.5 5.0 %right_factor.1 = (f32[32,512]{1,0:T(8,128)}, bf16[16,2,3584]{2,1,0:T(2,128)(2,1)}) custom-call(f32[32,512]{1,0:T(8,128)S(1)} %add_add_fusion.l0, f32[32,512]{1,0:T(8,128)S(1)} %collective-permute-done.18.l1, f32[32,512]{1,0:T(8,128)S(1)} %collective-permute-done.19.l2, f32[32,512]{1,0:T(8,128)S(1)} %collective-permute-done.20.l3, ...), custom_call_target="tpu_custom_call" | custom-call | flops 100000000 | bytes 8000000 | tf_op jit(solution)/shard_map/right_factor/pallas_call | solution.py:278
  74.5 5.0 %all-to-all-start = ((bf16[16,2,3584]{2,1,0:T(2,128)(2,1)}), bf16[16,2,3584]{2,1,0:T(2,128)(2,1)S(1)}, u32[]{:S(2)}, u32[]{:S(2)}) async-start(bf16[16,2,3584]{2,1,0:T(2,128)(2,1)} %get-tuple-element.58), calls=%async_computation | async-start | bytes 458752 | tf_op jit(solution)/shard_map/all_to_all | solution.py:490
  79.4 3.4 %weight_grad_rest.2.lower = bf16[512,1792]{1,0:T(8,128)(2,1)S(1)} custom-call(bf16[512,1024]{1,0:T(8,128)(2,1)} %copy-done.4, bf16[256,3584]{1,0:T(8,128)(2,1)} %copy-done.6, bf16[128,3584]{1,0:T(8,128)(2,1)} %copy-done.7, bf16[512,3584]{1,0:T(8,128)(2,1)} %copy-done.5), custom_call_target="tpu_custom_call" | custom-call | flops 704643072 | bytes 6000000 | tf_op jit(solution)/shard_map/weight_grad_rest/pallas_call | solution.py:323
  82.9 4.8 %all-to-all-done.parts = bf16[16,2,3584]{2,1,0:T(2,128)(2,1)S(1)} async-done(((bf16[16,2,3584]{2,1,0:T(2,128)(2,1)}), bf16[16,2,3584]{2,1,0:T(2,128)(2,1)S(1)}, u32[]{:S(2)}, u32[]{:S(2)}) %all-to-all-start) | async-done | bytes 229408 | tf_op jit(solution)/shard_map/all_to_all | solution.py:490
  87.7 0.9 sum_of_ranks.1
  88.6 3.7 %all-to-all-start.1 = ((bf16[16,2,3584]{2,1,0:T(2,128)(2,1)}), bf16[16,2,3584]{2,1,0:T(2,128)(2,1)S(1)}, u32[]{:S(2)}, u32[]{:S(2)}) async-start(bf16[16,2,3584]{2,1,0:T(2,128)(2,1)} %sum_of_ranks.1), calls=%async_computation.1 | async-start | bytes 458752 | tf_op jit(solution)/shard_map/all_to_all | solution.py:493
  92.3 3.5 %weight_grad_rest.3.upper = bf16[512,1792]{1,0:T(8,128)(2,1)S(1)} custom-call(bf16[512,1024]{1,0:T(8,128)(2,1)} %copy-done.4, bf16[256,3584]{1,0:T(8,128)(2,1)} %copy-done.6, bf16[128,3584]{1,0:T(8,128)(2,1)} %copy-done.7, bf16[512,3584]{1,0:T(8,128)(2,1)} %copy-done.5), custom_call_target="tpu_custom_call" | custom-call | flops 704643072 | bytes 6000000 | tf_op jit(solution)/shard_map/weight_grad_rest/pallas_call | solution.py:323
  95.8 1.2 %copy-done.8 = bf16[512,1792]{1,0:T(8,128)(2,1)} copy-done((bf16[512,1792]{1,0:T(8,128)(2,1)}, bf16[512,1792]{1,0:T(8,128)(2,1)S(1)}, u32[]{:S(2)}) %copy-start.8) | copy-done | bytes 1835032
  97.0 3.6 %all-to-all-done.1.summed = bf16[16,2,3584]{2,1,0:T(2,128)(2,1)S(1)} async-done(((bf16[16,2,3584]{2,1,0:T(2,128)(2,1)}), bf16[16,2,3584]{2,1,0:T(2,128)(2,1)S(1)}, u32[]{:S(2)}, u32[]{:S(2)}) %all-to-all-start.1) | async-done | bytes 229408 | tf_op jit(solution)/shard_map/all_to_all | solution.py:493
  100.6 1.5 %copy-done.9 = bf16[512,1792]{1,0:T(8,128)(2,1)S(1)} copy-done((bf16[512,1792]{1,0:T(8,128)(2,1)S(1)}, bf16[512,1792]{1,0:T(8,128)(2,1)}, u32[]{:S(2)}) %copy-start.9) | copy-done | bytes 1835032
  102.1 3.8 %new_error.1 = (bf16[512,3584]{1,0:T(8,128)(2,1)}, f32[32,3584]{1,0:T(8,128)}) custom-call(f32[32,512]{1,0:T(8,128)S(1)} %copy-done.12, bf16[512,1792]{1,0:T(8,128)(2,1)S(1)} %weight_grad_rest.2.lower, bf16[512,1792]{1,0:T(8,128)(2,1)S(1)} %copy-done.9, bf16[16,2,3584]{2,1,0:T(2,128)(2,1)S(1)} %all-to-all-done.1.summed), custom_call_target="tpu_custom_call" | custom-call | flops 234881024 | bytes 8000000 | tf_op jit(solution)/shard_map/new_error/pallas_call | solution.py:364
  (43 shorter events, 0.3 us)
Async XLA Ops:
  0.6 7.7 %collective-permute-start.1 = (bf16[64,3584]{1,0:T(8,128)(2,1)}, bf16[64,3584]{1,0:T(8,128)(2,1)S(1)}, u32[]{:S(2)}, u32[]{:S(2)}) collective-permute-start(bf16[64,3584]{1,0:T(8,128)(2,1)} %refs_0_.3), channel_id=1, source_target_pairs={{0,1},{1,0},{2,3},{3,2},{4,5},{5,4},{6,7},{7,6},{8,9},{9,8},{10,11... | collective-permute-start | bytes 1376264 | tf_op jit(solution)/shard_map/ppermute | solution.py:90
  0.7 13.4 %collective-permute-start = (bf16[64,3584]{1,0:T(8,128)(2,1)}, bf16[64,3584]{1,0:T(8,128)(2,1)S(1)}, u32[]{:S(2)}, u32[]{:S(2)}) collective-permute-start(bf16[64,3584]{1,0:T(8,128)(2,1)} %refs_0_.3), channel_id=1, source_target_pairs={{0,2},{1,15},{2,4},{3,1},{4,6},{5,3},{6,8},{7,5},{8,10},{9,7},{10,... | collective-permute-start | bytes 1376264 | tf_op jit(solution)/shard_map/ppermute | solution.py:94
  4.0 1.6 %copy-start = (bf16[2,1024,512]{2,1,0:T(8,128)(2,1)S(1)}, bf16[2,1024,512]{2,1,0:T(8,128)(2,1)}, u32[]{:S(2)}) copy-start(bf16[2,1024,512]{2,1,0:T(8,128)(2,1)} %refs_4_.5) | copy-start | bytes 6291460
  5.6 3.8 %copy-start.1 = (bf16[2,1024,512]{2,1,0:T(8,128)(2,1)S(1)}, bf16[2,1024,512]{2,1,0:T(8,128)(2,1)}, u32[]{:S(2)}) copy-start(bf16[2,1024,512]{2,1,0:T(8,128)(2,1)} %refs_4_.5) | copy-start | bytes 6291460
  5.6 3.8 %copy-start.11 = (bf16[64,3584]{1,0:T(8,128)(2,1)S(1)}, bf16[64,3584]{1,0:T(8,128)(2,1)}, u32[]{:S(2)}) copy-start(bf16[64,3584]{1,0:T(8,128)(2,1)} %refs_0_.3) | copy-start | bytes 1376260
  5.6 19.3 %copy-start.13 = (f32[32,3584]{1,0:T(8,128)S(1)}, f32[32,3584]{1,0:T(8,128)}, u32[]{:S(2)}) copy-start(f32[32,3584]{1,0:T(8,128)} %param.9) | copy-start | bytes 1376260
  8.3 61.1 %copy-start.4 = (bf16[512,1024]{1,0:T(8,128)(2,1)}, bf16[512,1024]{1,0:T(8,128)(2,1)S(1)}, u32[]{:S(2)}) copy-start(bf16[512,1024]{1,0:T(8,128)(2,1)S(1)} %hidden.1.refs_10_.refs_4_.refs_2_.hidden_t) | copy-start | bytes 3145732
  8.3 8.6 %collective-permute-start.3 = (bf16[64,3584]{1,0:T(8,128)(2,1)S(1)}, bf16[64,3584]{1,0:T(8,128)(2,1)S(1)}, u32[]{:S(2)}, u32[]{:S(2)}) collective-permute-start(bf16[64,3584]{1,0:T(8,128)(2,1)S(1)} %collective-permute-done.1.refs_1_), channel_id=1, source_target_pairs={{0,2},{1,15},{2,4},{3,1},{4,6},{5,3},{6,8},{7,5},{8,10},{9,7},{10,... | collective-permute-start | bytes 1376264 | tf_op jit(solution)/shard_map/ppermute | solution.py:94
  9.4 2.0 %copy-start.2 = (bf16[512,3584]{1,0:T(8,128)(2,1)S(1)}, bf16[512,3584]{1,0:T(8,128)(2,1)}, u32[]{:S(2)}) copy-start(bf16[512,3584]{1,0:T(8,128)(2,1)} %refs_5_.5) | copy-start | bytes 11010052
  11.5 13.6 %copy-start.3 = (bf16[512,3584]{1,0:T(8,128)(2,1)S(1)}, bf16[512,3584]{1,0:T(8,128)(2,1)}, u32[]{:S(2)}) copy-start(bf16[512,3584]{1,0:T(8,128)(2,1)} %refs_5_.5) | copy-start | bytes 11010052
  14.1 8.6 %collective-permute-start.2 = (bf16[64,3584]{1,0:T(8,128)(2,1)S(1)}, bf16[64,3584]{1,0:T(8,128)(2,1)S(1)}, u32[]{:S(2)}, u32[]{:S(2)}) collective-permute-start(bf16[64,3584]{1,0:T(8,128)(2,1)S(1)} %collective-permute-done.refs_0_.refs_2_), channel_id=1, source_target_pairs={{0,2},{1,15},{2,4},{3,1},{4,6},{5,3},{6,8},{7,5},{8,10},{9,7},{10,... | collective-permute-start | bytes 1376264 | tf_op jit(solution)/shard_map/ppermute | solution.py:94
  16.9 8.1 %collective-permute-start.7 = (bf16[64,3584]{1,0:T(8,128)(2,1)S(1)}, bf16[64,3584]{1,0:T(8,128)(2,1)S(1)}, u32[]{:S(2)}, u32[]{:S(2)}) collective-permute-start(bf16[64,3584]{1,0:T(8,128)(2,1)S(1)} %collective-permute-done.3.refs_1_.refs_3_), channel_id=1, source_target_pairs={{0,1},{1,0},{2,3},{3,2},{4,5},{5,4},{6,7},{7,6},{8,9},{9,8},{10,11... | collective-permute-start | bytes 1376264 | tf_op jit(solution)/shard_map/ppermute | solution.py:90
  16.9 11.0 %collective-permute-start.5 = (bf16[64,3584]{1,0:T(8,128)(2,1)S(1)}, bf16[64,3584]{1,0:T(8,128)(2,1)S(1)}, u32[]{:S(2)}, u32[]{:S(2)}) collective-permute-start(bf16[64,3584]{1,0:T(8,128)(2,1)S(1)} %collective-permute-done.3.refs_1_.refs_3_), channel_id=1, source_target_pairs={{0,2},{1,15},{2,4},{3,1},{4,6},{5,3},{6,8},{7,5},{8,10},{9,7},{10,... | collective-permute-start | bytes 1376264 | tf_op jit(solution)/shard_map/ppermute | solution.py:94
  19.1 5.9 %collective-permute-start.6 = (bf16[64,3584]{1,0:T(8,128)(2,1)S(1)}, bf16[64,3584]{1,0:T(8,128)(2,1)S(1)}, u32[]{:S(2)}, u32[]{:S(2)}) collective-permute-start(bf16[64,3584]{1,0:T(8,128)(2,1)S(1)} %collective-permute-done.refs_0_.refs_2_), channel_id=1, source_target_pairs={{0,1},{1,0},{2,3},{3,2},{4,5},{5,4},{6,7},{7,6},{8,9},{9,8},{10,11... | collective-permute-start | bytes 1376264 | tf_op jit(solution)/shard_map/ppermute | solution.py:90
  22.7 9.8 %collective-permute-start.4 = (bf16[64,3584]{1,0:T(8,128)(2,1)S(1)}, bf16[64,3584]{1,0:T(8,128)(2,1)S(1)}, u32[]{:S(2)}, u32[]{:S(2)}) collective-permute-start(bf16[64,3584]{1,0:T(8,128)(2,1)S(1)} %collective-permute-done.2.refs_6_.refs_0_), channel_id=1, source_target_pairs={{0,2},{1,15},{2,4},{3,1},{4,6},{5,3},{6,8},{7,5},{8,10},{9,7},{10,... | collective-permute-start | bytes 1376264 | tf_op jit(solution)/shard_map/ppermute | solution.py:94
  25.1 11.5 %copy-start.10 = (bf16[512,3584]{1,0:T(8,128)(2,1)S(1)}, bf16[512,3584]{1,0:T(8,128)(2,1)}, u32[]{:S(2)}) copy-start(bf16[512,3584]{1,0:T(8,128)(2,1)} %refs_11_.1) | copy-start | bytes 11010052
  27.9 6.9 %collective-permute-start.10 = (bf16[64,3584]{1,0:T(8,128)(2,1)S(1)}, bf16[64,3584]{1,0:T(8,128)(2,1)S(1)}, u32[]{:S(2)}, u32[]{:S(2)}) collective-permute-start(bf16[64,3584]{1,0:T(8,128)(2,1)S(1)} %collective-permute-done.5.refs_7_.refs_1_), channel_id=1, source_target_pairs={{0,1},{1,0},{2,3},{3,2},{4,5},{5,4},{6,7},{7,6},{8,9},{9,8},{10,11... | collective-permute-start | bytes 1376264 | tf_op jit(solution)/shard_map/ppermute | solution.py:90
  28.0 17.4 %collective-permute-start.8 = (bf16[64,3584]{1,0:T(8,128)(2,1)S(1)}, bf16[64,3584]{1,0:T(8,128)(2,1)S(1)}, u32[]{:S(2)}, u32[]{:S(2)}) collective-permute-start(bf16[64,3584]{1,0:T(8,128)(2,1)S(1)} %collective-permute-done.5.refs_7_.refs_1_), channel_id=1, source_target_pairs={{0,2},{1,15},{2,4},{3,1},{4,6},{5,3},{6,8},{7,5},{8,10},{9,7},{10,... | collective-permute-start | bytes 1376264 | tf_op jit(solution)/shard_map/ppermute | solution.py:94
  32.5 13.5 %collective-permute-start.13 = (bf16[64,3584]{1,0:T(8,128)(2,1)S(1)}, bf16[64,3584]{1,0:T(8,128)(2,1)S(1)}, u32[]{:S(2)}, u32[]{:S(2)}) collective-permute-start(bf16[64,3584]{1,0:T(8,128)(2,1)S(1)} %collective-permute-done.4.refs_0_), channel_id=1, source_target_pairs={{0,2},{1,15},{2,4},{3,1},{4,6},{5,3},{6,8},{7,5},{8,10},{9,7},{10,... | collective-permute-start | bytes 1376264 | tf_op jit(solution)/shard_map/ppermute | solution.py:94
  34.8 1.8 %collective-permute-start.9 = (bf16[64,3584]{1,0:T(8,128)(2,1)S(1)}, bf16[64,3584]{1,0:T(8,128)(2,1)S(1)}, u32[]{:S(2)}, u32[]{:S(2)}) collective-permute-start(bf16[64,3584]{1,0:T(8,128)(2,1)S(1)} %collective-permute-done.2.refs_6_.refs_0_), channel_id=1, source_target_pairs={{0,1},{1,0},{2,3},{3,2},{4,5},{5,4},{6,7},{7,6},{8,9},{9,8},{10,11... | collective-permute-start | bytes 1376264 | tf_op jit(solution)/shard_map/ppermute | solution.py:90
  45.4 24.1 %copy-start.5 = (bf16[512,3584]{1,0:T(8,128)(2,1)}, bf16[512,3584]{1,0:T(8,128)(2,1)S(1)}, u32[]{:S(2)}) copy-start(bf16[512,3584]{1,0:T(8,128)(2,1)S(1)} %get-tuple-element.56.merged) | copy-start | bytes 11010052
  45.4 1.9 %collective-permute-start.11 = (bf16[64,3584]{1,0:T(8,128)(2,1)S(1)}, bf16[64,3584]{1,0:T(8,128)(2,1)S(1)}, u32[]{:S(2)}, u32[]{:S(2)}) collective-permute-start(bf16[64,3584]{1,0:T(8,128)(2,1)S(1)} %collective-permute-done.4.refs_0_), channel_id=1, source_target_pairs={{0,1},{1,0},{2,3},{3,2},{4,5},{5,4},{6,7},{7,6},{8,9},{9,8},{10,11... | collective-permute-start | bytes 1376264 | tf_op jit(solution)/shard_map/ppermute | solution.py:90
  45.6 2.3 %collective-permute-start.12 = (bf16[64,3584]{1,0:T(8,128)(2,1)S(1)}, bf16[64,3584]{1,0:T(8,128)(2,1)S(1)}, u32[]{:S(2)}, u32[]{:S(2)}) collective-permute-start(bf16[64,3584]{1,0:T(8,128)(2,1)S(1)} %collective-permute-done.8.refs_1_), channel_id=1, source_target_pairs={{0,1},{1,0},{2,3},{3,2},{4,5},{5,4},{6,7},{7,6},{8,9},{9,8},{10,11... | collective-permute-start | bytes 1376264 | tf_op jit(solution)/shard_map/ppermute | solution.py:90
  46.0 3.6 %collective-permute-start.14 = (bf16[64,3584]{1,0:T(8,128)(2,1)S(1)}, bf16[64,3584]{1,0:T(8,128)(2,1)S(1)}, u32[]{:S(2)}, u32[]{:S(2)}) collective-permute-start(bf16[64,3584]{1,0:T(8,128)(2,1)S(1)} %collective-permute-done.13.refs_0_), channel_id=1, source_target_pairs={{0,1},{1,0},{2,3},{3,2},{4,5},{5,4},{6,7},{7,6},{8,9},{9,8},{10,11... | collective-permute-start | bytes 1376264 | tf_op jit(solution)/shard_map/ppermute | solution.py:90
  49.5 19.9 %copy-start.6 = (bf16[256,3584]{1,0:T(8,128)(2,1)}, bf16[256,3584]{1,0:T(8,128)(2,1)S(1)}, u32[]{:S(2)}) copy-start(bf16[256,3584]{1,0:T(8,128)(2,1)S(1)} %get-tuple-element.53.refs_0_.last_a) | copy-start | bytes 5505028
  50.8 18.6 %copy-start.7 = (bf16[128,3584]{1,0:T(8,128)(2,1)}, bf16[128,3584]{1,0:T(8,128)(2,1)S(1)}, u32[]{:S(2)}) copy-start(bf16[128,3584]{1,0:T(8,128)(2,1)S(1)} %get-tuple-element.54.refs_1_.last_b) | copy-start | bytes 2752516
  50.8 7.9 %collective-permute-start.17 = (f32[32,512]{1,0:T(8,128)S(1)}, f32[32,512]{1,0:T(8,128)S(1)}, u32[]{:S(2)}, u32[]{:S(2)}) collective-permute-start(f32[32,512]{1,0:T(8,128)S(1)} %get-tuple-element.51), channel_id=1, source_target_pairs={{0,192},{1,49},{2,194},{3,51},{4,196},{5,53},{6,198},{7,55},{8,200... | collective-permute-start | bytes 196616 | tf_op jit(solution)/shard_map/ppermute | solution.py:110
  53.7 6.2 %collective-permute-start.16 = (f32[32,512]{1,0:T(8,128)S(1)}, f32[32,512]{1,0:T(8,128)S(1)}, u32[]{:S(2)}, u32[]{:S(2)}) collective-permute-start(f32[32,512]{1,0:T(8,128)S(1)} %get-tuple-element.51), channel_id=1, source_target_pairs={{0,64},{1,17},{2,66},{3,19},{4,68},{5,21},{6,70},{7,23},{8,72},{9,... | collective-permute-start | bytes 196616 | tf_op jit(solution)/shard_map/ppermute | solution.py:110
  53.7 6.2 %collective-permute-start.15 = (f32[32,512]{1,0:T(8,128)S(1)}, f32[32,512]{1,0:T(8,128)S(1)}, u32[]{:S(2)}, u32[]{:S(2)}) collective-permute-start(f32[32,512]{1,0:T(8,128)S(1)} %get-tuple-element.51), channel_id=1, source_target_pairs={{0,128},{1,33},{2,130},{3,35},{4,132},{5,37},{6,134},{7,39},{8,136... | collective-permute-start | bytes 196616 | tf_op jit(solution)/shard_map/ppermute | solution.py:110
  59.9 8.6 %collective-permute-start.20 = (f32[32,512]{1,0:T(8,128)S(1)}, f32[32,512]{1,0:T(8,128)S(1)}, u32[]{:S(2)}, u32[]{:S(2)}) collective-permute-start(f32[32,512]{1,0:T(8,128)S(1)} %add_add_fusion.l0), channel_id=1, source_target_pairs={{0,48},{1,193},{2,50},{3,195},{4,52},{5,197},{6,54},{7,199},{8,56}... | collective-permute-start | bytes 196616 | tf_op jit(solution)/shard_map/ppermute | solution.py:110
  63.0 5.8 %collective-permute-start.19 = (f32[32,512]{1,0:T(8,128)S(1)}, f32[32,512]{1,0:T(8,128)S(1)}, u32[]{:S(2)}, u32[]{:S(2)}) collective-permute-start(f32[32,512]{1,0:T(8,128)S(1)} %add_add_fusion.l0), channel_id=1, source_target_pairs={{0,32},{1,129},{2,34},{3,131},{4,36},{5,133},{6,38},{7,135},{8,40}... | collective-permute-start | bytes 196616 | tf_op jit(solution)/shard_map/ppermute | solution.py:110
  63.6 5.8 %collective-permute-start.18 = (f32[32,512]{1,0:T(8,128)S(1)}, f32[32,512]{1,0:T(8,128)S(1)}, u32[]{:S(2)}, u32[]{:S(2)}) collective-permute-start(f32[32,512]{1,0:T(8,128)S(1)} %add_add_fusion.l0), channel_id=1, source_target_pairs={{0,16},{1,65},{2,18},{3,67},{4,20},{5,69},{6,22},{7,71},{8,24},{9,... | collective-permute-start | bytes 196616 | tf_op jit(solution)/shard_map/ppermute | solution.py:110
  74.5 13.2 %all-to-all-start = ((bf16[16,2,3584]{2,1,0:T(2,128)(2,1)}), bf16[16,2,3584]{2,1,0:T(2,128)(2,1)S(1)}, u32[]{:S(2)}, u32[]{:S(2)}) async-start(bf16[16,2,3584]{2,1,0:T(2,128)(2,1)} %get-tuple-element.58), calls=%async_computation | async-start | bytes 458752 | tf_op jit(solution)/shard_map/all_to_all | solution.py:490
  88.6 12.0 %all-to-all-start.1 = ((bf16[16,2,3584]{2,1,0:T(2,128)(2,1)}), bf16[16,2,3584]{2,1,0:T(2,128)(2,1)S(1)}, u32[]{:S(2)}, u32[]{:S(2)}) async-start(bf16[16,2,3584]{2,1,0:T(2,128)(2,1)} %sum_of_ranks.1), calls=%async_computation.1 | async-start | bytes 458752 | tf_op jit(solution)/shard_map/all_to_all | solution.py:493
  92.3 8.3 %copy-start.12 = (f32[32,512]{1,0:T(8,128)S(1)}, f32[32,512]{1,0:T(8,128)}, u32[]{:S(2)}) copy-start(f32[32,512]{1,0:T(8,128)} %get-tuple-element.32.factor) | copy-start | bytes 196612
  95.8 1.2 %copy-start.8 = (bf16[512,1792]{1,0:T(8,128)(2,1)}, bf16[512,1792]{1,0:T(8,128)(2,1)S(1)}, u32[]{:S(2)}) copy-start(bf16[512,1792]{1,0:T(8,128)(2,1)S(1)} %weight_grad_rest.3.upper) | copy-start | bytes 5505028
  100.6 1.5 %copy-start.9 = (bf16[512,1792]{1,0:T(8,128)(2,1)S(1)}, bf16[512,1792]{1,0:T(8,128)(2,1)}, u32[]{:S(2)}) copy-start(bf16[512,1792]{1,0:T(8,128)(2,1)} %copy-done.8) | copy-start | bytes 5505028

commit v5 on v4

--- a/solution.py
+++ b/solution.py
@@ -318,6 +318,7 @@
 
 
 def merge_call(half, hidden_t, last_a, last_b, merged):
+    place = kept if half else kept_out
     first = half * (HALF // WIDE)
     cols = lambda rows: pl.BlockSpec((rows, WIDE), lambda i: (0, first + i))
     return pl.pallas_call(
@@ -330,18 +331,21 @@
             cols(UNITS),
         ],
         out_specs=pl.BlockSpec((UNITS, WIDE), lambda i: (0, i)),
-        out_shape=kept((UNITS, HALF), BF),
+        out_shape=place((UNITS, HALF), BF),
         compiler_params=params(14),
         cost_estimate=cost(3 * CHIP * UNITS * D, 6_000_000),
         name="weight_grad_rest",
     )(*map(from_hbm, (hidden_t, last_a, last_b, merged)))
 
 
-def error_kernel(factor, lower, upper, summed, out, q, p2_t):
+def error_kernel(factor, lower, upper, summed, out, q, p2_t, low, sem):
     i = pl.program_id(0)
+    per = HALF // WIDE
+    load = pltpu.make_async_copy(lower, low, sem)
 
     @pl.when(i == 0)
     def _():
+        load.start()
         p2_t[...] = jnp.concatenate(split(jnp.transpose(factor[...]), 2), axis=1)
 
     mean = summed[...].astype(F32).reshape(RANK, WIDE) * (1.0 / DP)
@@ -350,36 +354,45 @@
     rounded = jnp.concatenate([rounded, rounded], axis=0)
     estimate = dot(p2_t[...], rounded, 1, 0)
 
-    per = HALF // WIDE
+    @pl.when(i == per)
+    def _():
+        load.wait()
+
     for k in range(2 * per):
 
         @pl.when(i == k)
         def _():
-            part = (lower, upper)[k // per][:, k % per * WIDE : (k % per + 1) * WIDE]
+            part = (upper, low)[k // per][:, k % per * WIDE : (k % per + 1) * WIDE]
             out[...] = (part.astype(F32) - estimate).astype(BF)
 
 
 def error_call(factor, lower, upper, summed):
-    cols = lambda rows: pl.BlockSpec((rows, WIDE), lambda i: (0, i))
+    per = HALF // WIDE
+    turned = lambda i: lax.rem(i + per, 2 * per)
+    cols = lambda rows: pl.BlockSpec((rows, WIDE), lambda i: (0, turned(i)))
     return pl.pallas_call(
         error_kernel,
         grid=(D // WIDE,),
         in_specs=[
             pl.BlockSpec((RANK, UNITS), lambda i: (0, 0)),
+            pl.BlockSpec(memory_space=pl.ANY),
             WHOLE,
-            WHOLE,
-            pl.BlockSpec((DP, RANK // DP, WIDE), lambda i: (0, 0, i)),
+            pl.BlockSpec((DP, RANK // DP, WIDE), lambda i: (0, 0, turned(i))),
         ],
         out_specs=[cols(UNITS), cols(RANK)],
-        scratch_shapes=[pltpu.VMEM((UNITS, 2 * RANK), BF)],
+        scratch_shapes=[
+            pltpu.VMEM((UNITS, 2 * RANK), BF),
+            pltpu.VMEM((UNITS, HALF), BF),
+            pltpu.SemaphoreType.DMA,
+        ],
         out_shape=[
             jax.ShapeDtypeStruct((UNITS, D), BF),
             jax.ShapeDtypeStruct((RANK, D), F32),
         ],
-        compiler_params=params(8),
+        compiler_params=params(10),
         cost_estimate=cost(2 * 64 * UNITS * D, 8_000_000),
         name="new_error",
-    )(factor, held(lower), held(upper), summed)
+    )(factor, from_hbm(lower), held(upper), summed)
 
 
 def slots_of_step(s):

time: 107 us -> 106 us (level)
  local copies, waits for them, and re-layouts: 6.45 us -> 3.73 us
    unnamed x28 -> x24, local copies, waits for them, and re-layouts: 6.45 us -> 3.73 us
    all_to_all x1, waiting for transfers between devices: 3.56 us -> 4.79 us  [on_device(): right = lax.all_to_all(summed, 'dp', 0, 0, tiled=True)]
  transfers between devices with their start and end apart: 23 -> 23, of which waited for: 11 -> 11; matrix products, arithmetic and copies ran while one was open for 0% -> 0% of each run, Pallas kernels for 30% -> 31%
where the time goes in v5:
time: 106 us; the launch traced here: 105 us
  Pallas kernels  43.8 us (41%)
  starting transfers between devices  33.5 us (32%)
  waiting for transfers between devices  22.3 us (21%)
  local copies, waits for them, and re-layouts  3.73 us (4%)
  between operations  1.07 us (1%)
    ppermute x7, starting transfers between devices, along_z(): lax.ppermute(value, 'tensor', [(i, (i + 2 - 4 * (i % 2)) % (2 * NZ)) for...  13.9 us
    pallas_call x4, Pallas kernels, pre_call(): pl.pallas_call(functools.partial(pre_kernel, s), grid_spec=pltpu.Prefetch...  12.1 us
    ppermute x6, starting transfers between devices, sum_over_ring(): lax.ppermute(value, ('dp', 'tensor'), list(pairs(k)))  9.81 us
    pallas_call x1, Pallas kernels, main_call(): pl.pallas_call(main_kernel, grid_spec=pltpu.PrefetchScalarGridSpec(num_sc...  8.8 us
    ppermute x7, waiting for transfers between devices, along_z(): lax.ppermute(value, 'tensor', [(i, (i + 2 - 4 * (i % 2)) % (2 * NZ)) for...  7.92 us
    pallas_call x2, Pallas kernels, merge_call(): pl.pallas_call(merge_kernel, grid=(HALF // WIDE,), in_specs=[pl.BlockSpec...  7.7 us
    pallas_call x1, Pallas kernels, right_call(): pl.pallas_call(right_kernel, in_specs=[WHOLE] * 8, out_specs=[WHOLE] * 2,...  5.01 us
    all_to_all x1, starting transfers between devices, on_device(): parts = lax.all_to_all(right, 'dp', 0, 0, tiled=True)  4.97 us
  transfers between devices with their start and end apart: 23, of which 11 were waited for; matrix products, arithmetic and copies ran while one was open for 0% of the time, Pallas kernels for 31%

profile of v5, /device:TPU:96, one launch (start us, length us, event | category | flops | bytes accessed | tf_op | source)
XLA Modules:
  0.0 104.6 jit_solution(12141118718051592326)
XLA Ops:
  0.6 0.1 collective-permute-start.1
  0.7 3.2 %collective-permute-start = (bf16[64,3584]{1,0:T(8,128)(2,1)}, bf16[64,3584]{1,0:T(8,128)(2,1)S(1)}, u32[]{:S(2)}, u32[]{:S(2)}) collective-permute-start(bf16[64,3584]{1,0:T(8,128)(2,1)} %refs_0_.3), channel_id=1, source_target_pairs={{0,2},{1,15},{2,4},{3,1},{4,6},{5,3},{6,8},{7,5},{8,10},{9,7},{10,... | collective-permute-start | bytes 1376264 | tf_op jit(solution)/shard_map/ppermute | solution.py:94
  3.9 0.1 pad_add_fusion.place
  4.0 1.6 %copy-done = bf16[2,1024,512]{2,1,0:T(8,128)(2,1)S(1)} copy-done((bf16[2,1024,512]{2,1,0:T(8,128)(2,1)S(1)}, bf16[2,1024,512]{2,1,0:T(8,128)(2,1)}, u32[]{:S(2)}) %copy-start) | copy-done | bytes 2097176
  5.6 2.7 %hidden.1.refs_10_.refs_4_.refs_2_.hidden_t = bf16[512,1024]{1,0:T(8,128)(2,1)S(1)} custom-call(s32[2]{0:T(128)S(1)} %pad_add_fusion.place, bf16[2,1024,512]{2,1,0:T(8,128)(2,1)S(1)} %copy-done), custom_call_target="tpu_custom_call" | custom-call | flops 1000000 | bytes 100000 | tf_op jit(solution)/shard_map/hidden/pallas_call | solution.py:155
  8.3 1.1 %collective-permute-start.3 = (bf16[64,3584]{1,0:T(8,128)(2,1)S(1)}, bf16[64,3584]{1,0:T(8,128)(2,1)S(1)}, u32[]{:S(2)}, u32[]{:S(2)}) collective-permute-start(bf16[64,3584]{1,0:T(8,128)(2,1)S(1)} %collective-permute-done.1.refs_1_), channel_id=1, source_target_pairs={{0,2},{1,15},{2,4},{3,1},{4,6},{5,3},{6,8},{7,5},{8,10},{9,7},{10,... | collective-permute-start | bytes 1376264 | tf_op jit(solution)/shard_map/ppermute | solution.py:94
  9.4 2.0 %copy-done.2 = bf16[512,3584]{1,0:T(8,128)(2,1)S(1)} copy-done((bf16[512,3584]{1,0:T(8,128)(2,1)S(1)}, bf16[512,3584]{1,0:T(8,128)(2,1)}, u32[]{:S(2)}) %copy-start.2) | copy-done | bytes 3670040
  11.5 2.7 %grad_pre.4.refs_7_ = bf16[2,1024,512]{2,1,0:T(8,128)(2,1)} custom-call(s32[2]{0:T(128)S(1)} %pad_add_fusion.place, bf16[64,3584]{1,0:T(8,128)(2,1)S(1)} %copy-done.9, bf16[64,3584]{1,0:T(8,128)(2,1)S(1)} %collective-permute-done.1.refs_1_, bf16[2,1024,512]{2,1,0:T(8,128)(2,1)S(1)} %copy-done.1, bf16[512,3584]{1,0:T(8,128)(2,1)S(1)} %copy-done.2), custom_call_target="tpu_custom_call" | custom-call | flops 1000000 | bytes 100000 | tf_op jit(solution)/shard_map/grad_pre/pallas_call | solution.py:445
  14.1 1.1 %collective-permute-start.2 = (bf16[64,3584]{1,0:T(8,128)(2,1)S(1)}, bf16[64,3584]{1,0:T(8,128)(2,1)S(1)}, u32[]{:S(2)}, u32[]{:S(2)}) collective-permute-start(bf16[64,3584]{1,0:T(8,128)(2,1)S(1)} %collective-permute-done.refs_0_.refs_2_), channel_id=1, source_target_pairs={{0,2},{1,15},{2,4},{3,1},{4,6},{5,3},{6,8},{7,5},{8,10},{9,7},{10,... | collective-permute-start | bytes 1376264 | tf_op jit(solution)/shard_map/ppermute | solution.py:94
  15.2 1.6 %collective-permute-done.3.refs_1_.refs_3_ = bf16[64,3584]{1,0:T(8,128)(2,1)S(1)} collective-permute-done((bf16[64,3584]{1,0:T(8,128)(2,1)S(1)}, bf16[64,3584]{1,0:T(8,128)(2,1)S(1)}, u32[]{:S(2)}, u32[]{:S(2)}) %collective-permute-start.3) | collective-permute-done | bytes 458784 | tf_op jit(solution)/shard_map/ppermute | solution.py:94
  16.9 2.2 %collective-permute-start.5 = (bf16[64,3584]{1,0:T(8,128)(2,1)S(1)}, bf16[64,3584]{1,0:T(8,128)(2,1)S(1)}, u32[]{:S(2)}, u32[]{:S(2)}) collective-permute-start(bf16[64,3584]{1,0:T(8,128)(2,1)S(1)} %collective-permute-done.3.refs_1_.refs_3_), channel_id=1, source_target_pairs={{0,2},{1,15},{2,4},{3,1},{4,6},{5,3},{6,8},{7,5},{8,10},{9,7},{10,... | collective-permute-start | bytes 1376264 | tf_op jit(solution)/shard_map/ppermute | solution.py:94
  19.1 3.6 %collective-permute-done.2.refs_6_.refs_0_ = bf16[64,3584]{1,0:T(8,128)(2,1)S(1)} collective-permute-done((bf16[64,3584]{1,0:T(8,128)(2,1)S(1)}, bf16[64,3584]{1,0:T(8,128)(2,1)S(1)}, u32[]{:S(2)}, u32[]{:S(2)}) %collective-permute-start.2) | collective-permute-done | bytes 458784 | tf_op jit(solution)/shard_map/ppermute | solution.py:94
  22.7 2.2 %collective-permute-start.4 = (bf16[64,3584]{1,0:T(8,128)(2,1)S(1)}, bf16[64,3584]{1,0:T(8,128)(2,1)S(1)}, u32[]{:S(2)}, u32[]{:S(2)}) collective-permute-start(bf16[64,3584]{1,0:T(8,128)(2,1)S(1)} %collective-permute-done.2.refs_6_.refs_0_), channel_id=1, source_target_pairs={{0,2},{1,15},{2,4},{3,1},{4,6},{5,3},{6,8},{7,5},{8,10},{9,7},{10,... | collective-permute-start | bytes 1376264 | tf_op jit(solution)/shard_map/ppermute | solution.py:94
  24.9 0.1 reduce-precision_convert_fusion.1
  25.1 2.8 %grad_pre.5.refs_7_ = bf16[2,1024,512]{2,1,0:T(8,128)(2,1)} custom-call(s32[2]{0:T(128)S(1)} %pad_add_fusion.place, bf16[64,3584]{1,0:T(8,128)(2,1)S(1)} %collective-permute-done.refs_0_.refs_2_, bf16[64,3584]{1,0:T(8,128)(2,1)S(1)} %collective-permute-done.3.refs_1_.refs_3_, ...), custom_call_target="tpu_custom_call", output_to_operand_aliasing={{}: (8, {})} | custom-call | flops 1000000 | bytes 100000 | tf_op jit(solution)/shard_map/grad_pre/pallas_call | solution.py:445
  27.9 0.1 collective-permute-start.10
  28.0 1.9 %collective-permute-start.8 = (bf16[64,3584]{1,0:T(8,128)(2,1)S(1)}, bf16[64,3584]{1,0:T(8,128)(2,1)S(1)}, u32[]{:S(2)}, u32[]{:S(2)}) collective-permute-start(bf16[64,3584]{1,0:T(8,128)(2,1)S(1)} %collective-permute-done.5.refs_7_.refs_1_), channel_id=1, source_target_pairs={{0,2},{1,15},{2,4},{3,1},{4,6},{5,3},{6,8},{7,5},{8,10},{9,7},{10,... | collective-permute-start | bytes 1376264 | tf_op jit(solution)/shard_map/ppermute | solution.py:94
  29.8 2.7 %collective-permute-done.4.refs_0_ = bf16[64,3584]{1,0:T(8,128)(2,1)S(1)} collective-permute-done((bf16[64,3584]{1,0:T(8,128)(2,1)S(1)}, bf16[64,3584]{1,0:T(8,128)(2,1)S(1)}, u32[]{:S(2)}, u32[]{:S(2)}) %collective-permute-start.4) | collective-permute-done | bytes 458784 | tf_op jit(solution)/shard_map/ppermute | solution.py:94
  32.5 2.2 %collective-permute-start.13 = (bf16[64,3584]{1,0:T(8,128)(2,1)S(1)}, bf16[64,3584]{1,0:T(8,128)(2,1)S(1)}, u32[]{:S(2)}, u32[]{:S(2)}) collective-permute-start(bf16[64,3584]{1,0:T(8,128)(2,1)S(1)} %collective-permute-done.4.refs_0_), channel_id=1, source_target_pairs={{0,2},{1,15},{2,4},{3,1},{4,6},{5,3},{6,8},{7,5},{8,10},{9,7},{10,... | collective-permute-start | bytes 1376264 | tf_op jit(solution)/shard_map/ppermute | solution.py:94
  34.8 0.1 pad_maximum_fusion.refs_12_.refs_5_.refs_3_
  34.8 1.7 %collective-permute-done.9.refs_8_.refs_2_ = bf16[64,3584]{1,0:T(8,128)(2,1)S(1)} collective-permute-done((bf16[64,3584]{1,0:T(8,128)(2,1)S(1)}, bf16[64,3584]{1,0:T(8,128)(2,1)S(1)}, u32[]{:S(2)}, u32[]{:S(2)}) %collective-permute-start.9) | collective-permute-done | bytes 458784 | tf_op jit(solution)/shard_map/ppermute | solution.py:90
  36.6 8.8 %weight_grad.1 = (bf16[512,3584]{1,0:T(8,128)(2,1)S(1)}, f32[32,512]{1,0:T(8,128)S(1)}) custom-call(s32[2]{0:T(128)S(1)} %pad_add_fusion.place, bf16[64,3584]{1,0:T(8,128)(2,1)S(1)} %copy-done.9, bf16[64,3584]{1,0:T(8,128)(2,1)S(1)} %collective-permute-done.1.refs_1_, bf16[64,3584]{1,0:T(8,128)(2,1)S(1)} %collective-permute-done.refs_0_.refs_2_, ...), custom_call_target="tpu_custom_call" | custom-call | flops 1000000 | bytes 100000 | tf_op jit(solution)/shard_map/weight_grad/pallas_call | solution.py:199
  45.4 0.2 collective-permute-start.11
  45.6 0.4 collective-permute-start.12
  46.0 0.3 collective-permute-start.14
  46.3 1.0 collective-permute-done.11.refs_2_
  47.3 0.7 collective-permute-done.12.refs_3_
  48.0 1.6 %left_of_step.2 = (f32[32,512]{1,0:T(8,128)S(1)}, bf16[256,3584]{1,0:T(8,128)(2,1)S(1)}) custom-call(s32[2]{0:T(128)S(1)} %pad_add_fusion.place, bf16[64,3584]{1,0:T(8,128)(2,1)S(1)} %collective-permute-done.4.refs_0_, bf16[64,3584]{1,0:T(8,128)(2,1)S(1)} %collective-permute-done.8.refs_1_, bf16[64,3584]{1,0:T(8,128)(2,1)S(1)} %collective-permute-done.11.refs_2_, ...), custom_call_target="tpu_custom_call" | custom-call | flops 1000000 | bytes 100000 | tf_op jit(solution)/shard_map/left_of_step/pallas_call | solution.py:237
  49.6 1.2 %left_of_step.3 = (f32[32,512]{1,0:T(8,128)S(1)}, bf16[128,3584]{1,0:T(8,128)(2,1)S(1)}) custom-call(s32[2]{0:T(128)S(1)} %pad_add_fusion.place, bf16[64,3584]{1,0:T(8,128)(2,1)S(1)} %collective-permute-done.13.refs_0_, bf16[64,3584]{1,0:T(8,128)(2,1)S(1)} %collective-permute-done.14.refs_1_, bf16[512,1024]{1,0:T(8,128)(2,1)S(1)} %hidden.1.refs_10_.refs_4_.refs_2_.hidden_t, ...), custom_call_target="tpu_custom_call" | custom-call | flops 1000000 | bytes 100000 | tf_op jit(solution)/shard_map/left_of_step/pallas_call | solution.py:237
  50.8 2.8 %collective-permute-start.17 = (f32[32,512]{1,0:T(8,128)S(1)}, f32[32,512]{1,0:T(8,128)S(1)}, u32[]{:S(2)}, u32[]{:S(2)}) collective-permute-start(f32[32,512]{1,0:T(8,128)S(1)} %get-tuple-element.51), channel_id=1, source_target_pairs={{0,192},{1,49},{2,194},{3,51},{4,196},{5,53},{6,198},{7,55},{8,200... | collective-permute-start | bytes 196616 | tf_op jit(solution)/shard_map/ppermute | solution.py:110
  53.7 2.3 %collective-permute-start.15 = (f32[32,512]{1,0:T(8,128)S(1)}, f32[32,512]{1,0:T(8,128)S(1)}, u32[]{:S(2)}, u32[]{:S(2)}) collective-permute-start(f32[32,512]{1,0:T(8,128)S(1)} %get-tuple-element.51), channel_id=1, source_target_pairs={{0,128},{1,33},{2,130},{3,35},{4,132},{5,37},{6,134},{7,39},{8,136... | collective-permute-start | bytes 196616 | tf_op jit(solution)/shard_map/ppermute | solution.py:110
  56.0 2.8 %grad_pre.6.refs_6_ = bf16[2,1024,512]{2,1,0:T(8,128)(2,1)} custom-call(s32[2]{0:T(128)S(1)} %pad_add_fusion.place, bf16[64,3584]{1,0:T(8,128)(2,1)S(1)} %collective-permute-done.2.refs_6_.refs_0_, bf16[64,3584]{1,0:T(8,128)(2,1)S(1)} %collective-permute-done.5.refs_7_.refs_1_, ...), custom_call_target="tpu_custom_call", output_to_operand_aliasing={{}: (8, {})} | custom-call | flops 1000000 | bytes 100000 | tf_op jit(solution)/shard_map/grad_pre/pallas_call | solution.py:445
  58.7 1.1 %collective-permute-done.16 = f32[32,512]{1,0:T(8,128)S(1)} collective-permute-done((f32[32,512]{1,0:T(8,128)S(1)}, f32[32,512]{1,0:T(8,128)S(1)}, u32[]{:S(2)}, u32[]{:S(2)}) %collective-permute-start.16) | collective-permute-done | bytes 65568 | tf_op jit(solution)/shard_map/ppermute | solution.py:110
  59.9 3.1 %collective-permute-start.20 = (f32[32,512]{1,0:T(8,128)S(1)}, f32[32,512]{1,0:T(8,128)S(1)}, u32[]{:S(2)}, u32[]{:S(2)}) collective-permute-start(f32[32,512]{1,0:T(8,128)S(1)} %add_add_fusion.l0), channel_id=1, source_target_pairs={{0,48},{1,193},{2,50},{3,195},{4,52},{5,197},{6,54},{7,199},{8,56}... | collective-permute-start | bytes 196616 | tf_op jit(solution)/shard_map/ppermute | solution.py:110
  63.0 0.6 collective-permute-start.19
  63.6 1.0 collective-permute-start.18
  64.6 3.9 %grad_pre.7 = bf16[2,1024,512]{2,1,0:T(8,128)(2,1)} custom-call(s32[2]{0:T(128)S(1)} %pad_add_fusion.place, bf16[256,3584]{1,0:T(8,128)(2,1)S(1)} %get-tuple-element.53.refs_0_.last_a, bf16[128,3584]{1,0:T(8,128)(2,1)S(1)} %get-tuple-element.54.refs_1_.last_b, bf16[2,1024,512]{2,1,0:T(8,128)(2,1)S(1)} %copy-done.1, ...), custom_call_target="tpu_custom_call", output_to_operand_aliasing={{}: (7, {})} | custom-call | flops 1000000 | bytes 100000 | tf_op jit(solution)/shard_map/grad_pre/pallas_call | solution.py:445
  68.4 0.3 collective-permute-done.19.l2
  68.8 0.7 collective-permute-done.18.l1
  69.5 5.0 %right_factor.1 = (f32[32,512]{1,0:T(8,128)}, bf16[16,2,3584]{2,1,0:T(2,128)(2,1)}) custom-call(f32[32,512]{1,0:T(8,128)S(1)} %add_add_fusion.l0, f32[32,512]{1,0:T(8,128)S(1)} %collective-permute-done.18.l1, f32[32,512]{1,0:T(8,128)S(1)} %collective-permute-done.19.l2, f32[32,512]{1,0:T(8,128)S(1)} %collective-permute-done.20.l3, ...), custom_call_target="tpu_custom_call" | custom-call | flops 100000000 | bytes 8000000 | tf_op jit(solution)/shard_map/right_factor/pallas_call | solution.py:278
  74.5 5.0 %all-to-all-start = ((bf16[16,2,3584]{2,1,0:T(2,128)(2,1)}), bf16[16,2,3584]{2,1,0:T(2,128)(2,1)S(1)}, u32[]{:S(2)}, u32[]{:S(2)}) async-start(bf16[16,2,3584]{2,1,0:T(2,128)(2,1)} %get-tuple-element.58), calls=%async_computation | async-start | bytes 458752 | tf_op jit(solution)/shard_map/all_to_all | solution.py:503
  79.4 4.2 %weight_grad_rest.2.lower = bf16[512,1792]{1,0:T(8,128)(2,1)} custom-call(bf16[512,1024]{1,0:T(8,128)(2,1)} %copy-done.4, bf16[256,3584]{1,0:T(8,128)(2,1)} %copy-done.6, bf16[128,3584]{1,0:T(8,128)(2,1)} %copy-done.7, bf16[512,3584]{1,0:T(8,128)(2,1)} %copy-done.5), custom_call_target="tpu_custom_call" | custom-call | flops 704643072 | bytes 6000000 | tf_op jit(solution)/shard_map/weight_grad_rest/pallas_call | solution.py:324
  83.7 4.0 %all-to-all-done.parts = bf16[16,2,3584]{2,1,0:T(2,128)(2,1)S(1)} async-done(((bf16[16,2,3584]{2,1,0:T(2,128)(2,1)}), bf16[16,2,3584]{2,1,0:T(2,128)(2,1)S(1)}, u32[]{:S(2)}, u32[]{:S(2)}) %all-to-all-start) | async-done | bytes 229408 | tf_op jit(solution)/shard_map/all_to_all | solution.py:503
  87.7 0.9 sum_of_ranks.1
  88.6 3.7 %all-to-all-start.1 = ((bf16[16,2,3584]{2,1,0:T(2,128)(2,1)}), bf16[16,2,3584]{2,1,0:T(2,128)(2,1)S(1)}, u32[]{:S(2)}, u32[]{:S(2)}) async-start(bf16[16,2,3584]{2,1,0:T(2,128)(2,1)} %sum_of_ranks.1), calls=%async_computation.1 | async-start | bytes 458752 | tf_op jit(solution)/shard_map/all_to_all | solution.py:506
  92.3 3.5 %weight_grad_rest.3.upper = bf16[512,1792]{1,0:T(8,128)(2,1)S(1)} custom-call(bf16[512,1024]{1,0:T(8,128)(2,1)} %copy-done.4, bf16[256,3584]{1,0:T(8,128)(2,1)} %copy-done.6, bf16[128,3584]{1,0:T(8,128)(2,1)} %copy-done.7, bf16[512,3584]{1,0:T(8,128)(2,1)} %copy-done.5), custom_call_target="tpu_custom_call" | custom-call | flops 704643072 | bytes 6000000 | tf_op jit(solution)/shard_map/weight_grad_rest/pallas_call | solution.py:324
  95.8 4.8 %all-to-all-done.1.summed = bf16[16,2,3584]{2,1,0:T(2,128)(2,1)S(1)} async-done(((bf16[16,2,3584]{2,1,0:T(2,128)(2,1)}), bf16[16,2,3584]{2,1,0:T(2,128)(2,1)S(1)}, u32[]{:S(2)}, u32[]{:S(2)}) %all-to-all-start.1) | async-done | bytes 229408 | tf_op jit(solution)/shard_map/all_to_all | solution.py:506
  100.6 3.9 %new_error.1 = (bf16[512,3584]{1,0:T(8,128)(2,1)}, f32[32,3584]{1,0:T(8,128)}) custom-call(f32[32,512]{1,0:T(8,128)S(1)} %copy-done.10, bf16[512,1792]{1,0:T(8,128)(2,1)} %weight_grad_rest.2.lower, bf16[512,1792]{1,0:T(8,128)(2,1)S(1)} %weight_grad_rest.3.upper, bf16[16,2,3584]{2,1,0:T(2,128)(2,1)S(1)} %all-to-all-done.1.summed), custom_call_target="tpu_custom_call" | custom-call | flops 234881024 | bytes 8000000 | tf_op jit(solution)/shard_map/new_error/pallas_call | solution.py:373
  (39 shorter events, 0.2 us)
Async XLA Ops:
  0.6 7.7 %collective-permute-start.1 = (bf16[64,3584]{1,0:T(8,128)(2,1)}, bf16[64,3584]{1,0:T(8,128)(2,1)S(1)}, u32[]{:S(2)}, u32[]{:S(2)}) collective-permute-start(bf16[64,3584]{1,0:T(8,128)(2,1)} %refs_0_.3), channel_id=1, source_target_pairs={{0,1},{1,0},{2,3},{3,2},{4,5},{5,4},{6,7},{7,6},{8,9},{9,8},{10,11... | collective-permute-start | bytes 1376264 | tf_op jit(solution)/shard_map/ppermute | solution.py:90
  0.7 13.4 %collective-permute-start = (bf16[64,3584]{1,0:T(8,128)(2,1)}, bf16[64,3584]{1,0:T(8,128)(2,1)S(1)}, u32[]{:S(2)}, u32[]{:S(2)}) collective-permute-start(bf16[64,3584]{1,0:T(8,128)(2,1)} %refs_0_.3), channel_id=1, source_target_pairs={{0,2},{1,15},{2,4},{3,1},{4,6},{5,3},{6,8},{7,5},{8,10},{9,7},{10,... | collective-permute-start | bytes 1376264 | tf_op jit(solution)/shard_map/ppermute | solution.py:94
  4.0 1.6 %copy-start = (bf16[2,1024,512]{2,1,0:T(8,128)(2,1)S(1)}, bf16[2,1024,512]{2,1,0:T(8,128)(2,1)}, u32[]{:S(2)}) copy-start(bf16[2,1024,512]{2,1,0:T(8,128)(2,1)} %refs_4_.5) | copy-start | bytes 6291460
  5.6 3.8 %copy-start.1 = (bf16[2,1024,512]{2,1,0:T(8,128)(2,1)S(1)}, bf16[2,1024,512]{2,1,0:T(8,128)(2,1)}, u32[]{:S(2)}) copy-start(bf16[2,1024,512]{2,1,0:T(8,128)(2,1)} %refs_4_.5) | copy-start | bytes 6291460
  5.6 3.8 %copy-start.9 = (bf16[64,3584]{1,0:T(8,128)(2,1)S(1)}, bf16[64,3584]{1,0:T(8,128)(2,1)}, u32[]{:S(2)}) copy-start(bf16[64,3584]{1,0:T(8,128)(2,1)} %refs_0_.3) | copy-start | bytes 1376260
  5.6 19.3 %copy-start.11 = (f32[32,3584]{1,0:T(8,128)S(1)}, f32[32,3584]{1,0:T(8,128)}, u32[]{:S(2)}) copy-start(f32[32,3584]{1,0:T(8,128)} %param.9) | copy-start | bytes 1376260
  8.3 61.1 %copy-start.4 = (bf16[512,1024]{1,0:T(8,128)(2,1)}, bf16[512,1024]{1,0:T(8,128)(2,1)S(1)}, u32[]{:S(2)}) copy-start(bf16[512,1024]{1,0:T(8,128)(2,1)S(1)} %hidden.1.refs_10_.refs_4_.refs_2_.hidden_t) | copy-start | bytes 3145732
  8.3 8.6 %collective-permute-start.3 = (bf16[64,3584]{1,0:T(8,128)(2,1)S(1)}, bf16[64,3584]{1,0:T(8,128)(2,1)S(1)}, u32[]{:S(2)}, u32[]{:S(2)}) collective-permute-start(bf16[64,3584]{1,0:T(8,128)(2,1)S(1)} %collective-permute-done.1.refs_1_), channel_id=1, source_target_pairs={{0,2},{1,15},{2,4},{3,1},{4,6},{5,3},{6,8},{7,5},{8,10},{9,7},{10,... | collective-permute-start | bytes 1376264 | tf_op jit(solution)/shard_map/ppermute | solution.py:94
  9.4 2.0 %copy-start.2 = (bf16[512,3584]{1,0:T(8,128)(2,1)S(1)}, bf16[512,3584]{1,0:T(8,128)(2,1)}, u32[]{:S(2)}) copy-start(bf16[512,3584]{1,0:T(8,128)(2,1)} %refs_5_.5) | copy-start | bytes 11010052
  11.5 13.6 %copy-start.3 = (bf16[512,3584]{1,0:T(8,128)(2,1)S(1)}, bf16[512,3584]{1,0:T(8,128)(2,1)}, u32[]{:S(2)}) copy-start(bf16[512,3584]{1,0:T(8,128)(2,1)} %refs_5_.5) | copy-start | bytes 11010052
  14.1 8.6 %collective-permute-start.2 = (bf16[64,3584]{1,0:T(8,128)(2,1)S(1)}, bf16[64,3584]{1,0:T(8,128)(2,1)S(1)}, u32[]{:S(2)}, u32[]{:S(2)}) collective-permute-start(bf16[64,3584]{1,0:T(8,128)(2,1)S(1)} %collective-permute-done.refs_0_.refs_2_), channel_id=1, source_target_pairs={{0,2},{1,15},{2,4},{3,1},{4,6},{5,3},{6,8},{7,5},{8,10},{9,7},{10,... | collective-permute-start | bytes 1376264 | tf_op jit(solution)/shard_map/ppermute | solution.py:94
  16.9 8.1 %collective-permute-start.7 = (bf16[64,3584]{1,0:T(8,128)(2,1)S(1)}, bf16[64,3584]{1,0:T(8,128)(2,1)S(1)}, u32[]{:S(2)}, u32[]{:S(2)}) collective-permute-start(bf16[64,3584]{1,0:T(8,128)(2,1)S(1)} %collective-permute-done.3.refs_1_.refs_3_), channel_id=1, source_target_pairs={{0,1},{1,0},{2,3},{3,2},{4,5},{5,4},{6,7},{7,6},{8,9},{9,8},{10,11... | collective-permute-start | bytes 1376264 | tf_op jit(solution)/shard_map/ppermute | solution.py:90
  16.9 11.0 %collective-permute-start.5 = (bf16[64,3584]{1,0:T(8,128)(2,1)S(1)}, bf16[64,3584]{1,0:T(8,128)(2,1)S(1)}, u32[]{:S(2)}, u32[]{:S(2)}) collective-permute-start(bf16[64,3584]{1,0:T(8,128)(2,1)S(1)} %collective-permute-done.3.refs_1_.refs_3_), channel_id=1, source_target_pairs={{0,2},{1,15},{2,4},{3,1},{4,6},{5,3},{6,8},{7,5},{8,10},{9,7},{10,... | collective-permute-start | bytes 1376264 | tf_op jit(solution)/shard_map/ppermute | solution.py:94
  19.1 5.9 %collective-permute-start.6 = (bf16[64,3584]{1,0:T(8,128)(2,1)S(1)}, bf16[64,3584]{1,0:T(8,128)(2,1)S(1)}, u32[]{:S(2)}, u32[]{:S(2)}) collective-permute-start(bf16[64,3584]{1,0:T(8,128)(2,1)S(1)} %collective-permute-done.refs_0_.refs_2_), channel_id=1, source_target_pairs={{0,1},{1,0},{2,3},{3,2},{4,5},{5,4},{6,7},{7,6},{8,9},{9,8},{10,11... | collective-permute-start | bytes 1376264 | tf_op jit(solution)/shard_map/ppermute | solution.py:90
  22.7 9.8 %collective-permute-start.4 = (bf16[64,3584]{1,0:T(8,128)(2,1)S(1)}, bf16[64,3584]{1,0:T(8,128)(2,1)S(1)}, u32[]{:S(2)}, u32[]{:S(2)}) collective-permute-start(bf16[64,3584]{1,0:T(8,128)(2,1)S(1)} %collective-permute-done.2.refs_6_.refs_0_), channel_id=1, source_target_pairs={{0,2},{1,15},{2,4},{3,1},{4,6},{5,3},{6,8},{7,5},{8,10},{9,7},{10,... | collective-permute-start | bytes 1376264 | tf_op jit(solution)/shard_map/ppermute | solution.py:94
  25.1 11.5 %copy-start.8 = (bf16[512,3584]{1,0:T(8,128)(2,1)S(1)}, bf16[512,3584]{1,0:T(8,128)(2,1)}, u32[]{:S(2)}) copy-start(bf16[512,3584]{1,0:T(8,128)(2,1)} %refs_11_.1) | copy-start | bytes 11010052
  27.9 6.9 %collective-permute-start.10 = (bf16[64,3584]{1,0:T(8,128)(2,1)S(1)}, bf16[64,3584]{1,0:T(8,128)(2,1)S(1)}, u32[]{:S(2)}, u32[]{:S(2)}) collective-permute-start(bf16[64,3584]{1,0:T(8,128)(2,1)S(1)} %collective-permute-done.5.refs_7_.refs_1_), channel_id=1, source_target_pairs={{0,1},{1,0},{2,3},{3,2},{4,5},{5,4},{6,7},{7,6},{8,9},{9,8},{10,11... | collective-permute-start | bytes 1376264 | tf_op jit(solution)/shard_map/ppermute | solution.py:90
  28.0 17.4 %collective-permute-start.8 = (bf16[64,3584]{1,0:T(8,128)(2,1)S(1)}, bf16[64,3584]{1,0:T(8,128)(2,1)S(1)}, u32[]{:S(2)}, u32[]{:S(2)}) collective-permute-start(bf16[64,3584]{1,0:T(8,128)(2,1)S(1)} %collective-permute-done.5.refs_7_.refs_1_), channel_id=1, source_target_pairs={{0,2},{1,15},{2,4},{3,1},{4,6},{5,3},{6,8},{7,5},{8,10},{9,7},{10,... | collective-permute-start | bytes 1376264 | tf_op jit(solution)/shard_map/ppermute | solution.py:94
  32.5 13.5 %collective-permute-start.13 = (bf16[64,3584]{1,0:T(8,128)(2,1)S(1)}, bf16[64,3584]{1,0:T(8,128)(2,1)S(1)}, u32[]{:S(2)}, u32[]{:S(2)}) collective-permute-start(bf16[64,3584]{1,0:T(8,128)(2,1)S(1)} %collective-permute-done.4.refs_0_), channel_id=1, source_target_pairs={{0,2},{1,15},{2,4},{3,1},{4,6},{5,3},{6,8},{7,5},{8,10},{9,7},{10,... | collective-permute-start | bytes 1376264 | tf_op jit(solution)/shard_map/ppermute | solution.py:94
  34.8 1.8 %collective-permute-start.9 = (bf16[64,3584]{1,0:T(8,128)(2,1)S(1)}, bf16[64,3584]{1,0:T(8,128)(2,1)S(1)}, u32[]{:S(2)}, u32[]{:S(2)}) collective-permute-start(bf16[64,3584]{1,0:T(8,128)(2,1)S(1)} %collective-permute-done.2.refs_6_.refs_0_), channel_id=1, source_target_pairs={{0,1},{1,0},{2,3},{3,2},{4,5},{5,4},{6,7},{7,6},{8,9},{9,8},{10,11... | collective-permute-start | bytes 1376264 | tf_op jit(solution)/shard_map/ppermute | solution.py:90
  45.4 24.1 %copy-start.5 = (bf16[512,3584]{1,0:T(8,128)(2,1)}, bf16[512,3584]{1,0:T(8,128)(2,1)S(1)}, u32[]{:S(2)}) copy-start(bf16[512,3584]{1,0:T(8,128)(2,1)S(1)} %get-tuple-element.56.merged) | copy-start | bytes 11010052
  45.4 1.9 %collective-permute-start.11 = (bf16[64,3584]{1,0:T(8,128)(2,1)S(1)}, bf16[64,3584]{1,0:T(8,128)(2,1)S(1)}, u32[]{:S(2)}, u32[]{:S(2)}) collective-permute-start(bf16[64,3584]{1,0:T(8,128)(2,1)S(1)} %collective-permute-done.4.refs_0_), channel_id=1, source_target_pairs={{0,1},{1,0},{2,3},{3,2},{4,5},{5,4},{6,7},{7,6},{8,9},{9,8},{10,11... | collective-permute-start | bytes 1376264 | tf_op jit(solution)/shard_map/ppermute | solution.py:90
  45.6 2.3 %collective-permute-start.12 = (bf16[64,3584]{1,0:T(8,128)(2,1)S(1)}, bf16[64,3584]{1,0:T(8,128)(2,1)S(1)}, u32[]{:S(2)}, u32[]{:S(2)}) collective-permute-start(bf16[64,3584]{1,0:T(8,128)(2,1)S(1)} %collective-permute-done.8.refs_1_), channel_id=1, source_target_pairs={{0,1},{1,0},{2,3},{3,2},{4,5},{5,4},{6,7},{7,6},{8,9},{9,8},{10,11... | collective-permute-start | bytes 1376264 | tf_op jit(solution)/shard_map/ppermute | solution.py:90
  46.0 3.6 %collective-permute-start.14 = (bf16[64,3584]{1,0:T(8,128)(2,1)S(1)}, bf16[64,3584]{1,0:T(8,128)(2,1)S(1)}, u32[]{:S(2)}, u32[]{:S(2)}) collective-permute-start(bf16[64,3584]{1,0:T(8,128)(2,1)S(1)} %collective-permute-done.13.refs_0_), channel_id=1, source_target_pairs={{0,1},{1,0},{2,3},{3,2},{4,5},{5,4},{6,7},{7,6},{8,9},{9,8},{10,11... | collective-permute-start | bytes 1376264 | tf_op jit(solution)/shard_map/ppermute | solution.py:90
  49.5 19.9 %copy-start.6 = (bf16[256,3584]{1,0:T(8,128)(2,1)}, bf16[256,3584]{1,0:T(8,128)(2,1)S(1)}, u32[]{:S(2)}) copy-start(bf16[256,3584]{1,0:T(8,128)(2,1)S(1)} %get-tuple-element.53.refs_0_.last_a) | copy-start | bytes 5505028
  50.8 18.6 %copy-start.7 = (bf16[128,3584]{1,0:T(8,128)(2,1)}, bf16[128,3584]{1,0:T(8,128)(2,1)S(1)}, u32[]{:S(2)}) copy-start(bf16[128,3584]{1,0:T(8,128)(2,1)S(1)} %get-tuple-element.54.refs_1_.last_b) | copy-start | bytes 2752516
  50.8 7.9 %collective-permute-start.17 = (f32[32,512]{1,0:T(8,128)S(1)}, f32[32,512]{1,0:T(8,128)S(1)}, u32[]{:S(2)}, u32[]{:S(2)}) collective-permute-start(f32[32,512]{1,0:T(8,128)S(1)} %get-tuple-element.51), channel_id=1, source_target_pairs={{0,192},{1,49},{2,194},{3,51},{4,196},{5,53},{6,198},{7,55},{8,200... | collective-permute-start | bytes 196616 | tf_op jit(solution)/shard_map/ppermute | solution.py:110
  53.7 6.2 %collective-permute-start.16 = (f32[32,512]{1,0:T(8,128)S(1)}, f32[32,512]{1,0:T(8,128)S(1)}, u32[]{:S(2)}, u32[]{:S(2)}) collective-permute-start(f32[32,512]{1,0:T(8,128)S(1)} %get-tuple-element.51), channel_id=1, source_target_pairs={{0,64},{1,17},{2,66},{3,19},{4,68},{5,21},{6,70},{7,23},{8,72},{9,... | collective-permute-start | bytes 196616 | tf_op jit(solution)/shard_map/ppermute | solution.py:110
  53.7 6.2 %collective-permute-start.15 = (f32[32,512]{1,0:T(8,128)S(1)}, f32[32,512]{1,0:T(8,128)S(1)}, u32[]{:S(2)}, u32[]{:S(2)}) collective-permute-start(f32[32,512]{1,0:T(8,128)S(1)} %get-tuple-element.51), channel_id=1, source_target_pairs={{0,128},{1,33},{2,130},{3,35},{4,132},{5,37},{6,134},{7,39},{8,136... | collective-permute-start | bytes 196616 | tf_op jit(solution)/shard_map/ppermute | solution.py:110
  59.9 8.6 %collective-permute-start.20 = (f32[32,512]{1,0:T(8,128)S(1)}, f32[32,512]{1,0:T(8,128)S(1)}, u32[]{:S(2)}, u32[]{:S(2)}) collective-permute-start(f32[32,512]{1,0:T(8,128)S(1)} %add_add_fusion.l0), channel_id=1, source_target_pairs={{0,48},{1,193},{2,50},{3,195},{4,52},{5,197},{6,54},{7,199},{8,56}... | collective-permute-start | bytes 196616 | tf_op jit(solution)/shard_map/ppermute | solution.py:110
  63.0 5.8 %collective-permute-start.19 = (f32[32,512]{1,0:T(8,128)S(1)}, f32[32,512]{1,0:T(8,128)S(1)}, u32[]{:S(2)}, u32[]{:S(2)}) collective-permute-start(f32[32,512]{1,0:T(8,128)S(1)} %add_add_fusion.l0), channel_id=1, source_target_pairs={{0,32},{1,129},{2,34},{3,131},{4,36},{5,133},{6,38},{7,135},{8,40}... | collective-permute-start | bytes 196616 | tf_op jit(solution)/shard_map/ppermute | solution.py:110
  63.6 5.8 %collective-permute-start.18 = (f32[32,512]{1,0:T(8,128)S(1)}, f32[32,512]{1,0:T(8,128)S(1)}, u32[]{:S(2)}, u32[]{:S(2)}) collective-permute-start(f32[32,512]{1,0:T(8,128)S(1)} %add_add_fusion.l0), channel_id=1, source_target_pairs={{0,16},{1,65},{2,18},{3,67},{4,20},{5,69},{6,22},{7,71},{8,24},{9,... | collective-permute-start | bytes 196616 | tf_op jit(solution)/shard_map/ppermute | solution.py:110
  74.5 13.2 %all-to-all-start = ((bf16[16,2,3584]{2,1,0:T(2,128)(2,1)}), bf16[16,2,3584]{2,1,0:T(2,128)(2,1)S(1)}, u32[]{:S(2)}, u32[]{:S(2)}) async-start(bf16[16,2,3584]{2,1,0:T(2,128)(2,1)} %get-tuple-element.58), calls=%async_computation | async-start | bytes 458752 | tf_op jit(solution)/shard_map/all_to_all | solution.py:503
  88.6 12.0 %all-to-all-start.1 = ((bf16[16,2,3584]{2,1,0:T(2,128)(2,1)}), bf16[16,2,3584]{2,1,0:T(2,128)(2,1)S(1)}, u32[]{:S(2)}, u32[]{:S(2)}) async-start(bf16[16,2,3584]{2,1,0:T(2,128)(2,1)} %sum_of_ranks.1), calls=%async_computation.1 | async-start | bytes 458752 | tf_op jit(solution)/shard_map/all_to_all | solution.py:506
  92.3 8.3 %copy-start.10 = (f32[32,512]{1,0:T(8,128)S(1)}, f32[32,512]{1,0:T(8,128)}, u32[]{:S(2)}) copy-start(f32[32,512]{1,0:T(8,128)} %get-tuple-element.32.factor) | copy-start | bytes 196612

commit v6 on v5

--- a/solution.py
+++ b/solution.py
@@ -483,7 +483,7 @@
     grad_pre = pre_of(1, [a1, b1, xa1, xb1], grad_pre)
     b3 = along_z(after(b2, a2, grad_pre))
     xa2, xb2 = other_core(after(a2, b2, grad_pre)), other_core(after(b2, a2, grad_pre))
-    a4 = along_z(after(a3, b2))
+    a4 = along_z(after(a3, b2, xa2))
     grad_pre = pre_of(2, [a2, b2, xa2, xb2], grad_pre)
     xa2, xb2, _ = lax.optimization_barrier((xa2, xb2, a3))
     early = [a0, b0, a1, b1, xa1, xb1, a2, b2, xa2, xb2]

time: 106 us -> 104 us (0.981)
  waiting for transfers between devices: 22.3 us -> 19.3 us
  starting transfers between devices: 33.5 us -> 34.7 us
    ppermute x8, waiting for transfers between devices: 3.44 us -> 1.69 us  [other_core(): return lax.ppermute(value, 'tensor', [(i, i ^ 1) for i in range(2 * NZ)])]
    ppermute x7, waiting for transfers between devices: 7.92 us -> 6.72 us  [along_z(): lax.ppermute(value, 'tensor', [(i, (i + 2 - 4 * (i % 2)) % (2 * NZ)) for...]
    ppermute x8, starting transfers between devices: 1.07 us -> 2.14 us  [other_core(): return lax.ppermute(value, 'tensor', [(i, i ^ 1) for i in range(2 * NZ)])]
  transfers between devices with their start and end apart: 23 -> 23, of which waited for: 11 -> 10; matrix products, arithmetic and copies ran while one was open for 0% -> 0% of each run, Pallas kernels for 31% -> 32%
where the time goes in v6:
time: 104 us; the launch traced here: 103 us
  Pallas kernels  43.8 us (42%)
  starting transfers between devices  34.7 us (33%)
  waiting for transfers between devices  19.3 us (19%)
  local copies, waits for them, and re-layouts  3.73 us (4%)
  between operations  1.08 us (1%)
    ppermute x7, starting transfers between devices, along_z(): lax.ppermute(value, 'tensor', [(i, (i + 2 - 4 * (i % 2)) % (2 * NZ)) for...  14.1 us
    pallas_call x4, Pallas kernels, pre_call(): pl.pallas_call(functools.partial(pre_kernel, s), grid_spec=pltpu.Prefetch...  12.1 us
    ppermute x6, starting transfers between devices, sum_over_ring(): lax.ppermute(value, ('dp', 'tensor'), list(pairs(k)))  9.82 us
    pallas_call x1, Pallas kernels, main_call(): pl.pallas_call(main_kernel, grid_spec=pltpu.PrefetchScalarGridSpec(num_sc...  8.81 us
    pallas_call x2, Pallas kernels, merge_call(): pl.pallas_call(merge_kernel, grid=(HALF // WIDE,), in_specs=[pl.BlockSpec...  7.7 us
    ppermute x7, waiting for transfers between devices, along_z(): lax.ppermute(value, 'tensor', [(i, (i + 2 - 4 * (i % 2)) % (2 * NZ)) for...  6.72 us
    pallas_call x1, Pallas kernels, right_call(): pl.pallas_call(right_kernel, in_specs=[WHOLE] * 8, out_specs=[WHOLE] * 2,...  5.01 us
    all_to_all x1, starting transfers between devices, on_device(): parts = lax.all_to_all(right, 'dp', 0, 0, tiled=True)  4.97 us
  transfers between devices with their start and end apart: 23, of which 10 were waited for; matrix products, arithmetic and copies ran while one was open for 0% of the time, Pallas kernels for 32%

profile of v6, /device:TPU:96, one launch (start us, length us, event | category | flops | bytes accessed | tf_op | source)
XLA Modules:
  0.0 102.9 jit_solution(8814985915892763346)
XLA Ops:
  0.6 0.1 collective-permute-start.1
  0.7 3.2 %collective-permute-start = (bf16[64,3584]{1,0:T(8,128)(2,1)}, bf16[64,3584]{1,0:T(8,128)(2,1)S(1)}, u32[]{:S(2)}, u32[]{:S(2)}) collective-permute-start(bf16[64,3584]{1,0:T(8,128)(2,1)} %refs_0_.3), channel_id=1, source_target_pairs={{0,2},{1,15},{2,4},{3,1},{4,6},{5,3},{6,8},{7,5},{8,10},{9,7},{10,... | collective-permute-start | bytes 1376264 | tf_op jit(solution)/shard_map/ppermute | solution.py:94
  3.9 0.1 pad_add_fusion.place
  4.0 1.6 %copy-done = bf16[2,1024,512]{2,1,0:T(8,128)(2,1)S(1)} copy-done((bf16[2,1024,512]{2,1,0:T(8,128)(2,1)S(1)}, bf16[2,1024,512]{2,1,0:T(8,128)(2,1)}, u32[]{:S(2)}) %copy-start) | copy-done | bytes 2097176
  5.6 2.7 %hidden.1.refs_10_.refs_4_.refs_2_.hidden_t = bf16[512,1024]{1,0:T(8,128)(2,1)S(1)} custom-call(s32[2]{0:T(128)S(1)} %pad_add_fusion.place, bf16[2,1024,512]{2,1,0:T(8,128)(2,1)S(1)} %copy-done), custom_call_target="tpu_custom_call" | custom-call | flops 1000000 | bytes 100000 | tf_op jit(solution)/shard_map/hidden/pallas_call | solution.py:155
  8.3 1.1 %collective-permute-start.3 = (bf16[64,3584]{1,0:T(8,128)(2,1)S(1)}, bf16[64,3584]{1,0:T(8,128)(2,1)S(1)}, u32[]{:S(2)}, u32[]{:S(2)}) collective-permute-start(bf16[64,3584]{1,0:T(8,128)(2,1)S(1)} %collective-permute-done.1.refs_1_), channel_id=1, source_target_pairs={{0,2},{1,15},{2,4},{3,1},{4,6},{5,3},{6,8},{7,5},{8,10},{9,7},{10,... | collective-permute-start | bytes 1376264 | tf_op jit(solution)/shard_map/ppermute | solution.py:94
  9.4 2.0 %copy-done.2 = bf16[512,3584]{1,0:T(8,128)(2,1)S(1)} copy-done((bf16[512,3584]{1,0:T(8,128)(2,1)S(1)}, bf16[512,3584]{1,0:T(8,128)(2,1)}, u32[]{:S(2)}) %copy-start.2) | copy-done | bytes 3670040
  11.5 2.7 %grad_pre.4.refs_7_ = bf16[2,1024,512]{2,1,0:T(8,128)(2,1)} custom-call(s32[2]{0:T(128)S(1)} %pad_add_fusion.place, bf16[64,3584]{1,0:T(8,128)(2,1)S(1)} %copy-done.9, bf16[64,3584]{1,0:T(8,128)(2,1)S(1)} %collective-permute-done.1.refs_1_, bf16[2,1024,512]{2,1,0:T(8,128)(2,1)S(1)} %copy-done.1, bf16[512,3584]{1,0:T(8,128)(2,1)S(1)} %copy-done.2), custom_call_target="tpu_custom_call" | custom-call | flops 1000000 | bytes 100000 | tf_op jit(solution)/shard_map/grad_pre/pallas_call | solution.py:445
  14.2 1.1 %collective-permute-start.2 = (bf16[64,3584]{1,0:T(8,128)(2,1)S(1)}, bf16[64,3584]{1,0:T(8,128)(2,1)S(1)}, u32[]{:S(2)}, u32[]{:S(2)}) collective-permute-start(bf16[64,3584]{1,0:T(8,128)(2,1)S(1)} %collective-permute-done.refs_0_.refs_2_), channel_id=1, source_target_pairs={{0,2},{1,15},{2,4},{3,1},{4,6},{5,3},{6,8},{7,5},{8,10},{9,7},{10,... | collective-permute-start | bytes 1376264 | tf_op jit(solution)/shard_map/ppermute | solution.py:94
  15.2 1.6 %collective-permute-done.3.refs_1_.refs_3_ = bf16[64,3584]{1,0:T(8,128)(2,1)S(1)} collective-permute-done((bf16[64,3584]{1,0:T(8,128)(2,1)S(1)}, bf16[64,3584]{1,0:T(8,128)(2,1)S(1)}, u32[]{:S(2)}, u32[]{:S(2)}) %collective-permute-start.3) | collective-permute-done | bytes 458784 | tf_op jit(solution)/shard_map/ppermute | solution.py:94
  16.9 0.5 collective-permute-start.6
  17.4 2.2 %collective-permute-start.5 = (bf16[64,3584]{1,0:T(8,128)(2,1)S(1)}, bf16[64,3584]{1,0:T(8,128)(2,1)S(1)}, u32[]{:S(2)}, u32[]{:S(2)}) collective-permute-start(bf16[64,3584]{1,0:T(8,128)(2,1)S(1)} %collective-permute-done.3.refs_1_.refs_3_), channel_id=1, source_target_pairs={{0,2},{1,15},{2,4},{3,1},{4,6},{5,3},{6,8},{7,5},{8,10},{9,7},{10,... | collective-permute-start | bytes 1376264 | tf_op jit(solution)/shard_map/ppermute | solution.py:94
  19.6 3.1 %collective-permute-done.2.refs_6_.refs_0_ = bf16[64,3584]{1,0:T(8,128)(2,1)S(1)} collective-permute-done((bf16[64,3584]{1,0:T(8,128)(2,1)S(1)}, bf16[64,3584]{1,0:T(8,128)(2,1)S(1)}, u32[]{:S(2)}, u32[]{:S(2)}) %collective-permute-start.2) | collective-permute-done | bytes 458784 | tf_op jit(solution)/shard_map/ppermute | solution.py:94
  22.7 2.2 %collective-permute-start.4 = (bf16[64,3584]{1,0:T(8,128)(2,1)S(1)}, bf16[64,3584]{1,0:T(8,128)(2,1)S(1)}, u32[]{:S(2)}, u32[]{:S(2)}) collective-permute-start(bf16[64,3584]{1,0:T(8,128)(2,1)S(1)} %collective-permute-done.2.refs_6_.refs_0_), channel_id=1, source_target_pairs={{0,2},{1,15},{2,4},{3,1},{4,6},{5,3},{6,8},{7,5},{8,10},{9,7},{10,... | collective-permute-start | bytes 1376264 | tf_op jit(solution)/shard_map/ppermute | solution.py:94
  25.0 2.8 %grad_pre.5.refs_7_ = bf16[2,1024,512]{2,1,0:T(8,128)(2,1)} custom-call(s32[2]{0:T(128)S(1)} %pad_add_fusion.place, bf16[64,3584]{1,0:T(8,128)(2,1)S(1)} %collective-permute-done.refs_0_.refs_2_, bf16[64,3584]{1,0:T(8,128)(2,1)S(1)} %collective-permute-done.3.refs_1_.refs_3_, ...), custom_call_target="tpu_custom_call", output_to_operand_aliasing={{}: (8, {})} | custom-call | flops 1000000 | bytes 100000 | tf_op jit(solution)/shard_map/grad_pre/pallas_call | solution.py:445
  27.8 0.1 collective-permute-start.9
  27.9 0.1 reduce-precision_convert_fusion.1
  28.0 0.6 collective-permute-start.10
  28.5 2.0 %collective-permute-start.8 = (bf16[64,3584]{1,0:T(8,128)(2,1)S(1)}, bf16[64,3584]{1,0:T(8,128)(2,1)S(1)}, u32[]{:S(2)}, u32[]{:S(2)}) collective-permute-start(bf16[64,3584]{1,0:T(8,128)(2,1)S(1)} %collective-permute-done.5.refs_7_.refs_1_), channel_id=1, source_target_pairs={{0,2},{1,15},{2,4},{3,1},{4,6},{5,3},{6,8},{7,5},{8,10},{9,7},{10,... | collective-permute-start | bytes 1376264 | tf_op jit(solution)/shard_map/ppermute | solution.py:94
  30.5 2.0 %collective-permute-done.4.refs_0_ = bf16[64,3584]{1,0:T(8,128)(2,1)S(1)} collective-permute-done((bf16[64,3584]{1,0:T(8,128)(2,1)S(1)}, bf16[64,3584]{1,0:T(8,128)(2,1)S(1)}, u32[]{:S(2)}, u32[]{:S(2)}) %collective-permute-start.4) | collective-permute-done | bytes 458784 | tf_op jit(solution)/shard_map/ppermute | solution.py:94
  32.5 2.2 %collective-permute-start.13 = (bf16[64,3584]{1,0:T(8,128)(2,1)S(1)}, bf16[64,3584]{1,0:T(8,128)(2,1)S(1)}, u32[]{:S(2)}, u32[]{:S(2)}) collective-permute-start(bf16[64,3584]{1,0:T(8,128)(2,1)S(1)} %collective-permute-done.4.refs_0_), channel_id=1, source_target_pairs={{0,2},{1,15},{2,4},{3,1},{4,6},{5,3},{6,8},{7,5},{8,10},{9,7},{10,... | collective-permute-start | bytes 1376264 | tf_op jit(solution)/shard_map/ppermute | solution.py:94
  34.8 8.8 %weight_grad.1 = (bf16[512,3584]{1,0:T(8,128)(2,1)S(1)}, f32[32,512]{1,0:T(8,128)S(1)}) custom-call(s32[2]{0:T(128)S(1)} %pad_add_fusion.place, bf16[64,3584]{1,0:T(8,128)(2,1)S(1)} %copy-done.9, bf16[64,3584]{1,0:T(8,128)(2,1)S(1)} %collective-permute-done.1.refs_1_, bf16[64,3584]{1,0:T(8,128)(2,1)S(1)} %collective-permute-done.refs_0_.refs_2_, ...), custom_call_target="tpu_custom_call" | custom-call | flops 1000000 | bytes 100000 | tf_op jit(solution)/shard_map/weight_grad/pallas_call | solution.py:199
  43.7 0.1 collective-permute-start.11
  43.8 0.5 collective-permute-start.12
  44.3 0.3 collective-permute-start.14
  44.6 1.0 collective-permute-done.11.refs_2_
  45.6 0.7 collective-permute-done.12.refs_3_
  46.2 1.6 %left_of_step.2 = (f32[32,512]{1,0:T(8,128)S(1)}, bf16[256,3584]{1,0:T(8,128)(2,1)S(1)}) custom-call(s32[2]{0:T(128)S(1)} %pad_add_fusion.place, bf16[64,3584]{1,0:T(8,128)(2,1)S(1)} %collective-permute-done.4.refs_0_, bf16[64,3584]{1,0:T(8,128)(2,1)S(1)} %collective-permute-done.8.refs_1_, bf16[64,3584]{1,0:T(8,128)(2,1)S(1)} %collective-permute-done.11.refs_2_, ...), custom_call_target="tpu_custom_call" | custom-call | flops 1000000 | bytes 100000 | tf_op jit(solution)/shard_map/left_of_step/pallas_call | solution.py:237
  47.9 1.2 %left_of_step.3 = (f32[32,512]{1,0:T(8,128)S(1)}, bf16[128,3584]{1,0:T(8,128)(2,1)S(1)}) custom-call(s32[2]{0:T(128)S(1)} %pad_add_fusion.place, bf16[64,3584]{1,0:T(8,128)(2,1)S(1)} %collective-permute-done.13.refs_0_, bf16[64,3584]{1,0:T(8,128)(2,1)S(1)} %collective-permute-done.14.refs_1_, bf16[512,1024]{1,0:T(8,128)(2,1)S(1)} %hidden.1.refs_10_.refs_4_.refs_2_.hidden_t, ...), custom_call_target="tpu_custom_call" | custom-call | flops 1000000 | bytes 100000 | tf_op jit(solution)/shard_map/left_of_step/pallas_call | solution.py:237
  49.1 2.8 %collective-permute-start.17 = (f32[32,512]{1,0:T(8,128)S(1)}, f32[32,512]{1,0:T(8,128)S(1)}, u32[]{:S(2)}, u32[]{:S(2)}) collective-permute-start(f32[32,512]{1,0:T(8,128)S(1)} %get-tuple-element.51), channel_id=1, source_target_pairs={{0,192},{1,49},{2,194},{3,51},{4,196},{5,53},{6,198},{7,55},{8,200... | collective-permute-start | bytes 196616 | tf_op jit(solution)/shard_map/ppermute | solution.py:110
  51.9 2.3 %collective-permute-start.15 = (f32[32,512]{1,0:T(8,128)S(1)}, f32[32,512]{1,0:T(8,128)S(1)}, u32[]{:S(2)}, u32[]{:S(2)}) collective-permute-start(f32[32,512]{1,0:T(8,128)S(1)} %get-tuple-element.51), channel_id=1, source_target_pairs={{0,128},{1,33},{2,130},{3,35},{4,132},{5,37},{6,134},{7,39},{8,136... | collective-permute-start | bytes 196616 | tf_op jit(solution)/shard_map/ppermute | solution.py:110
  54.2 2.8 %grad_pre.6.refs_6_ = bf16[2,1024,512]{2,1,0:T(8,128)(2,1)} custom-call(s32[2]{0:T(128)S(1)} %pad_add_fusion.place, bf16[64,3584]{1,0:T(8,128)(2,1)S(1)} %collective-permute-done.2.refs_6_.refs_0_, bf16[64,3584]{1,0:T(8,128)(2,1)S(1)} %collective-permute-done.5.refs_7_.refs_1_, ...), custom_call_target="tpu_custom_call", output_to_operand_aliasing={{}: (8, {})} | custom-call | flops 1000000 | bytes 100000 | tf_op jit(solution)/shard_map/grad_pre/pallas_call | solution.py:445
  57.0 1.1 %collective-permute-done.16 = f32[32,512]{1,0:T(8,128)S(1)} collective-permute-done((f32[32,512]{1,0:T(8,128)S(1)}, f32[32,512]{1,0:T(8,128)S(1)}, u32[]{:S(2)}, u32[]{:S(2)}) %collective-permute-start.16) | collective-permute-done | bytes 65568 | tf_op jit(solution)/shard_map/ppermute | solution.py:110
  58.2 3.1 %collective-permute-start.20 = (f32[32,512]{1,0:T(8,128)S(1)}, f32[32,512]{1,0:T(8,128)S(1)}, u32[]{:S(2)}, u32[]{:S(2)}) collective-permute-start(f32[32,512]{1,0:T(8,128)S(1)} %add_add_fusion.l0), channel_id=1, source_target_pairs={{0,48},{1,193},{2,50},{3,195},{4,52},{5,197},{6,54},{7,199},{8,56}... | collective-permute-start | bytes 196616 | tf_op jit(solution)/shard_map/ppermute | solution.py:110
  61.2 0.6 collective-permute-start.19
  61.9 1.0 collective-permute-start.18
  62.8 3.9 %grad_pre.7 = bf16[2,1024,512]{2,1,0:T(8,128)(2,1)} custom-call(s32[2]{0:T(128)S(1)} %pad_add_fusion.place, bf16[256,3584]{1,0:T(8,128)(2,1)S(1)} %get-tuple-element.53.refs_0_.last_a, bf16[128,3584]{1,0:T(8,128)(2,1)S(1)} %get-tuple-element.54.refs_1_.last_b, bf16[2,1024,512]{2,1,0:T(8,128)(2,1)S(1)} %copy-done.1, ...), custom_call_target="tpu_custom_call", output_to_operand_aliasing={{}: (7, {})} | custom-call | flops 1000000 | bytes 100000 | tf_op jit(solution)/shard_map/grad_pre/pallas_call | solution.py:445
  66.7 0.3 collective-permute-done.19.l2
  67.1 0.7 collective-permute-done.18.l1
  67.7 5.0 %right_factor.1 = (f32[32,512]{1,0:T(8,128)}, bf16[16,2,3584]{2,1,0:T(2,128)(2,1)}) custom-call(f32[32,512]{1,0:T(8,128)S(1)} %add_add_fusion.l0, f32[32,512]{1,0:T(8,128)S(1)} %collective-permute-done.18.l1, f32[32,512]{1,0:T(8,128)S(1)} %collective-permute-done.19.l2, f32[32,512]{1,0:T(8,128)S(1)} %collective-permute-done.20.l3, ...), custom_call_target="tpu_custom_call" | custom-call | flops 100000000 | bytes 8000000 | tf_op jit(solution)/shard_map/right_factor/pallas_call | solution.py:278
  72.7 5.0 %all-to-all-start = ((bf16[16,2,3584]{2,1,0:T(2,128)(2,1)}), bf16[16,2,3584]{2,1,0:T(2,128)(2,1)S(1)}, u32[]{:S(2)}, u32[]{:S(2)}) async-start(bf16[16,2,3584]{2,1,0:T(2,128)(2,1)} %get-tuple-element.58), calls=%async_computation | async-start | bytes 458752 | tf_op jit(solution)/shard_map/all_to_all | solution.py:503
  77.7 4.2 %weight_grad_rest.2.lower = bf16[512,1792]{1,0:T(8,128)(2,1)} custom-call(bf16[512,1024]{1,0:T(8,128)(2,1)} %copy-done.4, bf16[256,3584]{1,0:T(8,128)(2,1)} %copy-done.6, bf16[128,3584]{1,0:T(8,128)(2,1)} %copy-done.7, bf16[512,3584]{1,0:T(8,128)(2,1)} %copy-done.5), custom_call_target="tpu_custom_call" | custom-call | flops 704643072 | bytes 6000000 | tf_op jit(solution)/shard_map/weight_grad_rest/pallas_call | solution.py:324
  82.0 4.0 %all-to-all-done.parts = bf16[16,2,3584]{2,1,0:T(2,128)(2,1)S(1)} async-done(((bf16[16,2,3584]{2,1,0:T(2,128)(2,1)}), bf16[16,2,3584]{2,1,0:T(2,128)(2,1)S(1)}, u32[]{:S(2)}, u32[]{:S(2)}) %all-to-all-start) | async-done | bytes 229408 | tf_op jit(solution)/shard_map/all_to_all | solution.py:503
  86.0 0.9 sum_of_ranks.1
  86.9 3.7 %all-to-all-start.1 = ((bf16[16,2,3584]{2,1,0:T(2,128)(2,1)}), bf16[16,2,3584]{2,1,0:T(2,128)(2,1)S(1)}, u32[]{:S(2)}, u32[]{:S(2)}) async-start(bf16[16,2,3584]{2,1,0:T(2,128)(2,1)} %sum_of_ranks.1), calls=%async_computation.1 | async-start | bytes 458752 | tf_op jit(solution)/shard_map/all_to_all | solution.py:506
  90.6 3.5 %weight_grad_rest.3.upper = bf16[512,1792]{1,0:T(8,128)(2,1)S(1)} custom-call(bf16[512,1024]{1,0:T(8,128)(2,1)} %copy-done.4, bf16[256,3584]{1,0:T(8,128)(2,1)} %copy-done.6, bf16[128,3584]{1,0:T(8,128)(2,1)} %copy-done.7, bf16[512,3584]{1,0:T(8,128)(2,1)} %copy-done.5), custom_call_target="tpu_custom_call" | custom-call | flops 704643072 | bytes 6000000 | tf_op jit(solution)/shard_map/weight_grad_rest/pallas_call | solution.py:324
  94.1 4.8 %all-to-all-done.1.summed = bf16[16,2,3584]{2,1,0:T(2,128)(2,1)S(1)} async-done(((bf16[16,2,3584]{2,1,0:T(2,128)(2,1)}), bf16[16,2,3584]{2,1,0:T(2,128)(2,1)S(1)}, u32[]{:S(2)}, u32[]{:S(2)}) %all-to-all-start.1) | async-done | bytes 229408 | tf_op jit(solution)/shard_map/all_to_all | solution.py:506
  98.9 3.9 %new_error.1 = (bf16[512,3584]{1,0:T(8,128)(2,1)}, f32[32,3584]{1,0:T(8,128)}) custom-call(f32[32,512]{1,0:T(8,128)S(1)} %copy-done.10, bf16[512,1792]{1,0:T(8,128)(2,1)} %weight_grad_rest.2.lower, bf16[512,1792]{1,0:T(8,128)(2,1)S(1)} %weight_grad_rest.3.upper, bf16[16,2,3584]{2,1,0:T(2,128)(2,1)S(1)} %all-to-all-done.1.summed), custom_call_target="tpu_custom_call" | custom-call | flops 234881024 | bytes 8000000 | tf_op jit(solution)/shard_map/new_error/pallas_call | solution.py:373
  (39 shorter events, 0.2 us)
Async XLA Ops:
  0.6 7.7 %collective-permute-start.1 = (bf16[64,3584]{1,0:T(8,128)(2,1)}, bf16[64,3584]{1,0:T(8,128)(2,1)S(1)}, u32[]{:S(2)}, u32[]{:S(2)}) collective-permute-start(bf16[64,3584]{1,0:T(8,128)(2,1)} %refs_0_.3), channel_id=1, source_target_pairs={{0,1},{1,0},{2,3},{3,2},{4,5},{5,4},{6,7},{7,6},{8,9},{9,8},{10,11... | collective-permute-start | bytes 1376264 | tf_op jit(solution)/shard_map/ppermute | solution.py:90
  0.7 13.4 %collective-permute-start = (bf16[64,3584]{1,0:T(8,128)(2,1)}, bf16[64,3584]{1,0:T(8,128)(2,1)S(1)}, u32[]{:S(2)}, u32[]{:S(2)}) collective-permute-start(bf16[64,3584]{1,0:T(8,128)(2,1)} %refs_0_.3), channel_id=1, source_target_pairs={{0,2},{1,15},{2,4},{3,1},{4,6},{5,3},{6,8},{7,5},{8,10},{9,7},{10,... | collective-permute-start | bytes 1376264 | tf_op jit(solution)/shard_map/ppermute | solution.py:94
  4.0 1.6 %copy-start = (bf16[2,1024,512]{2,1,0:T(8,128)(2,1)S(1)}, bf16[2,1024,512]{2,1,0:T(8,128)(2,1)}, u32[]{:S(2)}) copy-start(bf16[2,1024,512]{2,1,0:T(8,128)(2,1)} %refs_4_.5) | copy-start | bytes 6291460
  5.6 3.8 %copy-start.1 = (bf16[2,1024,512]{2,1,0:T(8,128)(2,1)S(1)}, bf16[2,1024,512]{2,1,0:T(8,128)(2,1)}, u32[]{:S(2)}) copy-start(bf16[2,1024,512]{2,1,0:T(8,128)(2,1)} %refs_4_.5) | copy-start | bytes 6291460
  5.6 3.8 %copy-start.9 = (bf16[64,3584]{1,0:T(8,128)(2,1)S(1)}, bf16[64,3584]{1,0:T(8,128)(2,1)}, u32[]{:S(2)}) copy-start(bf16[64,3584]{1,0:T(8,128)(2,1)} %refs_0_.3) | copy-start | bytes 1376260
  8.3 59.4 %copy-start.4 = (bf16[512,1024]{1,0:T(8,128)(2,1)}, bf16[512,1024]{1,0:T(8,128)(2,1)S(1)}, u32[]{:S(2)}) copy-start(bf16[512,1024]{1,0:T(8,128)(2,1)S(1)} %hidden.1.refs_10_.refs_4_.refs_2_.hidden_t) | copy-start | bytes 3145732
  8.3 8.6 %collective-permute-start.3 = (bf16[64,3584]{1,0:T(8,128)(2,1)S(1)}, bf16[64,3584]{1,0:T(8,128)(2,1)S(1)}, u32[]{:S(2)}, u32[]{:S(2)}) collective-permute-start(bf16[64,3584]{1,0:T(8,128)(2,1)S(1)} %collective-permute-done.1.refs_1_), channel_id=1, source_target_pairs={{0,2},{1,15},{2,4},{3,1},{4,6},{5,3},{6,8},{7,5},{8,10},{9,7},{10,... | collective-permute-start | bytes 1376264 | tf_op jit(solution)/shard_map/ppermute | solution.py:94
  9.4 2.0 %copy-start.2 = (bf16[512,3584]{1,0:T(8,128)(2,1)S(1)}, bf16[512,3584]{1,0:T(8,128)(2,1)}, u32[]{:S(2)}) copy-start(bf16[512,3584]{1,0:T(8,128)(2,1)} %refs_5_.5) | copy-start | bytes 11010052
  11.5 13.5 %copy-start.3 = (bf16[512,3584]{1,0:T(8,128)(2,1)S(1)}, bf16[512,3584]{1,0:T(8,128)(2,1)}, u32[]{:S(2)}) copy-start(bf16[512,3584]{1,0:T(8,128)(2,1)} %refs_5_.5) | copy-start | bytes 11010052
  14.1 13.7 %copy-start.11 = (f32[32,3584]{1,0:T(8,128)S(1)}, f32[32,3584]{1,0:T(8,128)}, u32[]{:S(2)}) copy-start(f32[32,3584]{1,0:T(8,128)} %param.9) | copy-start | bytes 1376260
  14.2 8.6 %collective-permute-start.2 = (bf16[64,3584]{1,0:T(8,128)(2,1)S(1)}, bf16[64,3584]{1,0:T(8,128)(2,1)S(1)}, u32[]{:S(2)}, u32[]{:S(2)}) collective-permute-start(bf16[64,3584]{1,0:T(8,128)(2,1)S(1)} %collective-permute-done.refs_0_.refs_2_), channel_id=1, source_target_pairs={{0,2},{1,15},{2,4},{3,1},{4,6},{5,3},{6,8},{7,5},{8,10},{9,7},{10,... | collective-permute-start | bytes 1376264 | tf_op jit(solution)/shard_map/ppermute | solution.py:94
  16.9 8.1 %collective-permute-start.7 = (bf16[64,3584]{1,0:T(8,128)(2,1)S(1)}, bf16[64,3584]{1,0:T(8,128)(2,1)S(1)}, u32[]{:S(2)}, u32[]{:S(2)}) collective-permute-start(bf16[64,3584]{1,0:T(8,128)(2,1)S(1)} %collective-permute-done.3.refs_1_.refs_3_), channel_id=1, source_target_pairs={{0,1},{1,0},{2,3},{3,2},{4,5},{5,4},{6,7},{7,6},{8,9},{9,8},{10,11... | collective-permute-start | bytes 1376264 | tf_op jit(solution)/shard_map/ppermute | solution.py:90
  16.9 8.1 %collective-permute-start.6 = (bf16[64,3584]{1,0:T(8,128)(2,1)S(1)}, bf16[64,3584]{1,0:T(8,128)(2,1)S(1)}, u32[]{:S(2)}, u32[]{:S(2)}) collective-permute-start(bf16[64,3584]{1,0:T(8,128)(2,1)S(1)} %collective-permute-done.refs_0_.refs_2_), channel_id=1, source_target_pairs={{0,1},{1,0},{2,3},{3,2},{4,5},{5,4},{6,7},{7,6},{8,9},{9,8},{10,11... | collective-permute-start | bytes 1376264 | tf_op jit(solution)/shard_map/ppermute | solution.py:90
  17.4 10.4 %collective-permute-start.5 = (bf16[64,3584]{1,0:T(8,128)(2,1)S(1)}, bf16[64,3584]{1,0:T(8,128)(2,1)S(1)}, u32[]{:S(2)}, u32[]{:S(2)}) collective-permute-start(bf16[64,3584]{1,0:T(8,128)(2,1)S(1)} %collective-permute-done.3.refs_1_.refs_3_), channel_id=1, source_target_pairs={{0,2},{1,15},{2,4},{3,1},{4,6},{5,3},{6,8},{7,5},{8,10},{9,7},{10,... | collective-permute-start | bytes 1376264 | tf_op jit(solution)/shard_map/ppermute | solution.py:94
  22.7 9.8 %collective-permute-start.4 = (bf16[64,3584]{1,0:T(8,128)(2,1)S(1)}, bf16[64,3584]{1,0:T(8,128)(2,1)S(1)}, u32[]{:S(2)}, u32[]{:S(2)}) collective-permute-start(bf16[64,3584]{1,0:T(8,128)(2,1)S(1)} %collective-permute-done.2.refs_6_.refs_0_), channel_id=1, source_target_pairs={{0,2},{1,15},{2,4},{3,1},{4,6},{5,3},{6,8},{7,5},{8,10},{9,7},{10,... | collective-permute-start | bytes 1376264 | tf_op jit(solution)/shard_map/ppermute | solution.py:94
  24.9 9.9 %copy-start.8 = (bf16[512,3584]{1,0:T(8,128)(2,1)S(1)}, bf16[512,3584]{1,0:T(8,128)(2,1)}, u32[]{:S(2)}) copy-start(bf16[512,3584]{1,0:T(8,128)(2,1)} %refs_11_.1) | copy-start | bytes 11010052
  27.8 4.8 %collective-permute-start.9 = (bf16[64,3584]{1,0:T(8,128)(2,1)S(1)}, bf16[64,3584]{1,0:T(8,128)(2,1)S(1)}, u32[]{:S(2)}, u32[]{:S(2)}) collective-permute-start(bf16[64,3584]{1,0:T(8,128)(2,1)S(1)} %collective-permute-done.2.refs_6_.refs_0_), channel_id=1, source_target_pairs={{0,1},{1,0},{2,3},{3,2},{4,5},{5,4},{6,7},{7,6},{8,9},{9,8},{10,11... | collective-permute-start | bytes 1376264 | tf_op jit(solution)/shard_map/ppermute | solution.py:90
  28.0 6.9 %collective-permute-start.10 = (bf16[64,3584]{1,0:T(8,128)(2,1)S(1)}, bf16[64,3584]{1,0:T(8,128)(2,1)S(1)}, u32[]{:S(2)}, u32[]{:S(2)}) collective-permute-start(bf16[64,3584]{1,0:T(8,128)(2,1)S(1)} %collective-permute-done.5.refs_7_.refs_1_), channel_id=1, source_target_pairs={{0,1},{1,0},{2,3},{3,2},{4,5},{5,4},{6,7},{7,6},{8,9},{9,8},{10,11... | collective-permute-start | bytes 1376264 | tf_op jit(solution)/shard_map/ppermute | solution.py:90
  28.5 15.1 %collective-permute-start.8 = (bf16[64,3584]{1,0:T(8,128)(2,1)S(1)}, bf16[64,3584]{1,0:T(8,128)(2,1)S(1)}, u32[]{:S(2)}, u32[]{:S(2)}) collective-permute-start(bf16[64,3584]{1,0:T(8,128)(2,1)S(1)} %collective-permute-done.5.refs_7_.refs_1_), channel_id=1, source_target_pairs={{0,2},{1,15},{2,4},{3,1},{4,6},{5,3},{6,8},{7,5},{8,10},{9,7},{10,... | collective-permute-start | bytes 1376264 | tf_op jit(solution)/shard_map/ppermute | solution.py:94
  32.5 11.7 %collective-permute-start.13 = (bf16[64,3584]{1,0:T(8,128)(2,1)S(1)}, bf16[64,3584]{1,0:T(8,128)(2,1)S(1)}, u32[]{:S(2)}, u32[]{:S(2)}) collective-permute-start(bf16[64,3584]{1,0:T(8,128)(2,1)S(1)} %collective-permute-done.4.refs_0_), channel_id=1, source_target_pairs={{0,2},{1,15},{2,4},{3,1},{4,6},{5,3},{6,8},{7,5},{8,10},{9,7},{10,... | collective-permute-start | bytes 1376264 | tf_op jit(solution)/shard_map/ppermute | solution.py:94
  43.7 24.1 %copy-start.5 = (bf16[512,3584]{1,0:T(8,128)(2,1)}, bf16[512,3584]{1,0:T(8,128)(2,1)S(1)}, u32[]{:S(2)}) copy-start(bf16[512,3584]{1,0:T(8,128)(2,1)S(1)} %get-tuple-element.56.merged) | copy-start | bytes 11010052
  43.7 1.9 %collective-permute-start.11 = (bf16[64,3584]{1,0:T(8,128)(2,1)S(1)}, bf16[64,3584]{1,0:T(8,128)(2,1)S(1)}, u32[]{:S(2)}, u32[]{:S(2)}) collective-permute-start(bf16[64,3584]{1,0:T(8,128)(2,1)S(1)} %collective-permute-done.4.refs_0_), channel_id=1, source_target_pairs={{0,1},{1,0},{2,3},{3,2},{4,5},{5,4},{6,7},{7,6},{8,9},{9,8},{10,11... | collective-permute-start | bytes 1376264 | tf_op jit(solution)/shard_map/ppermute | solution.py:90
  43.8 2.5 %collective-permute-start.12 = (bf16[64,3584]{1,0:T(8,128)(2,1)S(1)}, bf16[64,3584]{1,0:T(8,128)(2,1)S(1)}, u32[]{:S(2)}, u32[]{:S(2)}) collective-permute-start(bf16[64,3584]{1,0:T(8,128)(2,1)S(1)} %collective-permute-done.8.refs_1_), channel_id=1, source_target_pairs={{0,1},{1,0},{2,3},{3,2},{4,5},{5,4},{6,7},{7,6},{8,9},{9,8},{10,11... | collective-permute-start | bytes 1376264 | tf_op jit(solution)/shard_map/ppermute | solution.py:90
  44.3 3.6 %collective-permute-start.14 = (bf16[64,3584]{1,0:T(8,128)(2,1)S(1)}, bf16[64,3584]{1,0:T(8,128)(2,1)S(1)}, u32[]{:S(2)}, u32[]{:S(2)}) collective-permute-start(bf16[64,3584]{1,0:T(8,128)(2,1)S(1)} %collective-permute-done.13.refs_0_), channel_id=1, source_target_pairs={{0,1},{1,0},{2,3},{3,2},{4,5},{5,4},{6,7},{7,6},{8,9},{9,8},{10,11... | collective-permute-start | bytes 1376264 | tf_op jit(solution)/shard_map/ppermute | solution.py:90
  47.8 19.9 %copy-start.6 = (bf16[256,3584]{1,0:T(8,128)(2,1)}, bf16[256,3584]{1,0:T(8,128)(2,1)S(1)}, u32[]{:S(2)}) copy-start(bf16[256,3584]{1,0:T(8,128)(2,1)S(1)} %get-tuple-element.53.refs_0_.last_a) | copy-start | bytes 5505028
  49.1 18.6 %copy-start.7 = (bf16[128,3584]{1,0:T(8,128)(2,1)}, bf16[128,3584]{1,0:T(8,128)(2,1)S(1)}, u32[]{:S(2)}) copy-start(bf16[128,3584]{1,0:T(8,128)(2,1)S(1)} %get-tuple-element.54.refs_1_.last_b) | copy-start | bytes 2752516
  49.1 7.9 %collective-permute-start.17 = (f32[32,512]{1,0:T(8,128)S(1)}, f32[32,512]{1,0:T(8,128)S(1)}, u32[]{:S(2)}, u32[]{:S(2)}) collective-permute-start(f32[32,512]{1,0:T(8,128)S(1)} %get-tuple-element.51), channel_id=1, source_target_pairs={{0,192},{1,49},{2,194},{3,51},{4,196},{5,53},{6,198},{7,55},{8,200... | collective-permute-start | bytes 196616 | tf_op jit(solution)/shard_map/ppermute | solution.py:110
  51.9 6.2 %collective-permute-start.16 = (f32[32,512]{1,0:T(8,128)S(1)}, f32[32,512]{1,0:T(8,128)S(1)}, u32[]{:S(2)}, u32[]{:S(2)}) collective-permute-start(f32[32,512]{1,0:T(8,128)S(1)} %get-tuple-element.51), channel_id=1, source_target_pairs={{0,64},{1,17},{2,66},{3,19},{4,68},{5,21},{6,70},{7,23},{8,72},{9,... | collective-permute-start | bytes 196616 | tf_op jit(solution)/shard_map/ppermute | solution.py:110
  51.9 6.2 %collective-permute-start.15 = (f32[32,512]{1,0:T(8,128)S(1)}, f32[32,512]{1,0:T(8,128)S(1)}, u32[]{:S(2)}, u32[]{:S(2)}) collective-permute-start(f32[32,512]{1,0:T(8,128)S(1)} %get-tuple-element.51), channel_id=1, source_target_pairs={{0,128},{1,33},{2,130},{3,35},{4,132},{5,37},{6,134},{7,39},{8,136... | collective-permute-start | bytes 196616 | tf_op jit(solution)/shard_map/ppermute | solution.py:110
  58.2 8.6 %collective-permute-start.20 = (f32[32,512]{1,0:T(8,128)S(1)}, f32[32,512]{1,0:T(8,128)S(1)}, u32[]{:S(2)}, u32[]{:S(2)}) collective-permute-start(f32[32,512]{1,0:T(8,128)S(1)} %add_add_fusion.l0), channel_id=1, source_target_pairs={{0,48},{1,193},{2,50},{3,195},{4,52},{5,197},{6,54},{7,199},{8,56}... | collective-permute-start | bytes 196616 | tf_op jit(solution)/shard_map/ppermute | solution.py:110
  61.2 5.8 %collective-permute-start.19 = (f32[32,512]{1,0:T(8,128)S(1)}, f32[32,512]{1,0:T(8,128)S(1)}, u32[]{:S(2)}, u32[]{:S(2)}) collective-permute-start(f32[32,512]{1,0:T(8,128)S(1)} %add_add_fusion.l0), channel_id=1, source_target_pairs={{0,32},{1,129},{2,34},{3,131},{4,36},{5,133},{6,38},{7,135},{8,40}... | collective-permute-start | bytes 196616 | tf_op jit(solution)/shard_map/ppermute | solution.py:110
  61.9 5.9 %collective-permute-start.18 = (f32[32,512]{1,0:T(8,128)S(1)}, f32[32,512]{1,0:T(8,128)S(1)}, u32[]{:S(2)}, u32[]{:S(2)}) collective-permute-start(f32[32,512]{1,0:T(8,128)S(1)} %add_add_fusion.l0), channel_id=1, source_target_pairs={{0,16},{1,65},{2,18},{3,67},{4,20},{5,69},{6,22},{7,71},{8,24},{9,... | collective-permute-start | bytes 196616 | tf_op jit(solution)/shard_map/ppermute | solution.py:110
  72.7 13.2 %all-to-all-start = ((bf16[16,2,3584]{2,1,0:T(2,128)(2,1)}), bf16[16,2,3584]{2,1,0:T(2,128)(2,1)S(1)}, u32[]{:S(2)}, u32[]{:S(2)}) async-start(bf16[16,2,3584]{2,1,0:T(2,128)(2,1)} %get-tuple-element.58), calls=%async_computation | async-start | bytes 458752 | tf_op jit(solution)/shard_map/all_to_all | solution.py:503
  86.9 12.0 %all-to-all-start.1 = ((bf16[16,2,3584]{2,1,0:T(2,128)(2,1)}), bf16[16,2,3584]{2,1,0:T(2,128)(2,1)S(1)}, u32[]{:S(2)}, u32[]{:S(2)}) async-start(bf16[16,2,3584]{2,1,0:T(2,128)(2,1)} %sum_of_ranks.1), calls=%async_computation.1 | async-start | bytes 458752 | tf_op jit(solution)/shard_map/all_to_all | solution.py:506
  90.6 8.3 %copy-start.10 = (f32[32,512]{1,0:T(8,128)S(1)}, f32[32,512]{1,0:T(8,128)}, u32[]{:S(2)}) copy-start(f32[32,512]{1,0:T(8,128)} %get-tuple-element.32.factor) | copy-start | bytes 196612
